TPU v7x, 128 devices: a whole 4x4x4 slice. The times are simulated.
128 devices in a mesh: dp: 8 (over z, x_lo), expert: 16 (over y, x_hi, core).
Axes of the slice: x: 4 (x_hi: 2, x_lo: 2; x = x_hi * 2 + x_lo), y: 4, z: 4, core: 2. Of those that a mesh axis runs over, the one named last changes fastest.
Arguments:
- tokens: bfloat16 [768, 7168], P('expert', 'dp'), may hold values from -6 to 6
- upstream: bfloat16 [768, 7168], P('expert', 'dp'), may hold values from -6 to 6
- expert_ids: int32 [768, 4], P('expert'), may hold values from 0 to 31, all different within a row; in each aligned block of 48 rows (0 to 47, 48 to 95, ...) at most 8 rows name the same one
- gate_values: float32 [768, 4], P('expert'), may hold values from 0.2 to 1
- gate_weight: bfloat16 [32, 7168, 1024], P('expert', None, 'dp'), may hold values from -0.0625 to 0.0625
- up_weight: bfloat16 [32, 7168, 1024], P('expert', None, 'dp'), may hold values from -0.0625 to 0.0625
- down_weight: bfloat16 [32, 1024, 7168], P('expert', 'dp'), may hold values from -0.1875 to 0.1875
Outputs:
- mixed: bfloat16 [768, 7168], P('expert', 'dp')
- token_grads: bfloat16 [768, 7168], P('expert', 'dp')
- gate_weight_grad: bfloat16 [32, 7168, 1024], P('expert', None, 'dp')
- up_weight_grad: bfloat16 [32, 7168, 1024], P('expert', None, 'dp')
- down_weight_grad: bfloat16 [32, 1024, 7168], P('expert', 'dp')
Inputs may be any that keep to these rules, and one draw needn't show every extreme that they name: `expert_ids`: each row names 4 different experts; among the rows of one device's block of 48 tokens no expert is named more than 8 times, a bound that some block reaches.
All inputs are finite; a program needn't handle non-finite values.
Results may differ from a plain program's by a relative error of at most 0.02.
Values may be sent and summed in bfloat16 or wider, within the bound.
No kernel may reach another device: no remote copies, remote signals or barrier semaphores. Data moves between devices by JAX's collectives and lax.ppermute only.
A program may use at most 320 MiB of HBM per device.

v0:
```python
import jax
import jax.numpy as jnp
from jax import lax
from jax.sharding import PartitionSpec as P


def spread(value, axis, source):
    kept = jnp.where(lax.axis_index(axis) == source, value, 0).astype(value.dtype)
    return lax.psum(kept, axis)


def activate(gate_pre, up_pre):
    sigmoid_gate = jax.nn.sigmoid(gate_pre)
    activated = gate_pre * sigmoid_gate
    return (sigmoid_gate, activated, (activated * up_pre).astype(jnp.bfloat16))


def differentiate(hidden_cotangent, gate_pre, up_pre, sigmoid_gate, activated):
    gate_diff = (
        hidden_cotangent * up_pre * sigmoid_gate * (1.0 + gate_pre * (1.0 - sigmoid_gate))
    ).astype(jnp.bfloat16)
    up_diff = (hidden_cotangent * activated).astype(jnp.bfloat16)
    return (gate_diff, up_diff)


def rounded_copy(values):
    return lax.optimization_barrier(values.astype(jnp.bfloat16)).astype(jnp.float32)


def on_device(tokens, upstream, expert_ids, gate_values, gate_weight, up_weight, down_weight):
    column_count = lax.axis_size("expert")
    column = lax.axis_index("expert")
    tok_dev, top_count = expert_ids.shape
    exp_dev = gate_weight.shape[0]
    slot_count = exp_dev + 1
    total_slots = column_count * slot_count
    capacity = tok_dev * top_count * 4 // (3 * exp_dev * column_count)
    resident = expert_ids // exp_dev * slot_count + expert_ids % exp_dev
    target = jnp.where(expert_ids == 0, column * slot_count + exp_dev, resident)
    onehot = (
        target.reshape(-1)[:, None] == jnp.arange(total_slots, dtype=jnp.int32)[None, :]
    ).astype(jnp.int32)
    earlier = jnp.cumsum(onehot, axis=0) - onehot
    position = jnp.sum(onehot * earlier, axis=1).reshape(tok_dev, top_count)
    place = target * capacity + position
    slot_index = jnp.arange(total_slots * capacity, dtype=jnp.int32)
    hits = place[None, :, :] == slot_index[:, None, None]
    select_map = jnp.sum(hits.astype(jnp.float32), axis=2).astype(jnp.bfloat16)
    gated_map = jnp.sum(jnp.where(hits, gate_values[None, :, :], 0.0), axis=2)
    row_gates = jnp.sum(gated_map, axis=1)

    def dispatch(source, row_scale):
        full_rows = lax.all_gather(source, "dp", axis=1, tiled=True)
        picked = jnp.dot(select_map, full_rows, preferred_element_type=jnp.float32)
        outgoing = (picked * row_scale[:, None]).astype(jnp.bfloat16)
        outgoing = outgoing.reshape(column_count, slot_count, capacity, full_rows.shape[1])
        return lax.all_to_all(outgoing, "expert", split_axis=0, concat_axis=0, tiled=True)

    def collect(partial_value):
        summed = lax.psum_scatter(
            partial_value.astype(jnp.bfloat16), "dp", scatter_dimension=3, tiled=True
        )
        returned = lax.all_to_all(summed, "expert", split_axis=0, concat_axis=0, tiled=True)
        return returned.reshape(total_slots * capacity, returned.shape[3])

    hot_gate, hot_up, hot_down = (
        spread(gate_weight[0], "expert", 0),
        spread(up_weight[0], "expert", 0),
        spread(down_weight[0], "expert", 0),
    )
    unit_scale = jnp.ones((total_slots * capacity,), jnp.float32)
    expert_rows = dispatch(tokens, unit_scale)
    resident_rows = expert_rows[:, :exp_dev]
    replica_rows = expert_rows[:, exp_dev]
    gate_res = jnp.einsum(
        "nscd,sdf->nscf", resident_rows, gate_weight, preferred_element_type=jnp.float32
    )
    up_res = jnp.einsum(
        "nscd,sdf->nscf", resident_rows, up_weight, preferred_element_type=jnp.float32
    )
    gate_rep = jnp.einsum("ncd,df->ncf", replica_rows, hot_gate, preferred_element_type=jnp.float32)
    up_rep = jnp.einsum("ncd,df->ncf", replica_rows, hot_up, preferred_element_type=jnp.float32)
    sigmoid_res, activated_res, hidden_res = activate(gate_res, up_res)
    sigmoid_rep, activated_rep, hidden_rep = activate(gate_rep, up_rep)
    out_res = jnp.einsum(
        "nscf,sfd->nscd", hidden_res, down_weight, preferred_element_type=jnp.float32
    )
    out_rep = jnp.einsum("ncf,fd->ncd", hidden_rep, hot_down, preferred_element_type=jnp.float32)
    output_rows = collect(jnp.concatenate([out_res, out_rep[:, None]], axis=1))
    mixed = jnp.dot(
        gated_map.T, output_rows.astype(jnp.float32), precision=lax.Precision.HIGHEST
    ).astype(jnp.bfloat16)
    cotangent_rows = dispatch(upstream, row_gates)
    cotangent_res = cotangent_rows[:, :exp_dev]
    cotangent_rep = cotangent_rows[:, exp_dev]
    hidden_cot_res = jnp.einsum(
        "nscd,sfd->nscf", cotangent_res, down_weight, preferred_element_type=jnp.float32
    )
    hidden_cot_rep = jnp.einsum(
        "ncd,fd->ncf", cotangent_rep, hot_down, preferred_element_type=jnp.float32
    )
    gate_diff_res, up_diff_res = differentiate(
        hidden_cot_res, gate_res, up_res, sigmoid_res, activated_res
    )
    gate_diff_rep, up_diff_rep = differentiate(
        hidden_cot_rep, gate_rep, up_rep, sigmoid_rep, activated_rep
    )
    input_res = jnp.einsum(
        "nscf,sdf->nscd", gate_diff_res, gate_weight, preferred_element_type=jnp.float32
    )
    input_res = input_res + jnp.einsum(
        "nscf,sdf->nscd", up_diff_res, up_weight, preferred_element_type=jnp.float32
    )
    input_rep = jnp.einsum(
        "ncf,df->ncd", gate_diff_rep, hot_gate, preferred_element_type=jnp.float32
    )
    input_rep = input_rep + jnp.einsum(
        "ncf,df->ncd", up_diff_rep, hot_up, preferred_element_type=jnp.float32
    )
    input_rows = collect(jnp.concatenate([input_res, input_rep[:, None]], axis=1))
    token_grads = jnp.dot(select_map.T, input_rows, preferred_element_type=jnp.float32).astype(
        jnp.bfloat16
    )
    grad_gate = jnp.einsum(
        "nscd,nscf->sdf", resident_rows, gate_diff_res, preferred_element_type=jnp.float32
    )
    grad_up = jnp.einsum(
        "nscd,nscf->sdf", resident_rows, up_diff_res, preferred_element_type=jnp.float32
    )
    grad_down = jnp.einsum(
        "nscf,nscd->sfd", hidden_res, cotangent_res, preferred_element_type=jnp.float32
    )
    replica_gate = rounded_copy(
        jnp.einsum("ncd,ncf->df", replica_rows, gate_diff_rep, preferred_element_type=jnp.float32)
    )
    replica_up = rounded_copy(
        jnp.einsum("ncd,ncf->df", replica_rows, up_diff_rep, preferred_element_type=jnp.float32)
    )
    replica_down = rounded_copy(
        jnp.einsum("ncf,ncd->fd", hidden_rep, cotangent_rep, preferred_element_type=jnp.float32)
    )
    sum_gate, sum_up, sum_down = (
        lax.psum(replica_gate.astype(jnp.bfloat16), "expert").astype(jnp.float32),
        lax.psum(replica_up.astype(jnp.bfloat16), "expert").astype(jnp.float32),
        lax.psum(replica_down.astype(jnp.bfloat16), "expert").astype(jnp.float32),
    )
    owner_flags = (column * exp_dev + jnp.arange(exp_dev, dtype=jnp.int32) == 0).astype(
        jnp.float32
    )[:, None, None]
    gate_weight_grad = (grad_gate + owner_flags * sum_gate[None]).astype(jnp.bfloat16)
    up_weight_grad = (grad_up + owner_flags * sum_up[None]).astype(jnp.bfloat16)
    down_weight_grad = (grad_down + owner_flags * sum_down[None]).astype(jnp.bfloat16)
    return (mixed, token_grads, gate_weight_grad, up_weight_grad, down_weight_grad)


def solution(mesh):
    return jax.shard_map(
        on_device,
        mesh=mesh,
        in_specs=(
            P("expert", "dp"),
            P("expert", "dp"),
            P("expert", None),
            P("expert", None),
            P("expert", None, "dp"),
            P("expert", None, "dp"),
            P("expert", "dp", None),
        ),
        out_specs=(
            P("expert", "dp"),
            P("expert", "dp"),
            P("expert", None, "dp"),
            P("expert", None, "dp"),
            P("expert", "dp", None),
        ),
        check_vma=False,
    )
```

profile of v0, /device:TPU:1, one launch (start us, length us, event | category | flops | bytes accessed | tf_op | source)
XLA Modules:
  0.0 875.1 jit_solution(11328381989421398499)
XLA Ops:
  10.1 28.1 %all_gather.6 = bf16[48,7168]{1,0:T(8,128)(2,1)S(1)} all-gather(bf16[48,896]{1,0:T(8,128)(2,1)} %param.7), channel_id=1, replica_groups=mesh['dp'=8,'expert'=16] {'dp'}, dimensions={1}, use_global_device_ids=true | all-gather | bytes 774144 | tf_op jit(solution)/shard_map/all_gather | solution.py:53
  39.6 4.0 convolution_convert_fusion
  43.6 12.5 %all-to-all-start = ((bf16[16,3,8,7168]{3,2,1,0:T(8,128)(2,1)}), bf16[16,3,8,7168]{3,2,1,0:T(8,128)(2,1)}, u32[]{:S(2)}, u32[]{:S(2)}) async-start(bf16[16,3,8,7168]{3,2,1,0:T(8,128)(2,1)} %bitcast.163), calls=%async_computation | async-start | bytes 11010048 | tf_op jit(solution)/shard_map/all_to_all | solution.py:57
  63.7 123.8 %all_gather.7 = bf16[48,7168]{1,0:T(8,128)(2,1)S(1)} all-gather(bf16[48,896]{1,0:T(8,128)(2,1)S(1)} %copy-done.13), channel_id=1, replica_groups=mesh['dp'=8,'expert'=16] {'dp'}, dimensions={1}, use_global_device_ids=true | all-gather | bytes 774144 | tf_op jit(solution)/shard_map/all_gather | solution.py:53
  187.5 4.1 multiply_convert_fusion
  191.5 13.5 %all-to-all-start.2 = ((bf16[16,3,8,7168]{3,2,1,0:T(8,128)(2,1)}), bf16[16,3,8,7168]{3,2,1,0:T(8,128)(2,1)}, u32[]{:S(2)}, u32[]{:S(2)}) async-start(bf16[16,3,8,7168]{3,2,1,0:T(8,128)(2,1)} %bitcast.164), calls=%async_computation.2 | async-start | bytes 11010048 | tf_op jit(solution)/shard_map/all_to_all | solution.py:57
  205.1 95.0 %all-reduce.8.cloned.1.call-done = (bf16[7168,128]{1,0:T(8,128)(2,1)}, bf16[7168,128]{1,0:T(8,128)(2,1)}, bf16[128,7168]{1,0:T(8,128)(2,1)}) async-done(((bf16[7168,128]{1,0:T(8,128)(2,1)}, bf16[7168,128]{1,0:T(8,128)(2,1)}, bf16[128,7168]{1,0:T(8,128)(2,1)}), (bf16[7168,128]{1,0:T(8,128)(2,1)}, bf16[7168,128]{1,0:T(8,128)(2,1)}, bf16[128,7168]{1,0:T(8,128)(2,1)})) %all-reduce.8.cloned.1.call-update) | async-done | bytes 5505040 | tf_op jit(solution)/shard_map/psum | solution.py:9
  305.1 10.9 %all-to-all-done.2 = bf16[16,3,8,7168]{3,2,1,0:T(8,128)(2,1)} async-done(((bf16[16,3,8,7168]{3,2,1,0:T(8,128)(2,1)}), bf16[16,3,8,7168]{3,2,1,0:T(8,128)(2,1)}, u32[]{:S(2)}, u32[]{:S(2)}) %all-to-all-start.2) | async-done | bytes 5505056 | tf_op jit(solution)/shard_map/all_to_all | solution.py:57
  329.0 4.4 fusion.46
  348.1 70.2 %copy.91 = bf16[16,3,8,7168]{2,0,1,3:T(8,128)(2,1)} copy(bf16[16,3,8,7168]{3,2,0,1:T(8,128)(2,1)} %pad_maximum_fusion.1) | data formatting | bytes 11010048
  418.2 102.3 %reshape.80 = bf16[7168,384]{1,0:T(8,128)(2,1)} reshape(bf16[7168,3,16,8]{3,2,1,0:T(8,128)(2,1)} %bitcast.42) | data formatting | bytes 11010048
  527.5 70.1 %copy.89 = bf16[16,3,8,7168]{2,0,1,3:T(8,128)(2,1)} copy(bf16[16,3,8,7168]{3,2,0,1:T(8,128)(2,1)} %pad_maximum_fusion) | data formatting | bytes 11010048
  597.6 102.2 %reshape.78 = bf16[7168,384]{1,0:T(8,128)(2,1)} reshape(bf16[7168,3,16,8]{3,2,1,0:T(8,128)(2,1)} %bitcast.39) | data formatting | bytes 11010048
  704.0 6.4 fusion.5
  710.3 15.2 %reshape.81 = bf16[896,3,16,8]{3,2,1,0:T(8,128)(2,1)} reshape(bf16[896,384]{1,0:T(8,128)(2,1)} %reduce-scatter.9.cloned.1.call-done) | data formatting | bytes 1376256
  725.5 12.6 %copy.82 = bf16[16,3,8,896]{3,2,1,0:T(8,128)(2,1)} copy(bf16[16,3,8,896]{2,0,1,3:T(8,128)(2,1)} %bitcast.161) | data formatting | bytes 1376256 | tf_op jit(solution)/shard_map/reduce_scatter | solution.py:60
  738.1 3.8 all-to-all-start.3
  741.9 7.1 fusion.6
  751.3 68.2 %reduce-scatter.7.cloned.1.call-done = bf16[896,384]{1,0:T(8,128)(2,1)} async-done(((bf16[7168,384]{1,0:T(8,128)(2,1)}), bf16[896,384]{1,0:T(8,128)(2,1)}) %reduce-scatter.7.cloned.1.call-update) | async-done | bytes 688144
  819.5 15.2 %reshape.79 = bf16[896,3,16,8]{3,2,1,0:T(8,128)(2,1)} reshape(bf16[896,384]{1,0:T(8,128)(2,1)} %reduce-scatter.7.cloned.1.call-done) | data formatting | bytes 1376256
  834.7 12.5 %copy.79 = bf16[16,3,8,896]{3,2,1,0:T(8,128)(2,1)} copy(bf16[16,3,8,896]{2,0,1,3:T(8,128)(2,1)} %bitcast.162) | data formatting | bytes 1376256 | tf_op jit(solution)/shard_map/reduce_scatter | solution.py:60
  847.2 7.3 all-to-all-start.1
  854.4 6.2 fusion.3
  861.5 6.0 all-to-all-done.1
  (85 shorter events, 59.6 us)
Async XLA Ops:
  39.6 147.9 %copy-start.10 = (bf16[384,48]{0,1:T(8,128)(2,1)}, bf16[384,48]{0,1:T(8,128)(2,1)S(1)}, u32[]{:S(2)}) copy-start(bf16[384,48]{0,1:T(8,128)(2,1)S(1)} %get-tuple-element.7) | copy-start | bytes 110596
  43.6 147.9 %all-to-all-start = ((bf16[16,3,8,7168]{3,2,1,0:T(8,128)(2,1)}), bf16[16,3,8,7168]{3,2,1,0:T(8,128)(2,1)}, u32[]{:S(2)}, u32[]{:S(2)}) async-start(bf16[16,3,8,7168]{3,2,1,0:T(8,128)(2,1)} %bitcast.163), calls=%async_computation | async-start | bytes 11010048 | tf_op jit(solution)/shard_map/all_to_all | solution.py:57
  56.1 244.0 %all-reduce.8.cloned.1.call-start = ((), (), s32[]{:S(2)}) async-start(), calls=%async_computation.9 | async-start | bytes 11010048 | tf_op jit(solution)/shard_map/psum | solution.py:9
  56.2 3.0 copy-start
  62.8 0.9 copy-start.13
  191.5 124.5 %all-to-all-start.2 = ((bf16[16,3,8,7168]{3,2,1,0:T(8,128)(2,1)}), bf16[16,3,8,7168]{3,2,1,0:T(8,128)(2,1)}, u32[]{:S(2)}, u32[]{:S(2)}) async-start(bf16[16,3,8,7168]{3,2,1,0:T(8,128)(2,1)} %bitcast.164), calls=%async_computation.2 | async-start | bytes 11010048 | tf_op jit(solution)/shard_map/all_to_all | solution.py:57
  205.0 494.8 %all-reduce.6.cloned.1.call-start = ((), (), s32[]{:S(2)}) async-start(), calls=%async_computation.8 | async-start | bytes 11010048 | tf_op jit(solution)/shard_map/psum | solution.py:143
  300.1 2.8 copy-start.6
  300.1 15.9 %copy-start.5 = (bf16[128,7168]{1,0:T(8,128)(2,1)S(1)}, bf16[128,7168]{1,0:T(8,128)(2,1)}, u32[]{:S(2)}) copy-start(bf16[128,7168]{1,0:T(8,128)(2,1)} %get-tuple-element.13) | copy-start | bytes 5505028
  328.8 381.6 %reduce-scatter.9.cloned.1.call-start = ((), (), s32[]{:S(2)}) async-start(), calls=%async_computation.7 | async-start | bytes 6193152
  329.0 4.4 copy-start.1
  333.4 3.6 copy-start.2
  337.0 3.3 copy-start.3
  340.4 1.1 copy-start.14
  341.5 1.5 copy-start.7
  343.0 1.5 copy-start.4
  520.6 298.9 %reduce-scatter.7.cloned.1.call-start = ((), (), s32[]{:S(2)}) async-start(), calls=%async_computation.6 | async-start | bytes 6193152
  699.9 2.1 copy-start.9
  725.5 16.3 %copy-start.15 = (bf16[16,2,8,128]{3,2,0,1:T(8,128)(2,1)S(1)}, bf16[16,2,8,128]{3,2,0,1:T(8,128)(2,1)}, u32[]{:S(2)}) copy-start(bf16[16,2,8,128]{3,2,0,1:T(8,128)(2,1)} %copy-done.14) | copy-start | bytes 196612
  738.1 109.1 %all-to-all-start.3 = ((bf16[16,3,8,896]{3,2,1,0:T(8,128)(2,1)}), bf16[16,3,8,896]{3,2,1,0:T(8,128)(2,1)S(1)}, u32[]{:S(2)}, u32[]{:S(2)}) async-start(bf16[16,3,8,896]{3,2,1,0:T(8,128)(2,1)} %copy.82), calls=%async_computation.3 | async-start | bytes 1376256 | tf_op jit(solution)/shard_map/all_to_all | solution.py:63
  741.9 7.1 copy-start.8
  847.2 20.3 %all-to-all-start.1 = ((bf16[16,3,8,896]{3,2,1,0:T(8,128)(2,1)}), bf16[16,3,8,896]{3,2,1,0:T(8,128)(2,1)S(1)}, u32[]{:S(2)}, u32[]{:S(2)}) async-start(bf16[16,3,8,896]{3,2,1,0:T(8,128)(2,1)} %copy.79), calls=%async_computation.1 | async-start | bytes 1376256 | tf_op jit(solution)/shard_map/all_to_all | solution.py:63
  854.4 6.2 copy-start.11
  854.4 13.1 %copy-start.12 = (f32[384,48]{0,1:T(8,128)S(1)}, f32[384,48]{0,1:T(8,128)}, u32[]{:S(2)}) copy-start(f32[384,48]{0,1:T(8,128)} %get-tuple-element.6) | copy-start | bytes 221188
Sparse Core Ops, SparseCore 0:
  62.9 237.1 all-reduce.7
  328.9 158.6 all-reduce.5
  520.7 112.0 reduce-scatter.8
  699.9 119.5 reduce-scatter.6
where the time goes:
time: 888 us; the launch traced here: 875 us
  local copies, waits for them, and re-layouts  404 us (45%)
  waiting for transfers between devices  180 us (20%)
  blocking collectives  152 us (17%)
  matrix products  66 us (7%)
  starting transfers between devices  37.6 us (4%)
  other arithmetic  21.4 us (2%)
  between operations  14.1 us (2%)
    unnamed x39, local copies, waits for them, and re-layouts  378 us
    all_gather x2, blocking collectives, dispatch(): full_rows = lax.all_gather(source, 'dp', axis=1, tiled=True)  152 us
    psum x1, waiting for transfers between devices, spread(): return lax.psum(kept, axis)  95 us
    unnamed x6, waiting for transfers between devices  68.2 us
    all_to_all x2, starting transfers between devices, dispatch(): lax.all_to_all(outgoing, 'expert', split_axis=0, concat_axis=0, tiled=True)  26 us
    reduce_scatter x2, local copies, waits for them, and re-layouts, collect(): lax.psum_scatter(partial_value.astype(jnp.bfloat16), 'dp', scatter_dimens...  25 us
  transfers between devices with their start and end apart: 8, of which 4 were waited for; matrix products, arithmetic and copies ran while one was open for 53% of the time, Pallas kernels for 0%

commit v1 on v0

v1 whole, which is shorter than its diff:
```python
import jax
import jax.numpy as jnp
from jax import lax
from jax.experimental import pallas as pl
from jax.experimental.pallas import tpu as pltpu
from jax.sharding import PartitionSpec as P

BF = jnp.bfloat16
F32 = jnp.float32
LOW, HIGH = 80, 176
PARAMS = pltpu.CompilerParams(vmem_limit_bytes=48 * 1024 * 1024)


def dot(a, b, dims=((1,), (0,)), precision=None):
    return lax.dot_general(a, b, (dims, ((), ())), precision=precision, preferred_element_type=F32)


def dispatch_kernel(ids_ref, gates_ref, tokens_ref, upstream_ref, rows_ref, pick_ref, gated_ref):
    count, top = ids_ref.shape
    total = rows_ref.shape[0]
    width = tokens_ref.shape[1]
    capacity = 8
    row = lax.broadcasted_iota(jnp.int32, (count, total), 1)
    expert = row // capacity
    named = jnp.zeros((count, total), F32)
    gate = jnp.zeros((count, total), F32)
    for k in range(top):
        hit = ids_ref[:, k : k + 1] == expert
        named = jnp.where(hit, 1.0, named)
        gate = jnp.where(hit, gates_ref[:, k : k + 1], gate)
    later = lax.broadcasted_iota(jnp.int32, (count, count), 0)
    sooner = lax.broadcasted_iota(jnp.int32, (count, count), 1)
    earlier = jnp.where(sooner < later, 1.0, 0.0)
    position = dot(earlier.astype(BF), named.astype(BF))
    chosen = (named > 0.5) & (position == (row % capacity).astype(F32))
    pick = jnp.where(chosen, 1.0, 0.0)
    gated = jnp.where(chosen, gate, 0.0)
    pick_ref[...] = pick.astype(BF)
    gated_ref[...] = gated
    rows_ref[:, :width] = dot(pick.astype(BF), tokens_ref[...], ((0,), (0,))).astype(BF)
    rows_ref[:, width:] = dot(
        gated, upstream_ref[...].astype(F32), ((0,), (0,)), lax.Precision.HIGHEST
    ).astype(BF)


def dispatch(ids, gates, tokens, upstream, total):
    count, width = tokens.shape
    return pl.pallas_call(
        dispatch_kernel,
        out_shape=(
            jax.ShapeDtypeStruct((total, 2 * width), BF),
            jax.ShapeDtypeStruct((count, total), BF),
            jax.ShapeDtypeStruct((count, total), F32),
        ),
        compiler_params=PARAMS,
        name="dispatch",
    )(ids, gates, tokens, upstream)


class Links:
    def __init__(self, size):
        rings = size // 2
        self.up = [(z * 2 + x, (z + 1) % rings * 2 + x) for z in range(rings) for x in range(2)]
        self.down = [(z * 2 + x, (z - 1) % rings * 2 + x) for z in range(rings) for x in range(2)]
        self.side = [(i, i ^ 1) for i in range(size)]

    def send_up(self, value):
        return lax.ppermute(value, "dp", self.up)

    def send_down(self, value):
        return lax.ppermute(value, "dp", self.down)

    def cross(self, value):
        return lax.ppermute(value, "dp", self.side)


def gather(links, own):
    above = links.send_down(own)
    below = links.send_up(own)
    beside = links.cross(own)
    above2 = links.send_down(jnp.concatenate([above[:HIGH], beside[:LOW]]))
    below2 = links.send_up(jnp.concatenate([below[HIGH:], beside[LOW:]]))
    beside2 = links.cross(jnp.concatenate([above[LOW:], below[:LOW]]))
    above3 = links.send_down(above2[HIGH:])
    beside3 = links.cross(above2[LOW:HIGH])
    below3 = links.send_up(below2[HIGH:])
    return (own, above, below, beside, above2, below2, beside2, above3, beside3, below3)


PIECES = 10


def assemble(pieces, full_ref):
    own, above, below, beside, above2, below2, beside2, above3, beside3, below3 = pieces
    full_ref[0] = own[...]
    full_ref[1] = above[...]
    full_ref[2] = below[...]
    full_ref[3] = beside[...]
    full_ref[4, :HIGH] = above2[:HIGH]
    full_ref[4, HIGH:] = below2[:LOW]
    full_ref[5, :LOW] = above2[HIGH:]
    full_ref[5, LOW:] = beside2[:HIGH]
    full_ref[6, :LOW] = beside2[HIGH:]
    full_ref[6, LOW:] = below2[LOW:]
    full_ref[7, :LOW] = above3[...]
    full_ref[7, LOW:HIGH] = beside3[...]
    full_ref[7, HIGH:] = below3[...]


def block_order():
    me = lax.axis_index("dp")
    rings = lax.axis_size("dp") // 2
    z, x = me // 2, me % 2
    steps = ((0, 0), (1, 0), (-1, 0), (0, 1), (2, 0), (1, 1), (-1, 1), (2, 1))
    return jnp.stack([(z + dz + rings) % rings * 2 + (x + dx) % 2 for dz, dx in steps]).astype(
        jnp.int32
    )


def store_partials(step, value, outs):
    cut_up, cut_side, cut_down = outs[:3]

    @pl.when(step == 7)
    def _():
        cut_up[...] = value[:LOW]
        cut_side[...] = value[LOW:HIGH]
        cut_down[...] = value[HIGH:]

    for block in range(7):

        @pl.when(step == block)
        def _(block=block):
            outs[3 + block][...] = value


def partial_shapes(rows, width):
    sizes = (LOW, HIGH - LOW, rows - HIGH) + (rows,) * 7
    return tuple(jax.ShapeDtypeStruct((size, width), BF) for size in sizes)


def row_slot(shape):
    return lax.broadcasted_iota(jnp.int32, shape, 0) // 8 % 2 == 0


def pair(first, value):
    zero = jnp.zeros_like(value)
    return jnp.concatenate([jnp.where(first, value, zero), jnp.where(first, zero, value)], axis=1)


def whole(array):
    return pl.BlockSpec(array.shape, lambda j, order, n=len(array.shape): (0,) * n)


def forward_kernel(order_ref, *refs):
    pieces, refs = refs[:PIECES], refs[PIECES:]
    gate_ref, up_ref, down_ref = refs[:3]
    full_ref, pre_ref, hidden_ref = refs[3:6]
    partials = refs[6:16]
    step = pl.program_id(0)
    half = pre_ref.shape[1] // 2

    @pl.when(step == 0)
    def _():
        assemble(pieces, full_ref)

    @pl.when(step < 8)
    def _():
        rows = full_ref[step]
        gate = dot(rows, jnp.concatenate([gate_ref[0], gate_ref[1]], axis=1))
        up = dot(rows, jnp.concatenate([up_ref[0], up_ref[1]], axis=1))
        first = row_slot((rows.shape[0], half))
        gate = jnp.where(first, gate[:, :half], gate[:, half:])
        up = jnp.where(first, up[:, :half], up[:, half:])

        @pl.when(step == 0)
        def _():
            pre_ref[:, :half] = gate
            pre_ref[:, half:] = up

        @pl.when(step > 0)
        def _():
            pre_ref[:, :half] += gate
            pre_ref[:, half:] += up

    @pl.when(step == 7)
    def _():
        gate = pre_ref[:, :half]
        hidden = (gate * jax.nn.sigmoid(gate) * pre_ref[:, half:]).astype(BF)
        hidden_ref[...] = pair(row_slot(hidden.shape), hidden)

    @pl.when(step >= 8)
    def _():
        store_partials(step - 8, dot(hidden_ref[...], down_ref[...]).astype(BF), partials)


def forward(order, pieces, gate_weight, up_weight, down_flat):
    rows, width = pieces[0].shape
    hid = gate_weight.shape[2]
    first = lambda j, order: (0, order[jnp.minimum(j, 7)], 0)
    second = lambda j, order: (0, order[jnp.maximum(j - 8, 0)])
    shapes = (
        jax.ShapeDtypeStruct((8, rows, width), BF),
        jax.ShapeDtypeStruct((rows, 2 * hid), F32),
        jax.ShapeDtypeStruct((rows, 2 * hid), BF),
    ) + partial_shapes(rows, width)
    out = pl.pallas_call(
        forward_kernel,
        grid_spec=pltpu.PrefetchScalarGridSpec(
            num_scalar_prefetch=1,
            grid=(16,),
            in_specs=[whole(p) for p in pieces]
            + [
                pl.BlockSpec((2, width, hid), first),
                pl.BlockSpec((2, width, hid), first),
                pl.BlockSpec((2 * hid, width), second),
            ],
            out_specs=[whole(s) for s in shapes],
        ),
        out_shape=shapes,
        compiler_params=PARAMS,
        name="forward",
    )(order, *pieces, gate_weight, up_weight, down_flat)
    return out[0], out[1], out[2], out[3:]


def backward_kernel(order_ref, *refs):
    pieces, refs = refs[:PIECES], refs[PIECES:]
    pre_ref, gate_ref, up_ref, down_ref = refs[:4]
    full_ref, gate_diff_ref, up_diff_ref = refs[4:7]
    partials = refs[7:17]
    acc_ref = refs[17]
    step = pl.program_id(0)
    half = pre_ref.shape[1] // 2

    @pl.when(step == 0)
    def _():
        assemble(pieces, full_ref)

    @pl.when(step < 8)
    def _():
        part = dot(full_ref[step], down_ref[...], ((1,), (1,)))

        @pl.when(step == 0)
        def _():
            acc_ref[...] = part

        @pl.when(step > 0)
        def _():
            acc_ref[...] += part

    @pl.when(step == 7)
    def _():
        first = row_slot((acc_ref.shape[0], half))
        cotangent = jnp.where(first, acc_ref[:, :half], acc_ref[:, half:])
        gate, up = pre_ref[:, :half], pre_ref[:, half:]
        sigmoid = jax.nn.sigmoid(gate)
        gate_diff = (cotangent * up * sigmoid * (1.0 + gate * (1.0 - sigmoid))).astype(BF)
        up_diff = (cotangent * (gate * sigmoid)).astype(BF)
        gate_diff_ref[...] = pair(first, gate_diff)
        up_diff_ref[...] = pair(first, up_diff)

    @pl.when(step >= 8)
    def _():
        nt = ((1,), (1,))
        value = dot(gate_diff_ref[...], jnp.concatenate([gate_ref[0], gate_ref[1]], axis=1), nt)
        value += dot(up_diff_ref[...], jnp.concatenate([up_ref[0], up_ref[1]], axis=1), nt)
        store_partials(step - 8, value.astype(BF), partials)


def backward(order, pieces, pre, gate_weight, up_weight, down_flat):
    rows, width = pieces[0].shape
    hid = gate_weight.shape[2]
    first = lambda j, order: (0, order[jnp.minimum(j, 7)])
    second = lambda j, order: (0, order[jnp.maximum(j - 8, 0)], 0)
    shapes = (
        jax.ShapeDtypeStruct((8, rows, width), BF),
        jax.ShapeDtypeStruct((rows, 2 * hid), BF),
        jax.ShapeDtypeStruct((rows, 2 * hid), BF),
    ) + partial_shapes(rows, width)
    out = pl.pallas_call(
        backward_kernel,
        grid_spec=pltpu.PrefetchScalarGridSpec(
            num_scalar_prefetch=1,
            grid=(16,),
            in_specs=[whole(p) for p in pieces]
            + [
                whole(pre),
                pl.BlockSpec((2, width, hid), second),
                pl.BlockSpec((2, width, hid), second),
                pl.BlockSpec((2 * hid, width), first),
            ],
            out_specs=[whole(s) for s in shapes],
            scratch_shapes=[pltpu.VMEM((rows, 2 * hid), F32)],
        ),
        out_shape=shapes,
        compiler_params=PARAMS,
        name="backward",
    )(order, *pieces, pre, gate_weight, up_weight, down_flat)
    return out[0], out[1], out[2], out[3:]


def weights_kernel(
    order_ref, x_ref, c_ref, hidden_ref, gate_diff_ref, up_diff_ref, gate_out, up_out, down_out
):
    tn = ((0,), (0,))
    hid = gate_out.shape[2]
    for diff_ref, out_ref in ((gate_diff_ref, gate_out), (up_diff_ref, up_out)):
        grad = dot(x_ref[0], diff_ref[...], tn).astype(BF)
        out_ref[0] = grad[:, :hid]
        out_ref[1] = grad[:, hid:]
    down_out[...] = dot(hidden_ref[...], c_ref[0], tn).astype(BF)


def weight_grads(order, x_full, c_full, hidden, gate_diff, up_diff):
    blocks, rows, width = x_full.shape
    hid = hidden.shape[1] // 2
    block = pl.BlockSpec((1, rows, width), lambda j, order: (j, 0, 0))
    grad = pl.BlockSpec((2, width, hid), lambda j, order: (0, order[j], 0))
    return pl.pallas_call(
        weights_kernel,
        grid_spec=pltpu.PrefetchScalarGridSpec(
            num_scalar_prefetch=1,
            grid=(blocks,),
            in_specs=[block, block, whole(hidden), whole(gate_diff), whole(up_diff)],
            out_specs=[
                grad,
                grad,
                pl.BlockSpec((2 * hid, width), lambda j, order: (0, order[j])),
            ],
        ),
        out_shape=(
            jax.ShapeDtypeStruct((2, blocks * width, hid), BF),
            jax.ShapeDtypeStruct((2, blocks * width, hid), BF),
            jax.ShapeDtypeStruct((2 * hid, blocks * width), BF),
        ),
        compiler_params=PARAMS,
        name="weight_grads",
    )(order, x_full, c_full, hidden, gate_diff, up_diff)


def add(a, b):
    return (a.astype(F32) + b.astype(F32)).astype(BF)


def second_hop_kernel(far, above1, below1, got_up, got_side, got_down, to_up, to_down, to_side):
    to_up[:LOW] = far[:LOW]
    to_up[LOW:HIGH] = add(far[LOW:HIGH], got_side[...])
    to_up[HIGH:] = add(above1[:LOW], got_up[...])
    to_down[:LOW] = far[HIGH:]
    to_down[LOW:HIGH] = below1[LOW:HIGH]
    to_down[HIGH:] = add(below1[HIGH:], got_down[...])
    to_side[:HIGH] = above1[LOW:]
    to_side[HIGH:] = below1[:LOW]


def third_hop_kernel(above, below, beside, got_up, got_down, got_side, to_up, to_down, to_side):
    to_up[:LOW] = add(above[:LOW], got_up[:LOW])
    to_up[LOW:HIGH] = (
        above[LOW:HIGH].astype(F32)
        + got_up[LOW:HIGH].astype(F32)
        + got_side[: HIGH - LOW].astype(F32)
    ).astype(BF)
    to_up[HIGH:] = add(above[HIGH:], got_side[HIGH - LOW : HIGH])
    to_down[:LOW] = add(below[:LOW], got_side[HIGH:])
    to_down[LOW:HIGH] = below[LOW:HIGH]
    to_down[HIGH:] = add(below[HIGH:], got_down[:LOW])
    to_side[:LOW] = add(beside[:LOW], got_up[HIGH:])
    to_side[LOW:] = add(beside[LOW:], got_down[LOW:])


def last_kernel(own, from_below, from_above, from_side, total):
    total[...] = (
        (own[...].astype(F32) + from_side[...].astype(F32))
        + (from_below[...].astype(F32) + from_above[...].astype(F32))
    ).astype(BF)


def local_call(kernel, name, count, *args):
    shape = jax.ShapeDtypeStruct(args[0].shape, BF)
    return pl.pallas_call(
        kernel,
        out_shape=(shape,) * count if count > 1 else shape,
        compiler_params=PARAMS,
        name=name,
    )(*args)


def reduce_scatter(links, partials):
    cut_up, cut_side, cut_down, own, above, below, beside, far, above1, below1 = partials
    got_up = links.send_up(cut_up)
    got_side = links.cross(cut_side)
    got_down = links.send_down(cut_down)
    to_up, to_down, to_side = local_call(
        second_hop_kernel, "second_hop", 3, far, above1, below1, got_up, got_side, got_down
    )
    got_up = links.send_up(to_up)
    got_down = links.send_down(to_down)
    got_side = links.cross(to_side)
    to_up, to_down, to_side = local_call(
        third_hop_kernel, "third_hop", 3, above, below, beside, got_up, got_down, got_side
    )
    got_up = links.send_up(to_up)
    got_down = links.send_down(to_down)
    got_side = links.cross(to_side)
    return local_call(last_kernel, "last_hop", 1, own, got_up, got_down, got_side)


def combine_kernel(pick_ref, gated_ref, out_ref, in_ref, mixed_ref, grads_ref):
    mixed_ref[...] = dot(
        gated_ref[...], out_ref[...].astype(F32), precision=lax.Precision.HIGHEST
    ).astype(BF)
    grads_ref[...] = dot(pick_ref[...], in_ref[...]).astype(BF)


def on_device(tokens, upstream, expert_ids, gate_values, gate_weight, up_weight, down_weight):
    columns = lax.axis_size("expert")
    exp_dev, hid, features = down_weight.shape
    rows = columns * exp_dev * 8
    width = tokens.shape[1]
    links = Links(lax.axis_size("dp"))
    order = block_order()
    down_flat = down_weight.reshape(exp_dev * hid, features)

    outgoing, pick, gated = dispatch(expert_ids, gate_values, tokens, upstream, rows)
    arrived = lax.all_to_all(
        outgoing.reshape(columns, exp_dev * 8, 2 * width), "expert", 0, 0, tiled=True
    ).reshape(rows, 2 * width)
    x_pieces = gather(links, arrived[:, :width])
    c_pieces = gather(links, arrived[:, width:])
    x_full, pre, hidden, out_partials = forward(order, x_pieces, gate_weight, up_weight, down_flat)
    out_rows = reduce_scatter(links, out_partials)
    c_full, gate_diff, up_diff, in_partials = backward(
        order, c_pieces, pre, gate_weight, up_weight, down_flat
    )
    in_rows = reduce_scatter(links, in_partials)
    gate_grad, up_grad, down_grad = weight_grads(
        order, x_full, c_full, hidden, gate_diff, up_diff
    )

    def give_back(value):
        return lax.all_to_all(
            value.reshape(columns, exp_dev * 8, width), "expert", 0, 0, tiled=True
        ).reshape(rows, width)

    shape = jax.ShapeDtypeStruct(tokens.shape, BF)
    mixed, token_grads = pl.pallas_call(
        combine_kernel, out_shape=(shape, shape), compiler_params=PARAMS, name="combine"
    )(pick, gated, give_back(out_rows), give_back(in_rows))
    return (mixed, token_grads, gate_grad, up_grad, down_grad.reshape(down_weight.shape))


def solution(mesh):
    return jax.shard_map(
        on_device,
        mesh=mesh,
        in_specs=(
            P("expert", "dp"),
            P("expert", "dp"),
            P("expert", None),
            P("expert", None),
            P("expert", None, "dp"),
            P("expert", None, "dp"),
            P("expert", "dp", None),
        ),
        out_specs=(
            P("expert", "dp"),
            P("expert", "dp"),
            P("expert", None, "dp"),
            P("expert", None, "dp"),
            P("expert", "dp", None),
        ),
        check_vma=False,
    )
```

time: 888 us -> 208 us (0.23); the launches traced: 875 us -> 207 us
  local copies, waits for them, and re-layouts: 404 us -> 10.7 us
  blocking collectives: 152 us -> 23.8 us
  waiting for transfers between devices: 180 us -> 54 us
  matrix products: 66 us -> 0 us
  Pallas kernels: 0 us -> 50.5 us
  starting transfers between devices: 37.6 us -> 65.6 us
  other arithmetic: 21.4 us -> 1.03 us
  between operations: 14.1 us -> 1.04 us
    unnamed x39 -> x34, local copies, waits for them, and re-layouts: 378 us -> 7.61 us
    all_gather x2 -> x0, blocking collectives: 152 us -> none  [dispatch(): full_rows = lax.all_gather(source, 'dp', axis=1, tiled=True)]
    psum x2 -> x0, waiting for transfers between devices: 95 us -> none  [the longest x1 95 us: spread(): return lax.psum(kept, axis)]
    unnamed x6 -> x0, waiting for transfers between devices: 68.2 us -> none
    dot_general x22 -> x0, matrix products: 66 us -> none  [the longest x2 8.13 us: dispatch(): picked = jnp.dot(select_map, full_rows, preferred_element_type=jnp.float32)]
    pallas_call x0 -> x11, Pallas kernels: none -> 50.5 us  [the longest x1 16.9 us: backward(): pl.pallas_call(backward_kernel, grid_spec=pltpu.PrefetchScalarGridSpec(nu...]
    ppermute x0 -> x36, waiting for transfers between devices: none -> 44.4 us  [the longest x12 28.2 us: send_up(): return lax.ppermute(value, 'dp', self.up)]
    ppermute x0 -> x36, starting transfers between devices: none -> 43.3 us  [the longest x12 28.5 us: send_down(): return lax.ppermute(value, 'dp', self.down)]
  transfers between devices with their start and end apart: 8 -> 38, of which waited for: 4 -> 13; matrix products, arithmetic and copies ran while one was open for 53% -> 2% of each run, Pallas kernels for 0% -> 23%
where the time goes in v1:
time: 208 us; the launch traced here: 207 us
  starting transfers between devices  65.6 us (32%)
  waiting for transfers between devices  54 us (26%)
  Pallas kernels  50.5 us (24%)
  blocking collectives  23.8 us (11%)
  local copies, waits for them, and re-layouts  10.7 us (5%)
    ppermute x12, starting transfers between devices, send_down(): return lax.ppermute(value, 'dp', self.down)  28.5 us
    ppermute x12, waiting for transfers between devices, send_up(): return lax.ppermute(value, 'dp', self.up)  28.2 us
    all_to_all x1, blocking collectives, on_device(): lax.all_to_all(outgoing.reshape(columns, exp_dev * 8, 2 * width), 'expert...  23.8 us
    all_to_all x2, starting transfers between devices, give_back(): lax.all_to_all(value.reshape(columns, exp_dev * 8, width), 'expert', 0, 0...  22.3 us
    pallas_call x1, Pallas kernels, backward(): pl.pallas_call(backward_kernel, grid_spec=pltpu.PrefetchScalarGridSpec(nu...  16.9 us
    pallas_call x1, Pallas kernels, forward(): pl.pallas_call(forward_kernel, grid_spec=pltpu.PrefetchScalarGridSpec(num...  16.7 us
    ppermute x12, waiting for transfers between devices, cross(): return lax.ppermute(value, 'dp', self.side)  15.4 us
    ppermute x12, starting transfers between devices, cross(): return lax.ppermute(value, 'dp', self.side)  11 us
  transfers between devices with their start and end apart: 38, of which 13 were waited for; matrix products, arithmetic and copies ran while one was open for 2% of the time, Pallas kernels for 23%

profile of v1, /device:TPU:1, one launch (start us, length us, event | category | flops | bytes accessed | tf_op | source)
XLA Modules:
  0.0 206.7 jit_solution(7826006206662382063)
XLA Ops:
  5.3 23.8 %all_to_all.15 = bf16[16,16,1792]{2,1,0:T(8,128)(2,1)S(1)} all-to-all(bf16[16,16,1792]{2,1,0:T(8,128)(2,1)S(1)} %bitcast.18), channel_id=1, replica_groups=mesh['dp'=8,'expert'=16] {'expert'}, dimensions={0} | all-to-all | bytes 1835008 | tf_op jit(solution)/shard_map/all_to_all | solution.py:425
  34.9 5.1 %collective-permute-done.20.refs_3_ = bf16[256,896]{1,0:T(8,128)(2,1)S(1)} collective-permute-done((bf16[256,896]{1,0:T(8,128)(2,1)S(1)}, bf16[256,896]{1,0:T(8,128)(2,1)S(1)}, u32[]{:S(2)}, u32[]{:S(2)}) %collective-permute-start.20) | collective-permute-done | bytes 458784 | tf_op jit(solution)/shard_map/ppermute | solution.py:74
  40.0 3.8 %collective-permute-start = (bf16[256,896]{1,0:T(8,128)(2,1)S(1)}, bf16[256,896]{1,0:T(8,128)(2,1)S(1)}, u32[]{:S(2)}, u32[]{:S(2)}) collective-permute-start(bf16[256,896]{1,0:T(8,128)(2,1)S(1)} %get-tuple-element.98.refs_0_), channel_id=1, source_target_pairs={{0,96},{16,112},{32,0},{48,16},{64,32},{80,48},{96,64},{112,80},{1... | collective-permute-start | bytes 1376264 | tf_op jit(solution)/shard_map/ppermute | solution.py:71
  44.0 5.9 %collective-permute-done.2.refs_3_ = bf16[256,896]{1,0:T(8,128)(2,1)S(1)} collective-permute-done((bf16[256,896]{1,0:T(8,128)(2,1)S(1)}, bf16[256,896]{1,0:T(8,128)(2,1)S(1)}, u32[]{:S(2)}, u32[]{:S(2)}) %collective-permute-start.2) | collective-permute-done | bytes 458784 | tf_op jit(solution)/shard_map/ppermute | solution.py:74
  49.9 2.6 %collective-permute-done.1.refs_2_ = bf16[256,896]{1,0:T(8,128)(2,1)S(1)} collective-permute-done((bf16[256,896]{1,0:T(8,128)(2,1)S(1)}, bf16[256,896]{1,0:T(8,128)(2,1)S(1)}, u32[]{:S(2)}, u32[]{:S(2)}) %collective-permute-start.1) | collective-permute-done | bytes 458784 | tf_op jit(solution)/shard_map/ppermute | solution.py:68
  57.8 14.3 %collective-permute-done.4.refs_5_ = bf16[256,896]{1,0:T(8,128)(2,1)S(1)} collective-permute-done((bf16[256,896]{1,0:T(8,128)(2,1)S(1)}, bf16[256,896]{1,0:T(8,128)(2,1)S(1)}, u32[]{:S(2)}, u32[]{:S(2)}) %collective-permute-start.4) | collective-permute-done | bytes 458784 | tf_op jit(solution)/shard_map/ppermute | solution.py:68
  74.4 2.6 %collective-permute-start.6 = (bf16[80,896]{1,0:T(8,128)(2,1)S(1)}, bf16[80,896]{1,0:T(8,128)(2,1)S(1)}, u32[]{:S(2)}, u32[]{:S(2)}) collective-permute-start(bf16[80,896]{1,0:T(8,128)(2,1)S(1)} %slice.87), channel_id=1, source_target_pairs={{0,96},{16,112},{32,0},{48,16},{64,32},{80,48},{96,64},{112,80},{1... | collective-permute-start | bytes 430088 | tf_op jit(solution)/shard_map/ppermute | solution.py:71
  80.9 2.7 %collective-permute-start.24 = (bf16[80,896]{1,0:T(8,128)(2,1)}, bf16[80,896]{1,0:T(8,128)(2,1)S(1)}, u32[]{:S(2)}, u32[]{:S(2)}) collective-permute-start(bf16[80,896]{1,0:T(8,128)(2,1)} %slice.97), channel_id=1, source_target_pairs={{0,96},{16,112},{32,0},{48,16},{64,32},{80,48},{96,64},{112,80},{1... | collective-permute-start | bytes 430088 | tf_op jit(solution)/shard_map/ppermute | solution.py:71
  83.8 2.2 %collective-permute-done.7.refs_8_ = bf16[96,896]{1,0:T(8,128)(2,1)S(1)} collective-permute-done((bf16[96,896]{1,0:T(8,128)(2,1)}, bf16[96,896]{1,0:T(8,128)(2,1)S(1)}, u32[]{:S(2)}, u32[]{:S(2)}) %collective-permute-start.7) | collective-permute-done | bytes 172064 | tf_op jit(solution)/shard_map/ppermute | solution.py:74
  87.0 16.7 %forward.1 = (bf16[8,256,896]{2,1,0:T(8,128)(2,1)}, f32[256,256]{1,0:T(8,128)S(1)}, bf16[256,256]{1,0:T(8,128)(2,1)S(1)}, bf16[80,896]{1,0:T(8,128)(2,1)S(1)}, b...) custom-call(s32[8]{0:T(128)S(1)} %stack.35.order_ref, ...), custom_call_target="tpu_custom_call" | custom-call | tf_op jit(solution)/shard_map/forward/pallas_call | solution.py:206
  105.5 2.7 %collective-permute-start.11 = (bf16[80,896]{1,0:T(8,128)(2,1)S(1)}, bf16[80,896]{1,0:T(8,128)(2,1)S(1)}, u32[]{:S(2)}, u32[]{:S(2)}) collective-permute-start(bf16[80,896]{1,0:T(8,128)(2,1)S(1)} %get-tuple-element.63), channel_id=1, source_target_pairs={{0,96},{16,112},{32,0},{48,16},{64,32},{80,48},{96,64},{112,80},{1... | collective-permute-start | bytes 430088 | tf_op jit(solution)/shard_map/ppermute | solution.py:71
  108.2 16.9 %backward.1 = (bf16[8,256,896]{2,1,0:T(8,128)(2,1)}, bf16[256,256]{1,0:T(8,128)(2,1)S(1)}, bf16[256,256]{1,0:T(8,128)(2,1)S(1)}, bf16[80,896]{1,0:T(8,128)(2,1)S...) custom-call(s32[8]{0:T(128)S(1)} %stack.35.order_ref, ...), custom_call_target="tpu_custom_call" | custom-call | tf_op jit(solution)/shard_map/backward/pallas_call | solution.py:280
  125.4 2.7 %collective-permute-start.29 = (bf16[80,896]{1,0:T(8,128)(2,1)S(1)}, bf16[80,896]{1,0:T(8,128)(2,1)S(1)}, u32[]{:S(2)}, u32[]{:S(2)}) collective-permute-start(bf16[80,896]{1,0:T(8,128)(2,1)S(1)} %get-tuple-element.80), channel_id=1, source_target_pairs={{0,96},{16,112},{32,0},{48,16},{64,32},{80,48},{96,64},{112,80},{1... | collective-permute-start | bytes 430088 | tf_op jit(solution)/shard_map/ppermute | solution.py:71
  128.4 2.7 %collective-permute-start.13 = (bf16[256,896]{1,0:T(8,128)(2,1)S(1)}, bf16[256,896]{1,0:T(8,128)(2,1)S(1)}, u32[]{:S(2)}, u32[]{:S(2)}) collective-permute-start(bf16[256,896]{1,0:T(8,128)(2,1)S(1)} %get-tuple-element.65), channel_id=1, source_target_pairs={{0,96},{16,112},{32,0},{48,16},{64,32},{80,48},{96,64},{112,80},{1... | collective-permute-start | bytes 1376264 | tf_op jit(solution)/shard_map/ppermute | solution.py:71
  132.4 2.7 %collective-permute-start.31 = (bf16[256,896]{1,0:T(8,128)(2,1)S(1)}, bf16[256,896]{1,0:T(8,128)(2,1)S(1)}, u32[]{:S(2)}, u32[]{:S(2)}) collective-permute-start(bf16[256,896]{1,0:T(8,128)(2,1)S(1)} %get-tuple-element.82), channel_id=1, source_target_pairs={{0,96},{16,112},{32,0},{48,16},{64,32},{80,48},{96,64},{112,80},{1... | collective-permute-start | bytes 1376264 | tf_op jit(solution)/shard_map/ppermute | solution.py:71
  135.1 3.3 %collective-permute-done.12.got_up = bf16[256,896]{1,0:T(8,128)(2,1)S(1)} collective-permute-done((bf16[256,896]{1,0:T(8,128)(2,1)S(1)}, bf16[256,896]{1,0:T(8,128)(2,1)S(1)}, u32[]{:S(2)}, u32[]{:S(2)}) %collective-permute-start.12) | collective-permute-done | bytes 458784 | tf_op jit(solution)/shard_map/ppermute | solution.py:68
  140.9 2.7 %collective-permute-start.16 = (bf16[256,896]{1,0:T(8,128)(2,1)S(1)}, bf16[256,896]{1,0:T(8,128)(2,1)S(1)}, u32[]{:S(2)}, u32[]{:S(2)}) collective-permute-start(bf16[256,896]{1,0:T(8,128)(2,1)S(1)} %get-tuple-element.68), channel_id=1, source_target_pairs={{0,96},{16,112},{32,0},{48,16},{64,32},{80,48},{96,64},{112,80},{1... | collective-permute-start | bytes 1376264 | tf_op jit(solution)/shard_map/ppermute | solution.py:71
  143.6 4.5 %collective-permute-done.30.got_up = bf16[256,896]{1,0:T(8,128)(2,1)S(1)} collective-permute-done((bf16[256,896]{1,0:T(8,128)(2,1)S(1)}, bf16[256,896]{1,0:T(8,128)(2,1)S(1)}, u32[]{:S(2)}, u32[]{:S(2)}) %collective-permute-start.30) | collective-permute-done | bytes 458784 | tf_op jit(solution)/shard_map/ppermute | solution.py:68
  151.7 2.7 %collective-permute-start.34 = (bf16[256,896]{1,0:T(8,128)(2,1)}, bf16[256,896]{1,0:T(8,128)(2,1)S(1)}, u32[]{:S(2)}, u32[]{:S(2)}) collective-permute-start(bf16[256,896]{1,0:T(8,128)(2,1)} %get-tuple-element.85), channel_id=1, source_target_pairs={{0,96},{16,112},{32,0},{48,16},{64,32},{80,48},{96,64},{112,80},{1... | collective-permute-start | bytes 1376264 | tf_op jit(solution)/shard_map/ppermute | solution.py:71
  154.3 3.5 %collective-permute-done.15.from_below = bf16[256,896]{1,0:T(8,128)(2,1)S(1)} collective-permute-done((bf16[256,896]{1,0:T(8,128)(2,1)S(1)}, bf16[256,896]{1,0:T(8,128)(2,1)S(1)}, u32[]{:S(2)}, u32[]{:S(2)}) %collective-permute-start.15) | collective-permute-done | bytes 458784 | tf_op jit(solution)/shard_map/ppermute | solution.py:68
  160.1 17.8 %all-to-all-start.1 = ((bf16[16,16,896]{2,1,0:T(8,128)(2,1)}), bf16[16,16,896]{2,1,0:T(8,128)(2,1)S(1)}, u32[]{:S(2)}, u32[]{:S(2)}) async-start(bf16[16,16,896]{2,1,0:T(8,128)(2,1)} %bitcast.11), calls=%async_computation.1 | async-start | bytes 917504 | tf_op jit(solution)/shard_map/all_to_all | solution.py:441
  178.9 9.6 %all-to-all-done.1 = bf16[16,16,896]{2,1,0:T(8,128)(2,1)S(1)} async-done(((bf16[16,16,896]{2,1,0:T(8,128)(2,1)}), bf16[16,16,896]{2,1,0:T(8,128)(2,1)S(1)}, u32[]{:S(2)}, u32[]{:S(2)}) %all-to-all-start.1) | async-done | bytes 458784 | tf_op jit(solution)/shard_map/all_to_all | solution.py:441
  188.5 4.5 %all-to-all-start.2 = ((bf16[16,16,896]{2,1,0:T(8,128)(2,1)}), bf16[16,16,896]{2,1,0:T(8,128)(2,1)S(1)}, u32[]{:S(2)}, u32[]{:S(2)}) async-start(bf16[16,16,896]{2,1,0:T(8,128)(2,1)} %bitcast.13), calls=%async_computation.2 | async-start | bytes 917504 | tf_op jit(solution)/shard_map/all_to_all | solution.py:441
  195.0 10.3 %weight_grads.1 = (bf16[2,7168,128]{2,1,0:T(8,128)(2,1)}, bf16[2,7168,128]{2,1,0:T(8,128)(2,1)}, bf16[256,7168]{1,0:T(8,128)(2,1)}) custom-call(s32[8]{0:T(128)S(1)} %stack.35.order_ref, bf16[8,256,896]{2,1,0:T(8,128)(2,1)S(1)} %copy-done, bf16[8,256,896]{2,1,0:T(8,128)(2,1)} %get-tuple-element.90.c_ref, bf16[256,256]{1,0:T(8,128)(2,1)S(1)} %copy-done.4, ...), custom_call_target="tpu_custom_call" | custom-call | tf_op jit(solution)/shard_map/weight_grads/pallas_call | solution.py:319
  (120 shorter events, 39.6 us)
Async XLA Ops:
  31.1 18.7 %collective-permute-start.2 = (bf16[256,896]{1,0:T(8,128)(2,1)S(1)}, bf16[256,896]{1,0:T(8,128)(2,1)S(1)}, u32[]{:S(2)}, u32[]{:S(2)}) collective-permute-start(bf16[256,896]{1,0:T(8,128)(2,1)S(1)} %get-tuple-element.98.refs_0_), channel_id=1, source_target_pairs={{0,16},{16,0},{32,48},{48,32},{64,80},{80,64},{96,112},{112,96},{1... | collective-permute-start | bytes 1376264 | tf_op jit(solution)/shard_map/ppermute | solution.py:74
  32.3 20.2 %collective-permute-start.1 = (bf16[256,896]{1,0:T(8,128)(2,1)S(1)}, bf16[256,896]{1,0:T(8,128)(2,1)S(1)}, u32[]{:S(2)}, u32[]{:S(2)}) collective-permute-start(bf16[256,896]{1,0:T(8,128)(2,1)S(1)} %get-tuple-element.98.refs_0_), channel_id=1, source_target_pairs={{0,32},{16,48},{32,64},{48,80},{64,96},{80,112},{96,0},{112,16},{1... | collective-permute-start | bytes 1376264 | tf_op jit(solution)/shard_map/ppermute | solution.py:68
  33.9 21.6 %collective-permute-start.18 = (bf16[256,896]{1,0:T(8,128)(2,1)S(1)}, bf16[256,896]{1,0:T(8,128)(2,1)S(1)}, u32[]{:S(2)}, u32[]{:S(2)}) collective-permute-start(bf16[256,896]{1,0:T(8,128)(2,1)S(1)} %get-tuple-element.97.refs_0_), channel_id=1, source_target_pairs={{0,96},{16,112},{32,0},{48,16},{64,32},{80,48},{96,64},{112,80},{1... | collective-permute-start | bytes 1376264 | tf_op jit(solution)/shard_map/ppermute | solution.py:71
  43.9 30.2 %collective-permute-start.22 = (bf16[256,896]{1,0:T(8,128)(2,1)S(1)}, bf16[256,896]{1,0:T(8,128)(2,1)S(1)}, u32[]{:S(2)}, u32[]{:S(2)}) collective-permute-start(bf16[256,896]{1,0:T(8,128)(2,1)S(1)} %pad_maximum_fusion.4), channel_id=1, source_target_pairs={{0,32},{16,48},{32,64},{48,80},{64,96},{80,112},{96,0},{112,16},{1... | collective-permute-start | bytes 1376264 | tf_op jit(solution)/shard_map/ppermute | solution.py:68
  52.5 19.6 %collective-permute-start.4 = (bf16[256,896]{1,0:T(8,128)(2,1)S(1)}, bf16[256,896]{1,0:T(8,128)(2,1)S(1)}, u32[]{:S(2)}, u32[]{:S(2)}) collective-permute-start(bf16[256,896]{1,0:T(8,128)(2,1)S(1)} %pad_maximum_fusion.1), channel_id=1, source_target_pairs={{0,32},{16,48},{32,64},{48,80},{64,96},{80,112},{96,0},{112,16},{1... | collective-permute-start | bytes 1376264 | tf_op jit(solution)/shard_map/ppermute | solution.py:68
  53.6 19.7 %collective-permute-start.3 = (bf16[256,896]{1,0:T(8,128)(2,1)S(1)}, bf16[256,896]{1,0:T(8,128)(2,1)S(1)}, u32[]{:S(2)}, u32[]{:S(2)}) collective-permute-start(bf16[256,896]{1,0:T(8,128)(2,1)S(1)} %pad_maximum_fusion), channel_id=1, source_target_pairs={{0,96},{16,112},{32,0},{48,16},{64,32},{80,48},{96,64},{112,80},{1... | collective-permute-start | bytes 1376264 | tf_op jit(solution)/shard_map/ppermute | solution.py:71
  55.6 18.8 %collective-permute-start.21 = (bf16[256,896]{1,0:T(8,128)(2,1)S(1)}, bf16[256,896]{1,0:T(8,128)(2,1)S(1)}, u32[]{:S(2)}, u32[]{:S(2)}) collective-permute-start(bf16[256,896]{1,0:T(8,128)(2,1)S(1)} %pad_maximum_fusion.3), channel_id=1, source_target_pairs={{0,96},{16,112},{32,0},{48,16},{64,32},{80,48},{96,64},{112,80},{1... | collective-permute-start | bytes 1376264 | tf_op jit(solution)/shard_map/ppermute | solution.py:71
  56.1 21.6 %collective-permute-start.5 = (bf16[256,896]{1,0:T(8,128)(2,1)S(1)}, bf16[256,896]{1,0:T(8,128)(2,1)S(1)}, u32[]{:S(2)}, u32[]{:S(2)}) collective-permute-start(bf16[256,896]{1,0:T(8,128)(2,1)S(1)} %pad_maximum_fusion.2), channel_id=1, source_target_pairs={{0,16},{16,0},{32,48},{48,32},{64,80},{80,64},{96,112},{112,96},{1... | collective-permute-start | bytes 1376264 | tf_op jit(solution)/shard_map/ppermute | solution.py:74
  72.1 32.2 %collective-permute-start.23 = (bf16[256,896]{1,0:T(8,128)(2,1)}, bf16[256,896]{1,0:T(8,128)(2,1)}, u32[]{:S(2)}, u32[]{:S(2)}) collective-permute-start(bf16[256,896]{1,0:T(8,128)(2,1)} %pad_maximum_fusion.5), channel_id=1, source_target_pairs={{0,16},{16,0},{32,48},{48,32},{64,80},{80,64},{96,112},{112,96},{1... | collective-permute-start | bytes 1376264 | tf_op jit(solution)/shard_map/ppermute | solution.py:74
  77.8 30.4 %collective-permute-start.25 = (bf16[96,896]{1,0:T(8,128)(2,1)}, bf16[96,896]{1,0:T(8,128)(2,1)S(1)}, u32[]{:S(2)}, u32[]{:S(2)}) collective-permute-start(bf16[96,896]{1,0:T(8,128)(2,1)} %slice.98), channel_id=1, source_target_pairs={{0,16},{16,0},{32,48},{48,32},{64,80},{80,64},{96,112},{112,96},{1... | collective-permute-start | bytes 516104 | tf_op jit(solution)/shard_map/ppermute | solution.py:74
  79.6 25.9 %collective-permute-start.26 = (bf16[80,896]{1,0:T(8,128)(2,1)}, bf16[80,896]{1,0:T(8,128)(2,1)S(1)}, u32[]{:S(2)}, u32[]{:S(2)}) collective-permute-start(bf16[80,896]{1,0:T(8,128)(2,1)} %slice.99), channel_id=1, source_target_pairs={{0,32},{16,48},{32,64},{48,80},{64,96},{80,112},{96,0},{112,16},{1... | collective-permute-start | bytes 430088 | tf_op jit(solution)/shard_map/ppermute | solution.py:68
  80.9 27.2 %collective-permute-start.24 = (bf16[80,896]{1,0:T(8,128)(2,1)}, bf16[80,896]{1,0:T(8,128)(2,1)S(1)}, u32[]{:S(2)}, u32[]{:S(2)}) collective-permute-start(bf16[80,896]{1,0:T(8,128)(2,1)} %slice.97), channel_id=1, source_target_pairs={{0,96},{16,112},{32,0},{48,16},{64,32},{80,48},{96,64},{112,80},{1... | collective-permute-start | bytes 430088 | tf_op jit(solution)/shard_map/ppermute | solution.py:71
  104.3 21.1 %collective-permute-start.9 = (bf16[80,896]{1,0:T(8,128)(2,1)S(1)}, bf16[80,896]{1,0:T(8,128)(2,1)S(1)}, u32[]{:S(2)}, u32[]{:S(2)}) collective-permute-start(bf16[80,896]{1,0:T(8,128)(2,1)S(1)} %get-tuple-element.61), channel_id=1, source_target_pairs={{0,32},{16,48},{32,64},{48,80},{64,96},{80,112},{96,0},{112,16},{1... | collective-permute-start | bytes 430088 | tf_op jit(solution)/shard_map/ppermute | solution.py:68
  104.3 23.8 %collective-permute-start.10 = (bf16[96,896]{1,0:T(8,128)(2,1)S(1)}, bf16[96,896]{1,0:T(8,128)(2,1)S(1)}, u32[]{:S(2)}, u32[]{:S(2)}) collective-permute-start(bf16[96,896]{1,0:T(8,128)(2,1)S(1)} %get-tuple-element.62), channel_id=1, source_target_pairs={{0,16},{16,0},{32,48},{48,32},{64,80},{80,64},{96,112},{112,96},{1... | collective-permute-start | bytes 516104 | tf_op jit(solution)/shard_map/ppermute | solution.py:74
  105.5 22.6 %collective-permute-start.11 = (bf16[80,896]{1,0:T(8,128)(2,1)S(1)}, bf16[80,896]{1,0:T(8,128)(2,1)S(1)}, u32[]{:S(2)}, u32[]{:S(2)}) collective-permute-start(bf16[80,896]{1,0:T(8,128)(2,1)S(1)} %get-tuple-element.63), channel_id=1, source_target_pairs={{0,96},{16,112},{32,0},{48,16},{64,32},{80,48},{96,64},{112,80},{1... | collective-permute-start | bytes 430088 | tf_op jit(solution)/shard_map/ppermute | solution.py:71
  132.4 15.7 %collective-permute-start.30 = (bf16[256,896]{1,0:T(8,128)(2,1)S(1)}, bf16[256,896]{1,0:T(8,128)(2,1)S(1)}, u32[]{:S(2)}, u32[]{:S(2)}) collective-permute-start(bf16[256,896]{1,0:T(8,128)(2,1)S(1)} %get-tuple-element.81), channel_id=1, source_target_pairs={{0,32},{16,48},{32,64},{48,80},{64,96},{80,112},{96,0},{112,16},{1... | collective-permute-start | bytes 1376264 | tf_op jit(solution)/shard_map/ppermute | solution.py:68
  132.4 16.8 %collective-permute-start.31 = (bf16[256,896]{1,0:T(8,128)(2,1)S(1)}, bf16[256,896]{1,0:T(8,128)(2,1)S(1)}, u32[]{:S(2)}, u32[]{:S(2)}) collective-permute-start(bf16[256,896]{1,0:T(8,128)(2,1)S(1)} %get-tuple-element.82), channel_id=1, source_target_pairs={{0,96},{16,112},{32,0},{48,16},{64,32},{80,48},{96,64},{112,80},{1... | collective-permute-start | bytes 1376264 | tf_op jit(solution)/shard_map/ppermute | solution.py:71
  140.8 17.0 %collective-permute-start.15 = (bf16[256,896]{1,0:T(8,128)(2,1)S(1)}, bf16[256,896]{1,0:T(8,128)(2,1)S(1)}, u32[]{:S(2)}, u32[]{:S(2)}) collective-permute-start(bf16[256,896]{1,0:T(8,128)(2,1)S(1)} %get-tuple-element.67), channel_id=1, source_target_pairs={{0,32},{16,48},{32,64},{48,80},{64,96},{80,112},{96,0},{112,16},{1... | collective-permute-start | bytes 1376264 | tf_op jit(solution)/shard_map/ppermute | solution.py:68
  140.9 18.1 %collective-permute-start.16 = (bf16[256,896]{1,0:T(8,128)(2,1)S(1)}, bf16[256,896]{1,0:T(8,128)(2,1)S(1)}, u32[]{:S(2)}, u32[]{:S(2)}) collective-permute-start(bf16[256,896]{1,0:T(8,128)(2,1)S(1)} %get-tuple-element.68), channel_id=1, source_target_pairs={{0,96},{16,112},{32,0},{48,16},{64,32},{80,48},{96,64},{112,80},{1... | collective-permute-start | bytes 1376264 | tf_op jit(solution)/shard_map/ppermute | solution.py:71
  151.7 26.2 %collective-permute-start.33 = (bf16[256,896]{1,0:T(8,128)(2,1)}, bf16[256,896]{1,0:T(8,128)(2,1)S(1)}, u32[]{:S(2)}, u32[]{:S(2)}) collective-permute-start(bf16[256,896]{1,0:T(8,128)(2,1)} %get-tuple-element.84), channel_id=1, source_target_pairs={{0,32},{16,48},{32,64},{48,80},{64,96},{80,112},{96,0},{112,16},{1... | collective-permute-start | bytes 1376264 | tf_op jit(solution)/shard_map/ppermute | solution.py:68
  151.7 26.2 %collective-permute-start.34 = (bf16[256,896]{1,0:T(8,128)(2,1)}, bf16[256,896]{1,0:T(8,128)(2,1)S(1)}, u32[]{:S(2)}, u32[]{:S(2)}) collective-permute-start(bf16[256,896]{1,0:T(8,128)(2,1)} %get-tuple-element.85), channel_id=1, source_target_pairs={{0,96},{16,112},{32,0},{48,16},{64,32},{80,48},{96,64},{112,80},{1... | collective-permute-start | bytes 1376264 | tf_op jit(solution)/shard_map/ppermute | solution.py:71
  157.9 20.0 %collective-permute-start.35 = (bf16[256,896]{1,0:T(8,128)(2,1)}, bf16[256,896]{1,0:T(8,128)(2,1)S(1)}, u32[]{:S(2)}, u32[]{:S(2)}) collective-permute-start(bf16[256,896]{1,0:T(8,128)(2,1)} %get-tuple-element.86), channel_id=1, source_target_pairs={{0,16},{16,0},{32,48},{48,32},{64,80},{80,64},{96,112},{112,96},{1... | collective-permute-start | bytes 1376264 | tf_op jit(solution)/shard_map/ppermute | solution.py:74
  160.1 28.4 %all-to-all-start.1 = ((bf16[16,16,896]{2,1,0:T(8,128)(2,1)}), bf16[16,16,896]{2,1,0:T(8,128)(2,1)S(1)}, u32[]{:S(2)}, u32[]{:S(2)}) async-start(bf16[16,16,896]{2,1,0:T(8,128)(2,1)} %bitcast.11), calls=%async_computation.1 | async-start | bytes 917504 | tf_op jit(solution)/shard_map/all_to_all | solution.py:441
  188.5 16.9 %all-to-all-start.2 = ((bf16[16,16,896]{2,1,0:T(8,128)(2,1)}), bf16[16,16,896]{2,1,0:T(8,128)(2,1)S(1)}, u32[]{:S(2)}, u32[]{:S(2)}) async-start(bf16[16,16,896]{2,1,0:T(8,128)(2,1)} %bitcast.13), calls=%async_computation.2 | async-start | bytes 917504 | tf_op jit(solution)/shard_map/all_to_all | solution.py:441
  (30 other events, 306.0 us)

commit v2 on v0

v2 whole, which is shorter than its diff:
```python
import jax
import jax.numpy as jnp
from jax import lax
from jax.experimental import pallas as pl
from jax.experimental.pallas import tpu as pltpu
from jax.sharding import PartitionSpec as P

BF = jnp.bfloat16
F32 = jnp.float32
LOW, HALF, HIGH = 112, 128, 144
ARRIVING = ((0, 1, 2, 3), (4, 5, 6), (7,))
LEAVING = ((7,), (4, 5, 6), (1, 2, 3, 0))
MIB = 1024 * 1024
SMALL = pltpu.CompilerParams(vmem_limit_bytes=8 * MIB)
LARGE = pltpu.CompilerParams(vmem_limit_bytes=16 * MIB)
HBM = pl.BlockSpec(memory_space=pl.ANY)
VMEM = pl.BlockSpec(memory_space=pltpu.VMEM)
SMEM = pl.BlockSpec(memory_space=pltpu.SMEM)


def dot(a, b, dims=((1,), (0,)), precision=None):
    return lax.dot_general(a, b, (dims, ((), ())), precision=precision, preferred_element_type=F32)


def in_hbm(value):
    return pltpu.with_memory_space_constraint(value, pltpu.HBM)


class Copies:
    def __init__(self, semaphores):
        self.semaphores = semaphores
        self.used = 0

    def start(self, pairs):
        started = []
        for source, target in pairs:
            started.append(pltpu.make_async_copy(source, target, self.semaphores.at[self.used]))
            started[-1].start()
            self.used += 1
        return started


def wait(copies):
    for copy in copies:
        copy.wait()


def dispatch_kernel(
    ids_hbm, gates_hbm, tokens_ref, upstream_ref, x_ref, c_ref, pick_ref, gated_ref,
    ids_ref, gates_ref, held, semaphores,
):
    copies = Copies(semaphores)
    routes = copies.start(((ids_hbm, ids_ref), (gates_hbm, gates_ref)))
    arriving = copies.start(((tokens_ref, held.at[0]), (upstream_ref, held.at[1])))
    total, count = pick_ref.shape
    capacity = 8
    row = lax.broadcasted_iota(jnp.int32, (total, count), 0)
    expert = row // capacity
    wait(routes)
    named = jnp.zeros((total, count), F32)
    gate = jnp.zeros((total, count), F32)
    for k in range(ids_ref.shape[0]):
        hit = ids_ref[k : k + 1, :] == expert
        named = jnp.where(hit, 1.0, named)
        gate = jnp.where(hit, gates_ref[k : k + 1, :], gate)
    sooner = lax.broadcasted_iota(jnp.int32, (count, count), 0)
    later = lax.broadcasted_iota(jnp.int32, (count, count), 1)
    earlier = jnp.where(sooner < later, 1.0, 0.0)
    position = dot(named.astype(BF), earlier.astype(BF))
    chosen = (named > 0.5) & (position == (row % capacity).astype(F32))
    pick = jnp.where(chosen, 1.0, 0.0).astype(BF)
    gated = jnp.where(chosen, gate, 0.0)
    pick_ref[...] = pick
    gated_ref[...] = gated
    wait(arriving)
    x_ref[...] = dot(pick, held[0]).astype(BF)
    c_ref[...] = dot(gated, held[1].astype(F32), precision=lax.Precision.HIGHEST).astype(BF)


def dispatch(ids, gates, tokens, upstream, total):
    count, width = tokens.shape
    return pl.pallas_call(
        dispatch_kernel,
        in_specs=[HBM] * 4,
        out_shape=(
            jax.ShapeDtypeStruct((total, width), BF),
            jax.ShapeDtypeStruct((total, width), BF),
            jax.ShapeDtypeStruct((total, count), BF),
            jax.ShapeDtypeStruct((total, count), F32),
        ),
        scratch_shapes=[
            pltpu.VMEM((ids.shape[1], count), jnp.int32),
            pltpu.VMEM((ids.shape[1], count), F32),
            pltpu.VMEM((2, count, width), BF),
            pltpu.SemaphoreType.DMA((4,)),
        ],
        compiler_params=SMALL,
        name="dispatch",
    )(*[in_hbm(value) for value in (ids.T, gates.T, tokens, upstream)])


class Links:
    def __init__(self, size):
        rings = size // 2
        self.up = [(z * 2 + x, (z + 1) % rings * 2 + x) for z in range(rings) for x in range(2)]
        self.down = [(z * 2 + x, (z - 1) % rings * 2 + x) for z in range(rings) for x in range(2)]
        self.side = [(i, i ^ 1) for i in range(size)]

    def send_up(self, value):
        return lax.ppermute(value, "dp", self.up)

    def send_down(self, value):
        return lax.ppermute(value, "dp", self.down)

    def cross(self, value):
        return lax.ppermute(value, "dp", self.side)


def after(value, *earlier):
    return lax.optimization_barrier((value, *earlier))[0]


def local_call(kernel, name, sizes, *args):
    width = args[0].shape[1]
    shapes = tuple(jax.ShapeDtypeStruct((size, width), BF) for size in sizes)
    return pl.pallas_call(kernel, out_shape=shapes, compiler_params=SMALL, name=name)(*args)


def relay_kernel(above, below, beside, to_down, to_up, to_side):
    to_down[:HALF] = above[:HALF]
    to_down[HALF:] = beside[:LOW]
    to_up[:HALF] = below[HALF:]
    to_up[HALF:] = beside[HIGH:]
    to_side[:HIGH] = above[LOW:]
    to_side[HIGH:] = below[:HIGH]


def ends_kernel(above2, below2, beside2, to_down, to_up):
    to_down[:LOW] = above2[HALF:]
    to_down[LOW:] = beside2[: HALF - LOW]
    to_up[: HALF - LOW] = beside2[HIGH + HALF :]
    to_up[HALF - LOW :] = below2[HALF:]


class Gather:
    def __init__(self, links, own):
        self.links = links
        self.arrived = [(own, links.send_down(own), links.send_up(own), links.cross(own))]

    def relay(self, *earlier):
        links = self.links
        outgoing = local_call(
            relay_kernel,
            "relay",
            (HALF + LOW, HALF + LOW, 2 * HIGH),
            *after(self.arrived[0][1:], *earlier),
        )
        to_down, to_up, to_side = outgoing
        self.arrived.append(
            (links.send_down(to_down), links.send_up(to_up), links.cross(to_side))
        )
        return outgoing

    def ends(self, *earlier):
        links = self.links
        outgoing = local_call(ends_kernel, "ends", (HALF, HALF), *after(self.arrived[1], *earlier))
        self.arrived.append((links.send_down(outgoing[0]), links.send_up(outgoing[1])))
        return outgoing


def arrived_blocks(part, pieces):
    if part == 0:
        return [piece[...] for piece in pieces]
    stack = lambda a, b: jnp.concatenate([a, b], axis=0)
    if part == 1:
        above2, below2, beside2 = pieces
        return [
            stack(above2[:HALF], below2[:HALF]),
            stack(above2[HALF:], beside2[:HIGH]),
            stack(beside2[HIGH:], below2[HALF:]),
        ]
    return [stack(pieces[0][...], pieces[1][...])]


def block_order():
    me = lax.axis_index("dp")
    rings = lax.axis_size("dp") // 2
    z, x = me // 2, me % 2
    steps = ((0, 0), (1, 0), (-1, 0), (0, 1), (2, 0), (1, 1), (-1, 1), (2, 1))
    return jnp.stack([(z + dz + rings) % rings * 2 + (x + dx) % 2 for dz, dx in steps]).astype(
        jnp.int32
    )


def row_slot(shape):
    return lax.broadcasted_iota(jnp.int32, shape, 0) // 8 % 2 == 0


def pair(first, value):
    zero = jnp.zeros_like(value)
    return jnp.concatenate([jnp.where(first, value, zero), jnp.where(first, zero, value)], axis=1)


def features_of(order_ref, block, width):
    return pl.ds(pl.multiple_of(order_ref[block] * width, 128), width)


def load_columns(copies, order_ref, refs, buffers, blocks):
    width = buffers[0].shape[2]
    return [
        copies.start(
            [
                (ref.at[:, features_of(order_ref, block, width), :], buffer.at[i])
                for ref, buffer in zip(refs, buffers)
            ]
        )
        for i, block in enumerate(blocks)
    ]


def load_rows(copies, order_ref, ref, buffer, blocks):
    width = buffer.shape[2]
    return [
        copies.start([(ref.at[:, features_of(order_ref, block, width)], buffer.at[i])])
        for i, block in enumerate(blocks)
    ]


def both(ref, i):
    return jnp.concatenate([ref[i, 0], ref[i, 1]], axis=1)


def column_buffers(blocks, width, hid):
    return [pltpu.VMEM((len(blocks), 2, width, hid), BF)] * 2


def row_buffers(blocks, width, hid):
    return [pltpu.VMEM((len(blocks), 2 * hid, width), BF)]


def semaphores_for(blocks, each):
    return [pltpu.SemaphoreType.DMA((each * len(blocks),))]


NT = ((1,), (1,))
TN = ((0,), (0,))


def gate_up(part, order, pieces, weights, before=None):
    blocks = ARRIVING[part]
    rows, width = 2 * HALF, pieces[0].shape[1]
    hid = weights[0].shape[2]
    last = part == len(ARRIVING) - 1

    def kernel(order_ref, *refs):
        count = len(pieces)
        held_pieces, refs = refs[:count], refs[count:]
        if before is not None:
            before_ref, refs = refs[0], refs[1:]
        columns, pre_ref, refs = refs[:2], refs[2], refs[3:]
        if last:
            hidden_ref, refs = refs[0], refs[1:]
        gate_held, up_held, semaphores = refs
        arriving = load_columns(
            Copies(semaphores), order_ref, columns, (gate_held, up_held), blocks
        )
        first = row_slot((rows, hid))
        for i, value in enumerate(arrived_blocks(part, held_pieces)):
            wait(arriving[i])
            gate = dot(value, both(gate_held, i))
            up = dot(value, both(up_held, i))
            gate = jnp.where(first, gate[:, :hid], gate[:, hid:])
            up = jnp.where(first, up[:, :hid], up[:, hid:])
            so_far = pre_ref if i else before_ref if before is not None else None
            if so_far is not None:
                gate += so_far[:, :hid]
                up += so_far[:, hid:]
            pre_ref[:, :hid] = gate
            pre_ref[:, hid:] = up
        if last:
            gate = pre_ref[:, :hid]
            hidden = (gate * jax.nn.sigmoid(gate) * pre_ref[:, hid:]).astype(BF)
            hidden_ref[...] = pair(first, hidden)

    shapes = [jax.ShapeDtypeStruct((rows, 2 * hid), F32)]
    if last:
        shapes.append(jax.ShapeDtypeStruct((rows, 2 * hid), BF))
    extra = [] if before is None else [before]
    out = pl.pallas_call(
        kernel,
        in_specs=[SMEM] + [VMEM] * (len(pieces) + len(extra)) + [HBM] * 2,
        out_shape=shapes,
        scratch_shapes=column_buffers(blocks, width, hid) + semaphores_for(blocks, 2),
        compiler_params=LARGE,
        name=f"gate_up_{part}",
    )(order, *pieces, *extra, *weights)
    return out if last else out[0]


def output_sums(part, order, hidden, down_flat, width):
    blocks = LEAVING[part]
    rows, units = hidden.shape

    def kernel(order_ref, hidden_ref, down_ref, *refs):
        outs = refs[:-2]
        down_held, semaphores = refs[-2:]
        arriving = load_rows(Copies(semaphores), order_ref, down_ref, down_held, blocks)
        for i in range(len(blocks)):
            wait(arriving[i])
            store_sum(part, i, dot(hidden_ref[...], down_held[i]).astype(BF), outs)

    return pl.pallas_call(
        kernel,
        in_specs=[SMEM, VMEM, HBM],
        out_shape=sum_shapes(part, rows, width),
        scratch_shapes=row_buffers(blocks, width, units // 2) + semaphores_for(blocks, 1),
        compiler_params=LARGE,
        name=f"output_sums_{part}",
    )(order, hidden, down_flat)


def sum_shapes(part, rows, width):
    sizes = (HALF, HALF) if part == 0 else (rows,) * len(LEAVING[part])
    return [jax.ShapeDtypeStruct((size, width), BF) for size in sizes]


def store_sum(part, i, value, outs):
    if part == 0:
        outs[0][...] = value[:HALF]
        outs[1][...] = value[HALF:]
    else:
        outs[i][...] = value


def cotangents(part, order, pieces, down_flat, before=None, pre=None):
    blocks = ARRIVING[part]
    rows, width = 2 * HALF, pieces[0].shape[1]
    hid = down_flat.shape[0] // 2
    last = part == len(ARRIVING) - 1

    def kernel(order_ref, *refs):
        count = len(pieces)
        held_pieces, refs = refs[:count], refs[count:]
        if before is not None:
            before_ref, refs = refs[0], refs[1:]
        if last:
            pre_ref, refs = refs[0], refs[1:]
        down_ref, outs = refs[0], refs[1:-2]
        down_held, semaphores = refs[-2:]
        arriving = load_rows(Copies(semaphores), order_ref, down_ref, down_held, blocks)
        first = row_slot((rows, hid))
        total = before_ref[...] if before is not None else None
        for i, value in enumerate(arrived_blocks(part, held_pieces)):
            wait(arriving[i])
            share = dot(value, down_held[i], NT)
            share = jnp.where(first, share[:, :hid], share[:, hid:])
            total = share if total is None else total + share
        if not last:
            outs[0][...] = total
            return
        gate, up = pre_ref[:, :hid], pre_ref[:, hid:]
        sigmoid = jax.nn.sigmoid(gate)
        gate_diff = (total * up * sigmoid * (1.0 + gate * (1.0 - sigmoid))).astype(BF)
        up_diff = (total * (gate * sigmoid)).astype(BF)
        outs[0][...] = pair(first, gate_diff)
        outs[1][...] = pair(first, up_diff)

    if last:
        shapes = [jax.ShapeDtypeStruct((rows, 2 * hid), BF)] * 2
    else:
        shapes = [jax.ShapeDtypeStruct((rows, hid), F32)]
    extra = [value for value in (before, pre) if value is not None]
    out = pl.pallas_call(
        kernel,
        in_specs=[SMEM] + [VMEM] * (len(pieces) + len(extra)) + [HBM],
        out_shape=shapes,
        scratch_shapes=row_buffers(blocks, width, hid) + semaphores_for(blocks, 1),
        compiler_params=LARGE,
        name=f"cotangents_{part}",
    )(order, *pieces, *extra, down_flat)
    return out if last else out[0]


def input_sums(part, order, diffs, weights, width):
    blocks = LEAVING[part]
    rows, units = diffs[0].shape

    def kernel(order_ref, gate_diff_ref, up_diff_ref, gate_ref, up_ref, *refs):
        outs = refs[:-3]
        gate_held, up_held, semaphores = refs[-3:]
        arriving = load_columns(
            Copies(semaphores), order_ref, (gate_ref, up_ref), (gate_held, up_held), blocks
        )
        for i in range(len(blocks)):
            wait(arriving[i])
            value = dot(gate_diff_ref[...], both(gate_held, i), NT)
            value += dot(up_diff_ref[...], both(up_held, i), NT)
            store_sum(part, i, value.astype(BF), outs)

    return pl.pallas_call(
        kernel,
        in_specs=[SMEM, VMEM, VMEM, HBM, HBM],
        out_shape=sum_shapes(part, rows, width),
        scratch_shapes=column_buffers(blocks, width, units // 2) + semaphores_for(blocks, 2),
        compiler_params=LARGE,
        name=f"input_sums_{part}",
    )(order, *diffs, *weights)


def all_blocks(pieces):
    at = 0
    for part, count in enumerate((4, 3, 2)):
        for block, value in zip(ARRIVING[part], arrived_blocks(part, pieces[at : at + count])):
            yield block, value
        at += count


def column_grads_kernel(order_ref, *refs):
    pieces = refs[:9]
    diffs, outs, held, semaphores = refs[9:11], refs[11:13], refs[13:15], refs[15]
    width, hid = held[0].shape[2:]
    copies = Copies(semaphores)
    leaving = []
    for block, value in all_blocks(pieces):
        for diff_ref, out_ref, held_ref in zip(diffs, outs, held):
            grad = dot(value, diff_ref[...], TN).astype(BF)
            held_ref[block, 0] = grad[:, :hid]
            held_ref[block, 1] = grad[:, hid:]
            target = out_ref.at[:, features_of(order_ref, block, width), :]
            leaving += copies.start([(held_ref.at[block], target)])
    wait(leaving)


def column_grads(order, pieces, diffs):
    width = pieces[0].shape[1]
    hid = diffs[0].shape[1] // 2
    blocks = range(8)
    return pl.pallas_call(
        column_grads_kernel,
        in_specs=[SMEM] + [VMEM] * 11,
        out_specs=[HBM] * 2,
        out_shape=[jax.ShapeDtypeStruct((2, 8 * width, hid), BF)] * 2,
        scratch_shapes=column_buffers(blocks, width, hid) + semaphores_for(blocks, 2),
        compiler_params=LARGE,
        name="column_grads",
    )(order, *pieces, *diffs)


def row_grads_kernel(order_ref, *refs):
    pieces = refs[:9]
    hidden_ref, down_out, held, semaphores = refs[9:]
    width = held.shape[2]
    copies = Copies(semaphores)
    leaving = []
    for block, value in all_blocks(pieces):
        held[block] = dot(hidden_ref[...], value, TN).astype(BF)
        target = down_out.at[:, features_of(order_ref, block, width)]
        leaving += copies.start([(held.at[block], target)])
    wait(leaving)


def row_grads(order, pieces, hidden):
    width = pieces[0].shape[1]
    units = hidden.shape[1]
    blocks = range(8)
    return pl.pallas_call(
        row_grads_kernel,
        in_specs=[SMEM] + [VMEM] * 10,
        out_specs=HBM,
        out_shape=jax.ShapeDtypeStruct((units, 8 * width), BF),
        scratch_shapes=row_buffers(blocks, width, units // 2) + semaphores_for(blocks, 1),
        compiler_params=LARGE,
        name="row_grads",
    )(order, *pieces, hidden)


def wide(value):
    return value.astype(F32)


def second_hop_kernel(far, above1, below1, got_up, got_down, to_up, to_down, to_side):
    to_up[:HALF] = far[:HALF]
    to_up[HALF:] = (wide(above1[:LOW]) + wide(got_up[:LOW])).astype(BF)
    to_down[:HALF] = far[HALF:]
    to_down[HALF:] = (wide(below1[HIGH:]) + wide(got_down[HIGH - HALF :])).astype(BF)
    cut = HALF - LOW
    to_side[:cut] = (wide(above1[LOW:HALF]) + wide(got_up[LOW:])).astype(BF)
    to_side[cut:HIGH] = above1[HALF:]
    to_side[HIGH : HIGH + HALF] = below1[:HALF]
    to_side[HIGH + HALF :] = (wide(below1[HALF:HIGH]) + wide(got_down[: HIGH - HALF])).astype(BF)


def third_hop_kernel(above, below, beside, got_up, got_down, got_side, to_up, to_down, to_side):
    cut = HALF - LOW
    to_up[:LOW] = (wide(above[:LOW]) + wide(got_up[:LOW])).astype(BF)
    to_up[LOW:HALF] = (
        wide(above[LOW:HALF]) + wide(got_up[LOW:HALF]) + wide(got_side[:cut])
    ).astype(BF)
    to_up[HALF:] = (wide(above[HALF:]) + wide(got_side[cut:HIGH])).astype(BF)
    to_down[:HALF] = (wide(below[:HALF]) + wide(got_side[HIGH : HIGH + HALF])).astype(BF)
    to_down[HALF:HIGH] = (
        wide(below[HALF:HIGH]) + wide(got_side[HIGH + HALF :]) + wide(got_down[:cut])
    ).astype(BF)
    to_down[HIGH:] = (wide(below[HIGH:]) + wide(got_down[cut:HALF])).astype(BF)
    to_side[:LOW] = (wide(beside[:LOW]) + wide(got_up[HALF:])).astype(BF)
    to_side[LOW:HIGH] = beside[LOW:HIGH]
    to_side[HIGH:] = (wide(beside[HIGH:]) + wide(got_down[HALF:])).astype(BF)


def both_hops_kernel(*refs):
    whole = 2 * HALF
    outs = refs[11:]
    third_hop_kernel(*refs[:6], *[ref.at[pl.ds(0, whole)] for ref in outs])
    second_hop_kernel(
        *refs[6:11], *[ref.at[pl.ds(whole, ref.shape[0] - whole)] for ref in outs]
    )


def last_kernel(own, from_below, from_above, from_side, total):
    rows = slice(0, 2 * HALF)
    total[...] = (
        (wide(own[...]) + wide(from_side[rows]))
        + (wide(from_below[rows]) + wide(from_above[rows]))
    ).astype(BF)


def final_hop_kernel(above, below, beside, got_up, got_down, got_side, to_up, to_down, to_side):
    got = [ref.at[pl.ds(2 * HALF, ref.shape[0] - 2 * HALF)] for ref in (got_up, got_down, got_side)]
    third_hop_kernel(above, below, beside, *got, to_up, to_down, to_side)


class Sums:
    def __init__(self, links):
        self.links = links

    def send(self, to_up, to_down, to_side):
        links = self.links
        return (links.send_up(to_up), links.send_down(to_down), links.cross(to_side))

    def first(self, sums):
        return (self.links.send_up(sums[0]), self.links.send_down(sums[1]))

    def second(self, *args):
        sizes = (HALF + LOW, HALF + LOW, 2 * HIGH)
        outgoing = local_call(second_hop_kernel, "second_hop", sizes, *args)
        return outgoing, self.send(*outgoing)

    def both(self, *args):
        sizes = (3 * HALF + LOW, 3 * HALF + LOW, 2 * HALF + 2 * HIGH)
        outgoing = local_call(both_hops_kernel, "both_hops", sizes, *args)
        return outgoing, self.send(*outgoing)

    def last(self, *args):
        outgoing = local_call(final_hop_kernel, "third_hop", (2 * HALF,) * 3, *args)
        return outgoing, self.send(*outgoing)

    def total(self, own, got):
        return local_call(last_kernel, "last_hop", (2 * HALF,), own, *got)[0]


def combine_kernel(pick_ref, gated_ref, out_ref, in_ref, mixed_ref, grads_ref):
    mixed_ref[...] = dot(gated_ref[...], wide(out_ref[...]), TN, lax.Precision.HIGHEST).astype(BF)
    grads_ref[...] = dot(pick_ref[...], in_ref[...], TN).astype(BF)


def combine(pick, gated, out_rows, in_rows):
    shape = jax.ShapeDtypeStruct((pick.shape[1], out_rows.shape[1]), BF)
    return pl.pallas_call(
        combine_kernel, out_shape=[shape] * 2, compiler_params=SMALL, name="combine"
    )(pick, gated, out_rows, in_rows)


def on_device(tokens, upstream, expert_ids, gate_values, gate_weight, up_weight, down_weight):
    columns = lax.axis_size("expert")
    exp_dev, hid, features = down_weight.shape
    rows = columns * exp_dev * 8
    width = tokens.shape[1]
    links = Links(lax.axis_size("dp"))
    order = block_order()
    columns_in = (in_hbm(gate_weight), in_hbm(up_weight))
    rows_in = in_hbm(down_weight.reshape(exp_dev * hid, features))

    def exchange(value):
        return lax.all_to_all(
            value.reshape(columns, exp_dev * 8, -1), "expert", 0, 0, tiled=True
        ).reshape(rows, -1)

    x_rows, c_rows, pick, gated = dispatch(expert_ids, gate_values, tokens, upstream, rows)
    arrived = exchange(jnp.concatenate([x_rows, c_rows], axis=1))
    x = Gather(links, arrived[:, :width])
    c = Gather(links, arrived[:, width:])
    x_sent = x.relay()
    pre = gate_up(0, order, after(x.arrived[0], *x_sent), columns_in)
    c_sent = c.relay(pre)
    total = cotangents(0, order, after(c.arrived[0], *c_sent), rows_in)
    x_sent = x.ends(total)
    pre = gate_up(1, order, after(x.arrived[1], *x_sent), columns_in, pre)
    c_sent = c.ends(pre)
    total = cotangents(1, order, after(c.arrived[1], *c_sent), rows_in, total)
    pre, hidden = gate_up(2, order, after(x.arrived[2], total), columns_in, pre)

    hops = Sums(links)
    out_cuts = output_sums(0, order, hidden, rows_in, width)
    out_got = hops.first(out_cuts)
    out_far = output_sums(1, order, after(hidden, *out_cuts, *c.arrived[2]), rows_in, width)
    diffs = cotangents(2, order, after(c.arrived[2], *out_far), rows_in, total, pre)
    sent, out_got = hops.second(*out_far, *after(out_got, *diffs))
    in_cuts = input_sums(0, order, after(diffs, *sent), columns_in, width)
    in_got = hops.first(in_cuts)
    in_far = input_sums(1, order, after(diffs, *in_cuts), columns_in, width)
    out_near = output_sums(2, order, after(hidden, *in_far), rows_in, width)
    sent, got = hops.both(*out_near[:3], *out_got, *in_far, *in_got)
    in_near = input_sums(2, order, after(diffs, *sent), columns_in, width)
    down_grad = row_grads(order, after(sum(c.arrived, ()), *in_near), hidden)
    gate_grad, up_grad = column_grads(order, after(sum(x.arrived, ()), down_grad), diffs)
    sent, in_got = hops.last(*in_near[:3], *after(got, gate_grad))
    out_back = exchange(hops.total(out_near[3], after(got, *sent)))
    in_back = exchange(hops.total(in_near[3], after(in_got, out_back)))
    mixed, token_grads = combine(pick, gated, out_back, in_back)
    return (mixed, token_grads, gate_grad, up_grad, down_grad.reshape(down_weight.shape))


def solution(mesh):
    return jax.shard_map(
        on_device,
        mesh=mesh,
        in_specs=(
            P("expert", "dp"),
            P("expert", "dp"),
            P("expert", None),
            P("expert", None),
            P("expert", None, "dp"),
            P("expert", None, "dp"),
            P("expert", "dp", None),
        ),
        out_specs=(
            P("expert", "dp"),
            P("expert", "dp"),
            P("expert", None, "dp"),
            P("expert", None, "dp"),
            P("expert", "dp", None),
        ),
        check_vma=False,
    )
```

time: 888 us -> 170 us (0.19); the launches traced: 875 us -> 169 us
  local copies, waits for them, and re-layouts: 404 us -> 2.22 us
  waiting for transfers between devices: 180 us -> 10.2 us
  blocking collectives: 152 us -> 67.4 us
  matrix products: 66 us -> 0 us
  Pallas kernels: 0 us -> 48 us
  other arithmetic: 21.4 us -> 0.07 us
  between operations: 14.1 us -> 1.03 us
    unnamed x39 -> x12, local copies, waits for them, and re-layouts: 378 us -> 2.06 us
    all_gather x2 -> x0, blocking collectives: 152 us -> none  [dispatch(): full_rows = lax.all_gather(source, 'dp', axis=1, tiled=True)]
    psum x2 -> x0, waiting for transfers between devices: 95 us -> none  [the longest x1 95 us: spread(): return lax.psum(kept, axis)]
    unnamed x6 -> x0, waiting for transfers between devices: 68.2 us -> none
    all_to_all x0 -> x3, blocking collectives: none -> 67.4 us  [exchange(): lax.all_to_all(value.reshape(columns, exp_dev * 8, -1), 'expert', 0, 0, t...]
    dot_general x22 -> x0, matrix products: 66 us -> none  [the longest x2 8.13 us: dispatch(): picked = jnp.dot(select_map, full_rows, preferred_element_type=jnp.float32)]
    pallas_call x0 -> x25, Pallas kernels: none -> 48 us  [the longest x3 9.11 us: gate_up(): pl.pallas_call(kernel, in_specs=[SMEM] + [VMEM] * (len(pieces) + len(extr...]
    ppermute x0 -> x29, starting transfers between devices: none -> 40 us  [the longest x11 27 us: send_down(): return lax.ppermute(value, 'dp', self.down)]
  transfers between devices with their start and end apart: 8 -> 29, of which waited for: 4 -> 5; matrix products, arithmetic and copies ran while one was open for 53% -> 0% of each run, Pallas kernels for 0% -> 26%
where the time goes in v2:
time: 170 us; the launch traced here: 169 us
  blocking collectives  67.4 us (40%)
  Pallas kernels  48 us (28%)
  starting transfers between devices  40 us (24%)
  waiting for transfers between devices  10.2 us (6%)
  local copies, waits for them, and re-layouts  2.22 us (1%)
    all_to_all x3, blocking collectives, exchange(): lax.all_to_all(value.reshape(columns, exp_dev * 8, -1), 'expert', 0, 0, t...  67.4 us
    ppermute x11, starting transfers between devices, send_down(): return lax.ppermute(value, 'dp', self.down)  27 us
    ppermute x7, waiting for transfers between devices, cross(): return lax.ppermute(value, 'dp', self.side)  9.23 us
    pallas_call x3, Pallas kernels, gate_up(): pl.pallas_call(kernel, in_specs=[SMEM] + [VMEM] * (len(pieces) + len(extr...  9.11 us
    pallas_call x3, Pallas kernels, input_sums(): pl.pallas_call(kernel, in_specs=[SMEM, VMEM, VMEM, HBM, HBM], out_shape=s...  9.01 us
    pallas_call x3, Pallas kernels, cotangents(): pl.pallas_call(kernel, in_specs=[SMEM] + [VMEM] * (len(pieces) + len(extr...  7.81 us
    pallas_call x3, Pallas kernels, output_sums(): pl.pallas_call(kernel, in_specs=[SMEM, VMEM, HBM], out_shape=sum_shapes(p...  7.22 us
    ppermute x7, starting transfers between devices, cross(): return lax.ppermute(value, 'dp', self.side)  6.67 us
  transfers between devices with their start and end apart: 29, of which 5 were waited for; matrix products, arithmetic and copies ran while one was open for 0% of the time, Pallas kernels for 26%

profile of v2, /device:TPU:1, one launch (start us, length us, event | category | flops | bytes accessed | tf_op | source)
XLA Modules:
  0.0 168.8 jit_solution(12915030970192069476)
XLA Ops:
  2.7 23.8 %all_to_all.15 = bf16[16,16,1792]{2,1,0:T(8,128)(2,1)S(1)} all-to-all(bf16[16,16,1792]{2,1,0:T(8,128)(2,1)S(1)} %bitcast.29), channel_id=1, replica_groups=mesh['dp'=8,'expert'=16] {'expert'}, dimensions={0} | all-to-all | bytes 1835008 | tf_op jit(solution)/shard_map/all_to_all | solution.py:584
  31.8 5.6 %collective-permute-done.2.beside.refs_3_ = bf16[256,896]{1,0:T(8,128)(2,1)S(1)} collective-permute-done((bf16[256,896]{1,0:T(8,128)(2,1)S(1)}, bf16[256,896]{1,0:T(8,128)(2,1)S(1)}, u32[]{:S(2)}, u32[]{:S(2)}) %collective-permute-start.2) | collective-permute-done | bytes 458784 | tf_op jit(solution)/shard_map/ppermute | solution.py:116
  37.5 3.8 %collective-permute-start.6 = (bf16[256,896]{1,0:T(8,128)(2,1)S(1)}, bf16[256,896]{1,0:T(8,128)(2,1)S(1)}, u32[]{:S(2)}, u32[]{:S(2)}) collective-permute-start(bf16[256,896]{1,0:T(8,128)(2,1)S(1)} %get-tuple-element.203.refs_0_), channel_id=1, source_target_pairs={{0,96},{16,112},{32,0},{48,16},{64,32},{80,48},{96,64},{112,80},{1... | collective-permute-start | bytes 1376264 | tf_op jit(solution)/shard_map/ppermute | solution.py:113
  44.8 2.5 %collective-permute-done.8.beside.refs_3_ = bf16[256,896]{1,0:T(8,128)(2,1)S(1)} collective-permute-done((bf16[256,896]{1,0:T(8,128)(2,1)S(1)}, bf16[256,896]{1,0:T(8,128)(2,1)S(1)}, u32[]{:S(2)}, u32[]{:S(2)}) %collective-permute-start.8) | collective-permute-done | bytes 458784 | tf_op jit(solution)/shard_map/ppermute | solution.py:116
  51.1 3.4 %gate_up_0.1.refs_3_ = f32[256,256]{1,0:T(8,128)S(1)} custom-call(s32[8]{0:T(128)S(1)} %stack.35.order_ref, bf16[256,896]{1,0:T(8,128)(2,1)S(1)} %get-tuple-element.212.refs_0_, bf16[256,896]{1,0:T(8,128)(2,1)S(1)} %copy-done.4, bf16[256,896]{1,0:T(8,128)(2,1)S(1)} %copy-done.1, bf16[256,896]{1,0:T(8,128)(2,1)S(1)} %collective-permute-done.2.beside.refs_3_, ...), custom_call_target="tpu_custom_call" | custom-call | tf_op jit(solution)/shard_map/gate_up_0/pallas_call | solution.py:289
  55.0 2.2 %collective-permute-start.11 = (bf16[240,896]{1,0:T(8,128)(2,1)S(1)}, bf16[240,896]{1,0:T(8,128)(2,1)S(1)}, u32[]{:S(2)}, u32[]{:S(2)}) collective-permute-start(bf16[240,896]{1,0:T(8,128)(2,1)S(1)} %get-tuple-element.138), channel_id=1, source_target_pairs={{0,96},{16,112},{32,0},{48,16},{64,32},{80,48},{96,64},{112,80},{1... | collective-permute-start | bytes 1290248 | tf_op jit(solution)/shard_map/ppermute | solution.py:113
  58.5 3.2 %cotangents_0.1.refs_3_ = f32[256,128]{1,0:T(8,128)S(1)} custom-call(s32[8]{0:T(128)S(1)} %stack.35.order_ref, bf16[256,896]{1,0:T(8,128)(2,1)S(1)} %get-tuple-element.203.refs_0_, bf16[256,896]{1,0:T(8,128)(2,1)S(1)} %collective-permute-done.6.above.refs_1_, bf16[256,896]{1,0:T(8,128)(2,1)S(1)} %collective-permute-done.7.below.refs_2_, ...), custom_call_target="tpu_custom_call" | custom-call | tf_op jit(solution)/shard_map/cotangents_0/pallas_call | solution.py:373
  64.5 3.6 %gate_up_1.1.refs_2_ = f32[256,256]{1,0:T(8,128)S(1)} custom-call(s32[8]{0:T(128)S(1)} %stack.35.order_ref, bf16[240,896]{1,0:T(8,128)(2,1)} %collective-permute-done.3.above2.refs_0_.refs_4_, bf16[240,896]{1,0:T(8,128)(2,1)} %collective-permute-done.4.below2.refs_1_.refs_5_, bf16[288,896]{1,0:T(8,128)(2,1)S(1)} %collective-permute-done.5.beside2.refs_2_.refs_6_, ...), custom_call_target="tpu_custom_call" | custom-call | tf_op jit(solution)/shard_map/gate_up_1/pallas_call | solution.py:289
  69.3 4.0 %collective-permute-start.14 = (bf16[128,896]{1,0:T(8,128)(2,1)S(1)}, bf16[128,896]{1,0:T(8,128)(2,1)S(1)}, u32[]{:S(2)}, u32[]{:S(2)}) collective-permute-start(bf16[128,896]{1,0:T(8,128)(2,1)S(1)} %get-tuple-element.156), channel_id=1, source_target_pairs={{0,96},{16,112},{32,0},{48,16},{64,32},{80,48},{96,64},{112,80},{1... | collective-permute-start | bytes 688136 | tf_op jit(solution)/shard_map/ppermute | solution.py:113
  73.3 2.7 %cotangents_1.1.refs_2_ = f32[256,128]{1,0:T(8,128)S(1)} custom-call(s32[8]{0:T(128)S(1)} %stack.35.order_ref, bf16[240,896]{1,0:T(8,128)(2,1)S(1)} %collective-permute-done.11.above2.refs_0_.refs_4_, bf16[240,896]{1,0:T(8,128)(2,1)S(1)} %collective-permute-done.12.below2.refs_1_.refs_5_, ...), custom_call_target="tpu_custom_call" | custom-call | tf_op jit(solution)/shard_map/cotangents_1/pallas_call | solution.py:373
  76.0 2.2 %gate_up_2.1 = (f32[256,256]{1,0:T(8,128)S(1)}, bf16[256,256]{1,0:T(8,128)(2,1)S(1)}) custom-call(s32[8]{0:T(128)S(1)} %stack.35.order_ref, bf16[128,896]{1,0:T(8,128)(2,1)S(1)} %collective-permute-done.9.refs_0_.refs_7_, bf16[128,896]{1,0:T(8,128)(2,1)S(1)} %collective-permute-done.10.refs_1_.refs_8_, f32[256,256]{1,0:T(8,128)S(1)} %gate_up_1.1.refs_2_, ...), custom_call_target="tpu_custom_call" | custom-call | tf_op jit(solution)/shard_map/gate_up_2/pallas_call | solution.py:289
  80.4 2.7 %collective-permute-start.17 = (bf16[128,896]{1,0:T(8,128)(2,1)S(1)}, bf16[128,896]{1,0:T(8,128)(2,1)S(1)}, u32[]{:S(2)}, u32[]{:S(2)}) collective-permute-start(bf16[128,896]{1,0:T(8,128)(2,1)S(1)} %get-tuple-element.165), channel_id=1, source_target_pairs={{0,96},{16,112},{32,0},{48,16},{64,32},{80,48},{96,64},{112,80},{1... | collective-permute-start | bytes 688136 | tf_op jit(solution)/shard_map/ppermute | solution.py:113
  83.1 2.5 %output_sums_1.1 = (bf16[256,896]{1,0:T(8,128)(2,1)S(1)}, bf16[256,896]{1,0:T(8,128)(2,1)S(1)}, bf16[256,896]{1,0:T(8,128)(2,1)S(1)}) custom-call(s32[8]{0:T(128)S(1)} %stack.35.order_ref, bf16[256,256]{1,0:T(8,128)(2,1)S(1)} %get-tuple-element.189.hidden_ref.refs_9_, bf16[256,7168]{1,0:T(8,128)(2,1)} %bitcast.25), custom_call_target="tpu_custom_call" | custom-call | tf_op jit(solution)/shard_map/output_sums_1/pallas_call | solution.py:312
  88.7 2.7 %collective-permute-start.19 = (bf16[240,896]{1,0:T(8,128)(2,1)S(1)}, bf16[240,896]{1,0:T(8,128)(2,1)S(1)}, u32[]{:S(2)}, u32[]{:S(2)}) collective-permute-start(bf16[240,896]{1,0:T(8,128)(2,1)S(1)} %get-tuple-element.178), channel_id=1, source_target_pairs={{0,96},{16,112},{32,0},{48,16},{64,32},{80,48},{96,64},{112,80},{1... | collective-permute-start | bytes 1290248 | tf_op jit(solution)/shard_map/ppermute | solution.py:113
  91.4 2.2 %input_sums_0.1 = (bf16[128,896]{1,0:T(8,128)(2,1)S(1)}, bf16[128,896]{1,0:T(8,128)(2,1)S(1)}) custom-call(s32[8]{0:T(128)S(1)} %stack.35.order_ref, bf16[256,256]{1,0:T(8,128)(2,1)S(1)} %get-tuple-element.197.gate_diff_ref.refs_9_, bf16[256,256]{1,0:T(8,128)(2,1)S(1)} %get-tuple-element.198.up_diff_ref.refs_10_, bf16[2,7168,128]{2,1,0:T(8,128)(2,1)} %gate_ref.5, ...), custom_call_target="tpu_custom_call" | custom-call | tf_op jit(solution)/shard_map/input_sums_0/pallas_call | solution.py:400
  93.7 2.7 %collective-permute-start.22 = (bf16[128,896]{1,0:T(8,128)(2,1)S(1)}, bf16[128,896]{1,0:T(8,128)(2,1)S(1)}, u32[]{:S(2)}, u32[]{:S(2)}) collective-permute-start(bf16[128,896]{1,0:T(8,128)(2,1)S(1)} %get-tuple-element.183), channel_id=1, source_target_pairs={{0,96},{16,112},{32,0},{48,16},{64,32},{80,48},{96,64},{112,80},{1... | collective-permute-start | bytes 688136 | tf_op jit(solution)/shard_map/ppermute | solution.py:113
  96.3 3.2 %input_sums_1.1 = (bf16[256,896]{1,0:T(8,128)(2,1)S(1)}, bf16[256,896]{1,0:T(8,128)(2,1)S(1)}, bf16[256,896]{1,0:T(8,128)(2,1)S(1)}) custom-call(s32[8]{0:T(128)S(1)} %stack.35.order_ref, bf16[256,256]{1,0:T(8,128)(2,1)S(1)} %get-tuple-element.197.gate_diff_ref.refs_9_, bf16[256,256]{1,0:T(8,128)(2,1)S(1)} %get-tuple-element.198.up_diff_ref.refs_10_, ...), custom_call_target="tpu_custom_call" | custom-call | tf_op jit(solution)/shard_map/input_sums_1/pallas_call | solution.py:400
  99.5 2.8 %output_sums_2.1 = (bf16[256,896]{1,0:T(8,128)(2,1)S(1)}, bf16[256,896]{1,0:T(8,128)(2,1)S(1)}, bf16[256,896]{1,0:T(8,128)(2,1)S(1)}, bf16[256,896]{1,0:T(8,128)(2,1)S(1)}) custom-call(s32[8]{0:T(128)S(1)} %stack.35.order_ref, bf16[256,256]{1,0:T(8,128)(2,1)S(1)} %get-tuple-element.189.hidden_ref.refs_9_, bf16[256,7168]{1,0:T(8,128)(2,1)} %bitcast.27), custom_call_target="tpu_custom_call" | custom-call | tf_op jit(solution)/shard_map/output_sums_2/pallas_call | solution.py:312
  104.4 2.7 %collective-permute-start.24 = (bf16[496,896]{1,0:T(8,128)(2,1)S(1)}, bf16[496,896]{1,0:T(8,128)(2,1)S(1)}, u32[]{:S(2)}, u32[]{:S(2)}) collective-permute-start(bf16[496,896]{1,0:T(8,128)(2,1)S(1)} %get-tuple-element.195), channel_id=1, source_target_pairs={{0,96},{16,112},{32,0},{48,16},{64,32},{80,48},{96,64},{112,80},{1... | collective-permute-start | bytes 2666504 | tf_op jit(solution)/shard_map/ppermute | solution.py:113
  107.0 3.7 %input_sums_2.1 = (bf16[256,896]{1,0:T(8,128)(2,1)S(1)}, bf16[256,896]{1,0:T(8,128)(2,1)S(1)}, bf16[256,896]{1,0:T(8,128)(2,1)S(1)}, bf16[256,896]{1,0:T(8,128)(2,1)S(1)}) custom-call(s32[8]{0:T(128)S(1)} %stack.35.order_ref, bf16[256,256]{1,0:T(8,128)(2,1)S(1)} %get-tuple-element.197.gate_diff_ref.refs_9_, ...), custom_call_target="tpu_custom_call" | custom-call | tf_op jit(solution)/shard_map/input_sums_2/pallas_call | solution.py:400
  110.7 2.8 %row_grads.1 = bf16[256,7168]{1,0:T(8,128)(2,1)} custom-call(s32[8]{0:T(128)S(1)} %stack.35.order_ref, bf16[256,896]{1,0:T(8,128)(2,1)S(1)} %get-tuple-element.203.refs_0_, bf16[256,896]{1,0:T(8,128)(2,1)S(1)} %collective-permute-done.6.above.refs_1_, bf16[256,896]{1,0:T(8,128)(2,1)S(1)} %collective-permute-done.7.below.refs_2_, ...), custom_call_target="tpu_custom_call" | custom-call | tf_op jit(solution)/shard_map/row_grads/pallas_call | solution.py:466
  113.5 4.7 %column_grads.1 = (bf16[2,7168,128]{2,1,0:T(8,128)(2,1)}, bf16[2,7168,128]{2,1,0:T(8,128)(2,1)}) custom-call(s32[8]{0:T(128)S(1)} %stack.35.order_ref, bf16[256,896]{1,0:T(8,128)(2,1)S(1)} %get-tuple-element.212.refs_0_, bf16[256,896]{1,0:T(8,128)(2,1)S(1)} %copy-done.5, bf16[256,896]{1,0:T(8,128)(2,1)S(1)} %copy-done.2, ...), custom_call_target="tpu_custom_call" | custom-call | tf_op jit(solution)/shard_map/column_grads/pallas_call | solution.py:438
  123.6 29.4 %all_to_all.16 = bf16[16,16,896]{2,1,0:T(8,128)(2,1)S(1)} all-to-all(bf16[16,16,896]{2,1,0:T(8,128)(2,1)S(1)} %bitcast.18), channel_id=1, replica_groups=mesh['dp'=8,'expert'=16] {'expert'}, dimensions={0} | all-to-all | bytes 917504 | tf_op jit(solution)/shard_map/all_to_all | solution.py:584
  153.2 14.3 %all_to_all.17 = bf16[16,16,896]{2,1,0:T(8,128)(2,1)S(1)} all-to-all(bf16[16,16,896]{2,1,0:T(8,128)(2,1)S(1)} %bitcast.21), channel_id=1, replica_groups=mesh['dp'=8,'expert'=16] {'expert'}, dimensions={0} | all-to-all | bytes 917504 | tf_op jit(solution)/shard_map/all_to_all | solution.py:584
  (77 shorter events, 34.8 us)
Async XLA Ops:
  26.5 10.9 %collective-permute-start.2 = (bf16[256,896]{1,0:T(8,128)(2,1)S(1)}, bf16[256,896]{1,0:T(8,128)(2,1)S(1)}, u32[]{:S(2)}, u32[]{:S(2)}) collective-permute-start(bf16[256,896]{1,0:T(8,128)(2,1)S(1)} %get-tuple-element.212.refs_0_), channel_id=1, source_target_pairs={{0,16},{16,0},{32,48},{48,32},{64,80},{80,64},{96,112},{112,96},{1... | collective-permute-start | bytes 1376264 | tf_op jit(solution)/shard_map/ppermute | solution.py:116
  26.9 14.3 %collective-permute-start.1 = (bf16[256,896]{1,0:T(8,128)(2,1)S(1)}, bf16[256,896]{1,0:T(8,128)(2,1)S(1)}, u32[]{:S(2)}, u32[]{:S(2)}) collective-permute-start(bf16[256,896]{1,0:T(8,128)(2,1)S(1)} %get-tuple-element.212.refs_0_), channel_id=1, source_target_pairs={{0,32},{16,48},{32,64},{48,80},{64,96},{80,112},{96,0},{112,16},{1... | collective-permute-start | bytes 1376264 | tf_op jit(solution)/shard_map/ppermute | solution.py:110
  28.6 12.6 %collective-permute-start = (bf16[256,896]{1,0:T(8,128)(2,1)S(1)}, bf16[256,896]{1,0:T(8,128)(2,1)S(1)}, u32[]{:S(2)}, u32[]{:S(2)}) collective-permute-start(bf16[256,896]{1,0:T(8,128)(2,1)S(1)} %get-tuple-element.212.refs_0_), channel_id=1, source_target_pairs={{0,96},{16,112},{32,0},{48,16},{64,32},{80,48},{96,64},{112,80},{1... | collective-permute-start | bytes 1376264 | tf_op jit(solution)/shard_map/ppermute | solution.py:113
  30.7 16.6 %collective-permute-start.8 = (bf16[256,896]{1,0:T(8,128)(2,1)S(1)}, bf16[256,896]{1,0:T(8,128)(2,1)S(1)}, u32[]{:S(2)}, u32[]{:S(2)}) collective-permute-start(bf16[256,896]{1,0:T(8,128)(2,1)S(1)} %get-tuple-element.203.refs_0_), channel_id=1, source_target_pairs={{0,16},{16,0},{32,48},{48,32},{64,80},{80,64},{96,112},{112,96},{1... | collective-permute-start | bytes 1376264 | tf_op jit(solution)/shard_map/ppermute | solution.py:116
  31.8 22.6 %collective-permute-start.7 = (bf16[256,896]{1,0:T(8,128)(2,1)S(1)}, bf16[256,896]{1,0:T(8,128)(2,1)S(1)}, u32[]{:S(2)}, u32[]{:S(2)}) collective-permute-start(bf16[256,896]{1,0:T(8,128)(2,1)S(1)} %get-tuple-element.203.refs_0_), channel_id=1, source_target_pairs={{0,32},{16,48},{32,64},{48,80},{64,96},{80,112},{96,0},{112,16},{1... | collective-permute-start | bytes 1376264 | tf_op jit(solution)/shard_map/ppermute | solution.py:110
  37.5 17.0 %collective-permute-start.6 = (bf16[256,896]{1,0:T(8,128)(2,1)S(1)}, bf16[256,896]{1,0:T(8,128)(2,1)S(1)}, u32[]{:S(2)}, u32[]{:S(2)}) collective-permute-start(bf16[256,896]{1,0:T(8,128)(2,1)S(1)} %get-tuple-element.203.refs_0_), channel_id=1, source_target_pairs={{0,96},{16,112},{32,0},{48,16},{64,32},{80,48},{96,64},{112,80},{1... | collective-permute-start | bytes 1376264 | tf_op jit(solution)/shard_map/ppermute | solution.py:113
  42.5 14.7 %collective-permute-start.3 = (bf16[240,896]{1,0:T(8,128)(2,1)}, bf16[240,896]{1,0:T(8,128)(2,1)}, u32[]{:S(2)}, u32[]{:S(2)}) collective-permute-start(bf16[240,896]{1,0:T(8,128)(2,1)} %get-tuple-element.128), channel_id=1, source_target_pairs={{0,96},{16,112},{32,0},{48,16},{64,32},{80,48},{96,64},{112,80},{1... | collective-permute-start | bytes 1290248 | tf_op jit(solution)/shard_map/ppermute | solution.py:113
  43.7 18.0 %collective-permute-start.5 = (bf16[288,896]{1,0:T(8,128)(2,1)}, bf16[288,896]{1,0:T(8,128)(2,1)S(1)}, u32[]{:S(2)}, u32[]{:S(2)}) collective-permute-start(bf16[288,896]{1,0:T(8,128)(2,1)} %get-tuple-element.130), channel_id=1, source_target_pairs={{0,16},{16,0},{32,48},{48,32},{64,80},{80,64},{96,112},{112,96},{1... | collective-permute-start | bytes 1548296 | tf_op jit(solution)/shard_map/ppermute | solution.py:116
  47.3 14.4 %collective-permute-start.4 = (bf16[240,896]{1,0:T(8,128)(2,1)}, bf16[240,896]{1,0:T(8,128)(2,1)}, u32[]{:S(2)}, u32[]{:S(2)}) collective-permute-start(bf16[240,896]{1,0:T(8,128)(2,1)} %get-tuple-element.129), channel_id=1, source_target_pairs={{0,32},{16,48},{32,64},{48,80},{64,96},{80,112},{96,0},{112,16},{1... | collective-permute-start | bytes 1290248 | tf_op jit(solution)/shard_map/ppermute | solution.py:110
  54.6 14.7 %collective-permute-start.13 = (bf16[288,896]{1,0:T(8,128)(2,1)S(1)}, bf16[288,896]{1,0:T(8,128)(2,1)S(1)}, u32[]{:S(2)}, u32[]{:S(2)}) collective-permute-start(bf16[288,896]{1,0:T(8,128)(2,1)S(1)} %get-tuple-element.140), channel_id=1, source_target_pairs={{0,16},{16,0},{32,48},{48,32},{64,80},{80,64},{96,112},{112,96},{1... | collective-permute-start | bytes 1548296 | tf_op jit(solution)/shard_map/ppermute | solution.py:116
  55.0 13.1 %collective-permute-start.11 = (bf16[240,896]{1,0:T(8,128)(2,1)S(1)}, bf16[240,896]{1,0:T(8,128)(2,1)S(1)}, u32[]{:S(2)}, u32[]{:S(2)}) collective-permute-start(bf16[240,896]{1,0:T(8,128)(2,1)S(1)} %get-tuple-element.138), channel_id=1, source_target_pairs={{0,96},{16,112},{32,0},{48,16},{64,32},{80,48},{96,64},{112,80},{1... | collective-permute-start | bytes 1290248 | tf_op jit(solution)/shard_map/ppermute | solution.py:113
  57.3 10.8 %collective-permute-start.12 = (bf16[240,896]{1,0:T(8,128)(2,1)S(1)}, bf16[240,896]{1,0:T(8,128)(2,1)S(1)}, u32[]{:S(2)}, u32[]{:S(2)}) collective-permute-start(bf16[240,896]{1,0:T(8,128)(2,1)S(1)} %get-tuple-element.139), channel_id=1, source_target_pairs={{0,32},{16,48},{32,64},{48,80},{64,96},{80,112},{96,0},{112,16},{1... | collective-permute-start | bytes 1290248 | tf_op jit(solution)/shard_map/ppermute | solution.py:110
  62.9 13.1 %collective-permute-start.9 = (bf16[128,896]{1,0:T(8,128)(2,1)S(1)}, bf16[128,896]{1,0:T(8,128)(2,1)S(1)}, u32[]{:S(2)}, u32[]{:S(2)}) collective-permute-start(bf16[128,896]{1,0:T(8,128)(2,1)S(1)} %get-tuple-element.148), channel_id=1, source_target_pairs={{0,96},{16,112},{32,0},{48,16},{64,32},{80,48},{96,64},{112,80},{1... | collective-permute-start | bytes 688136 | tf_op jit(solution)/shard_map/ppermute | solution.py:113
  64.4 11.6 %collective-permute-start.10 = (bf16[128,896]{1,0:T(8,128)(2,1)S(1)}, bf16[128,896]{1,0:T(8,128)(2,1)S(1)}, u32[]{:S(2)}, u32[]{:S(2)}) collective-permute-start(bf16[128,896]{1,0:T(8,128)(2,1)S(1)} %get-tuple-element.149), channel_id=1, source_target_pairs={{0,32},{16,48},{32,64},{48,80},{64,96},{80,112},{96,0},{112,16},{1... | collective-permute-start | bytes 688136 | tf_op jit(solution)/shard_map/ppermute | solution.py:110
  69.3 13.8 %collective-permute-start.14 = (bf16[128,896]{1,0:T(8,128)(2,1)S(1)}, bf16[128,896]{1,0:T(8,128)(2,1)S(1)}, u32[]{:S(2)}, u32[]{:S(2)}) collective-permute-start(bf16[128,896]{1,0:T(8,128)(2,1)S(1)} %get-tuple-element.156), channel_id=1, source_target_pairs={{0,96},{16,112},{32,0},{48,16},{64,32},{80,48},{96,64},{112,80},{1... | collective-permute-start | bytes 688136 | tf_op jit(solution)/shard_map/ppermute | solution.py:113
  88.5 13.8 %collective-permute-start.20 = (bf16[288,896]{1,0:T(8,128)(2,1)S(1)}, bf16[288,896]{1,0:T(8,128)(2,1)S(1)}, u32[]{:S(2)}, u32[]{:S(2)}) collective-permute-start(bf16[288,896]{1,0:T(8,128)(2,1)S(1)} %get-tuple-element.179), channel_id=1, source_target_pairs={{0,16},{16,0},{32,48},{48,32},{64,80},{80,64},{96,112},{112,96},{1... | collective-permute-start | bytes 1548296 | tf_op jit(solution)/shard_map/ppermute | solution.py:116
  88.6 13.7 %collective-permute-start.18 = (bf16[240,896]{1,0:T(8,128)(2,1)S(1)}, bf16[240,896]{1,0:T(8,128)(2,1)S(1)}, u32[]{:S(2)}, u32[]{:S(2)}) collective-permute-start(bf16[240,896]{1,0:T(8,128)(2,1)S(1)} %get-tuple-element.177), channel_id=1, source_target_pairs={{0,32},{16,48},{32,64},{48,80},{64,96},{80,112},{96,0},{112,16},{1... | collective-permute-start | bytes 1290248 | tf_op jit(solution)/shard_map/ppermute | solution.py:110
  88.7 13.7 %collective-permute-start.19 = (bf16[240,896]{1,0:T(8,128)(2,1)S(1)}, bf16[240,896]{1,0:T(8,128)(2,1)S(1)}, u32[]{:S(2)}, u32[]{:S(2)}) collective-permute-start(bf16[240,896]{1,0:T(8,128)(2,1)S(1)} %get-tuple-element.178), channel_id=1, source_target_pairs={{0,96},{16,112},{32,0},{48,16},{64,32},{80,48},{96,64},{112,80},{1... | collective-permute-start | bytes 1290248 | tf_op jit(solution)/shard_map/ppermute | solution.py:113
  102.9 15.3 %collective-permute-start.25 = (bf16[544,896]{1,0:T(8,128)(2,1)S(1)}, bf16[544,896]{1,0:T(8,128)(2,1)S(1)}, u32[]{:S(2)}, u32[]{:S(2)}) collective-permute-start(bf16[544,896]{1,0:T(8,128)(2,1)S(1)} %get-tuple-element.196), channel_id=1, source_target_pairs={{0,16},{16,0},{32,48},{48,32},{64,80},{80,64},{96,112},{112,96},{1... | collective-permute-start | bytes 2924552 | tf_op jit(solution)/shard_map/ppermute | solution.py:116
  104.4 13.9 %collective-permute-start.23 = (bf16[496,896]{1,0:T(8,128)(2,1)S(1)}, bf16[496,896]{1,0:T(8,128)(2,1)S(1)}, u32[]{:S(2)}, u32[]{:S(2)}) collective-permute-start(bf16[496,896]{1,0:T(8,128)(2,1)S(1)} %get-tuple-element.194), channel_id=1, source_target_pairs={{0,32},{16,48},{32,64},{48,80},{64,96},{80,112},{96,0},{112,16},{1... | collective-permute-start | bytes 2666504 | tf_op jit(solution)/shard_map/ppermute | solution.py:110
  104.4 13.9 %collective-permute-start.24 = (bf16[496,896]{1,0:T(8,128)(2,1)S(1)}, bf16[496,896]{1,0:T(8,128)(2,1)S(1)}, u32[]{:S(2)}, u32[]{:S(2)}) collective-permute-start(bf16[496,896]{1,0:T(8,128)(2,1)S(1)} %get-tuple-element.195), channel_id=1, source_target_pairs={{0,96},{16,112},{32,0},{48,16},{64,32},{80,48},{96,64},{112,80},{1... | collective-permute-start | bytes 2666504 | tf_op jit(solution)/shard_map/ppermute | solution.py:113
  118.6 34.4 %collective-permute-start.26 = (bf16[256,896]{1,0:T(8,128)(2,1)S(1)}, bf16[256,896]{1,0:T(8,128)(2,1)S(1)}, u32[]{:S(2)}, u32[]{:S(2)}) collective-permute-start(bf16[256,896]{1,0:T(8,128)(2,1)S(1)} %get-tuple-element.225), channel_id=1, source_target_pairs={{0,32},{16,48},{32,64},{48,80},{64,96},{80,112},{96,0},{112,16},{1... | collective-permute-start | bytes 1376264 | tf_op jit(solution)/shard_map/ppermute | solution.py:110
  119.9 33.1 %collective-permute-start.27 = (bf16[256,896]{1,0:T(8,128)(2,1)S(1)}, bf16[256,896]{1,0:T(8,128)(2,1)S(1)}, u32[]{:S(2)}, u32[]{:S(2)}) collective-permute-start(bf16[256,896]{1,0:T(8,128)(2,1)S(1)} %get-tuple-element.226), channel_id=1, source_target_pairs={{0,96},{16,112},{32,0},{48,16},{64,32},{80,48},{96,64},{112,80},{1... | collective-permute-start | bytes 1376264 | tf_op jit(solution)/shard_map/ppermute | solution.py:113
  121.3 31.7 %collective-permute-start.28 = (bf16[256,896]{1,0:T(8,128)(2,1)S(1)}, bf16[256,896]{1,0:T(8,128)(2,1)S(1)}, u32[]{:S(2)}, u32[]{:S(2)}) collective-permute-start(bf16[256,896]{1,0:T(8,128)(2,1)S(1)} %get-tuple-element.227), channel_id=1, source_target_pairs={{0,16},{16,0},{32,48},{48,32},{64,80},{80,64},{96,112},{112,96},{1... | collective-permute-start | bytes 1376264 | tf_op jit(solution)/shard_map/ppermute | solution.py:116
  (11 other events, 63.4 us)

commit v3 on v2

--- a/solution.py
+++ b/solution.py
@@ -7,7 +7,8 @@
 
 BF = jnp.bfloat16
 F32 = jnp.float32
-LOW, HALF, HIGH = 112, 128, 144
+HALF = 128
+GATHER_LOW, OUT_LOW, IN_LOW = 112, 64, 112
 ARRIVING = ((0, 1, 2, 3), (4, 5, 6), (7,))
 LEAVING = ((7,), (4, 5, 6), (1, 2, 3, 0))
 MIB = 1024 * 1024
@@ -15,7 +16,6 @@
 LARGE = pltpu.CompilerParams(vmem_limit_bytes=16 * MIB)
 HBM = pl.BlockSpec(memory_space=pl.ANY)
 VMEM = pl.BlockSpec(memory_space=pltpu.VMEM)
-SMEM = pl.BlockSpec(memory_space=pltpu.SMEM)
 
 
 def dot(a, b, dims=((1,), (0,)), precision=None):
@@ -127,19 +127,25 @@
 
 
 def relay_kernel(above, below, beside, to_down, to_up, to_side):
+    low, high = GATHER_LOW, 2 * HALF - GATHER_LOW
     to_down[:HALF] = above[:HALF]
-    to_down[HALF:] = beside[:LOW]
+    to_down[HALF:] = beside[:low]
     to_up[:HALF] = below[HALF:]
-    to_up[HALF:] = beside[HIGH:]
-    to_side[:HIGH] = above[LOW:]
-    to_side[HIGH:] = below[:HIGH]
+    to_up[HALF:] = beside[high:]
+    to_side[:high] = above[low:]
+    to_side[high:] = below[:high]
 
 
 def ends_kernel(above2, below2, beside2, to_down, to_up):
-    to_down[:LOW] = above2[HALF:]
-    to_down[LOW:] = beside2[: HALF - LOW]
-    to_up[: HALF - LOW] = beside2[HIGH + HALF :]
-    to_up[HALF - LOW :] = below2[HALF:]
+    low, high = GATHER_LOW, 2 * HALF - GATHER_LOW
+    to_down[:low] = above2[HALF:]
+    to_down[low:] = beside2[: HALF - low]
+    to_up[: HALF - low] = beside2[high + HALF :]
+    to_up[HALF - low :] = below2[HALF:]
+
+
+def hop_sizes(low):
+    return (HALF + low, HALF + low, 2 * (2 * HALF - low))
 
 
 class Gather:
@@ -152,7 +158,7 @@
         outgoing = local_call(
             relay_kernel,
             "relay",
-            (HALF + LOW, HALF + LOW, 2 * HIGH),
+            hop_sizes(GATHER_LOW),
             *after(self.arrived[0][1:], *earlier),
         )
         to_down, to_up, to_side = outgoing
@@ -174,22 +180,25 @@
     stack = lambda a, b: jnp.concatenate([a, b], axis=0)
     if part == 1:
         above2, below2, beside2 = pieces
+        high = 2 * HALF - GATHER_LOW
         return [
             stack(above2[:HALF], below2[:HALF]),
-            stack(above2[HALF:], beside2[:HIGH]),
-            stack(beside2[HIGH:], below2[HALF:]),
+            stack(above2[HALF:], beside2[:high]),
+            stack(beside2[high:], below2[HALF:]),
         ]
     return [stack(pieces[0][...], pieces[1][...])]
 
 
-def block_order():
+STEPS = ((0, 0), (1, 0), (-1, 0), (0, 1), (2, 0), (1, 1), (-1, 1), (2, 1))
+
+
+def features_of(block, width):
     me = lax.axis_index("dp")
     rings = lax.axis_size("dp") // 2
+    step_z, step_x = STEPS[block]
     z, x = me // 2, me % 2
-    steps = ((0, 0), (1, 0), (-1, 0), (0, 1), (2, 0), (1, 1), (-1, 1), (2, 1))
-    return jnp.stack([(z + dz + rings) % rings * 2 + (x + dx) % 2 for dz, dx in steps]).astype(
-        jnp.int32
-    )
+    other = (z + step_z + rings) % rings * 2 + (x + step_x) % 2
+    return pl.ds(pl.multiple_of(other * width, 128), width)
 
 
 def row_slot(shape):
@@ -201,16 +210,12 @@
     return jnp.concatenate([jnp.where(first, value, zero), jnp.where(first, zero, value)], axis=1)
 
 
-def features_of(order_ref, block, width):
-    return pl.ds(pl.multiple_of(order_ref[block] * width, 128), width)
-
-
-def load_columns(copies, order_ref, refs, buffers, blocks):
+def load_columns(copies, refs, buffers, blocks):
     width = buffers[0].shape[2]
     return [
         copies.start(
             [
-                (ref.at[:, features_of(order_ref, block, width), :], buffer.at[i])
+                (ref.at[:, features_of(block, width), :], buffer.at[i])
                 for ref, buffer in zip(refs, buffers)
             ]
         )
@@ -218,10 +223,10 @@
     ]
 
 
-def load_rows(copies, order_ref, ref, buffer, blocks):
+def load_rows(copies, ref, buffer, blocks):
     width = buffer.shape[2]
     return [
-        copies.start([(ref.at[:, features_of(order_ref, block, width)], buffer.at[i])])
+        copies.start([(ref.at[:, features_of(block, width)], buffer.at[i])])
         for i, block in enumerate(blocks)
     ]
 
@@ -246,24 +251,26 @@
 TN = ((0,), (0,))
 
 
-def gate_up(part, order, pieces, weights, before=None):
+def gate_up(part, pieces, weights, before=None, down_flat=None):
     blocks = ARRIVING[part]
     rows, width = 2 * HALF, pieces[0].shape[1]
     hid = weights[0].shape[2]
     last = part == len(ARRIVING) - 1
 
-    def kernel(order_ref, *refs):
+    def kernel(*refs):
         count = len(pieces)
         held_pieces, refs = refs[:count], refs[count:]
         if before is not None:
             before_ref, refs = refs[0], refs[1:]
-        columns, pre_ref, refs = refs[:2], refs[2], refs[3:]
+        columns, refs = refs[:2], refs[2:]
         if last:
-            hidden_ref, refs = refs[0], refs[1:]
-        gate_held, up_held, semaphores = refs
-        arriving = load_columns(
-            Copies(semaphores), order_ref, columns, (gate_held, up_held), blocks
-        )
+            down_ref, pre_ref, hidden_ref, *cuts, gate_held, up_held, down_held, semaphores = refs
+        else:
+            pre_ref, gate_held, up_held, semaphores = refs
+        copies = Copies(semaphores)
+        arriving = load_columns(copies, columns, (gate_held, up_held), blocks)
+        if last:
+            down_arriving = load_rows(copies, down_ref, down_held, blocks)
         first = row_slot((rows, hid))
         for i, value in enumerate(arrived_blocks(part, held_pieces)):
             wait(arriving[i])
@@ -279,44 +286,49 @@
             pre_ref[:, hid:] = up
         if last:
             gate = pre_ref[:, :hid]
-            hidden = (gate * jax.nn.sigmoid(gate) * pre_ref[:, hid:]).astype(BF)
-            hidden_ref[...] = pair(first, hidden)
+            hidden = pair(first, (gate * jax.nn.sigmoid(gate) * pre_ref[:, hid:]).astype(BF))
+            hidden_ref[...] = hidden
+            wait(down_arriving[0])
+            store_sum(0, 0, dot(hidden, down_held[0]).astype(BF), cuts)
 
     shapes = [jax.ShapeDtypeStruct((rows, 2 * hid), F32)]
+    scratch = column_buffers(blocks, width, hid)
     if last:
-        shapes.append(jax.ShapeDtypeStruct((rows, 2 * hid), BF))
+        shapes += [jax.ShapeDtypeStruct((rows, 2 * hid), BF)] + sum_shapes(0, rows, width)
+        scratch += row_buffers(blocks, width, hid)
+        weights = (*weights, down_flat)
     extra = [] if before is None else [before]
     out = pl.pallas_call(
         kernel,
-        in_specs=[SMEM] + [VMEM] * (len(pieces) + len(extra)) + [HBM] * 2,
+        in_specs=[VMEM] * (len(pieces) + len(extra)) + [HBM] * len(weights),
         out_shape=shapes,
-        scratch_shapes=column_buffers(blocks, width, hid) + semaphores_for(blocks, 2),
+        scratch_shapes=scratch + semaphores_for(blocks, 3),
         compiler_params=LARGE,
         name=f"gate_up_{part}",
-    )(order, *pieces, *extra, *weights)
+    )(*pieces, *extra, *weights)
     return out if last else out[0]
 
 
-def output_sums(part, order, hidden, down_flat, width):
+def output_sums(part, hidden, down_flat, width):
     blocks = LEAVING[part]
     rows, units = hidden.shape
 
-    def kernel(order_ref, hidden_ref, down_ref, *refs):
+    def kernel(hidden_ref, down_ref, *refs):
         outs = refs[:-2]
         down_held, semaphores = refs[-2:]
-        arriving = load_rows(Copies(semaphores), order_ref, down_ref, down_held, blocks)
+        arriving = load_rows(Copies(semaphores), down_ref, down_held, blocks)
         for i in range(len(blocks)):
             wait(arriving[i])
             store_sum(part, i, dot(hidden_ref[...], down_held[i]).astype(BF), outs)
 
     return pl.pallas_call(
         kernel,
-        in_specs=[SMEM, VMEM, HBM],
+        in_specs=[VMEM, HBM],
         out_shape=sum_shapes(part, rows, width),
         scratch_shapes=row_buffers(blocks, width, units // 2) + semaphores_for(blocks, 1),
         compiler_params=LARGE,
         name=f"output_sums_{part}",
-    )(order, hidden, down_flat)
+    )(hidden, down_flat)
 
 
 def sum_shapes(part, rows, width):
@@ -332,22 +344,29 @@
         outs[i][...] = value
 
 
-def cotangents(part, order, pieces, down_flat, before=None, pre=None):
+def cotangents(part, pieces, down_flat, before=None, pre=None, weights=()):
     blocks = ARRIVING[part]
     rows, width = 2 * HALF, pieces[0].shape[1]
     hid = down_flat.shape[0] // 2
     last = part == len(ARRIVING) - 1
 
-    def kernel(order_ref, *refs):
+    def kernel(*refs):
         count = len(pieces)
         held_pieces, refs = refs[:count], refs[count:]
         if before is not None:
             before_ref, refs = refs[0], refs[1:]
         if last:
             pre_ref, refs = refs[0], refs[1:]
-        down_ref, outs = refs[0], refs[1:-2]
-        down_held, semaphores = refs[-2:]
-        arriving = load_rows(Copies(semaphores), order_ref, down_ref, down_held, blocks)
+        down_ref, refs = refs[0], refs[1:]
+        if last:
+            columns, refs = refs[:2], refs[2:]
+            *outs, down_held, gate_held, up_held, semaphores = refs
+        else:
+            *outs, down_held, semaphores = refs
+        copies = Copies(semaphores)
+        arriving = load_rows(copies, down_ref, down_held, blocks)
+        if last:
+            columns_arriving = load_columns(copies, columns, (gate_held, up_held), blocks)
         first = row_slot((rows, hid))
         total = before_ref[...] if before is not None else None
         for i, value in enumerate(arrived_blocks(part, held_pieces)):
@@ -362,34 +381,40 @@
         sigmoid = jax.nn.sigmoid(gate)
         gate_diff = (total * up * sigmoid * (1.0 + gate * (1.0 - sigmoid))).astype(BF)
         up_diff = (total * (gate * sigmoid)).astype(BF)
-        outs[0][...] = pair(first, gate_diff)
-        outs[1][...] = pair(first, up_diff)
-
+        gate_diff, up_diff = pair(first, gate_diff), pair(first, up_diff)
+        outs[0][...] = gate_diff
+        outs[1][...] = up_diff
+        wait(columns_arriving[0])
+        value = dot(gate_diff, both(gate_held, 0), NT) + dot(up_diff, both(up_held, 0), NT)
+        store_sum(0, 0, value.astype(BF), outs[2:])
+
+    scratch = row_buffers(blocks, width, hid)
     if last:
-        shapes = [jax.ShapeDtypeStruct((rows, 2 * hid), BF)] * 2
+        shapes = [jax.ShapeDtypeStruct((rows, 2 * hid), BF)] * 2 + sum_shapes(0, rows, width)
+        scratch += column_buffers(blocks, width, hid)
     else:
         shapes = [jax.ShapeDtypeStruct((rows, hid), F32)]
     extra = [value for value in (before, pre) if value is not None]
     out = pl.pallas_call(
         kernel,
-        in_specs=[SMEM] + [VMEM] * (len(pieces) + len(extra)) + [HBM],
+        in_specs=[VMEM] * (len(pieces) + len(extra)) + [HBM] * (1 + len(weights)),
         out_shape=shapes,
-        scratch_shapes=row_buffers(blocks, width, hid) + semaphores_for(blocks, 1),
+        scratch_shapes=scratch + semaphores_for(blocks, 3),
         compiler_params=LARGE,
         name=f"cotangents_{part}",
-    )(order, *pieces, *extra, down_flat)
+    )(*pieces, *extra, down_flat, *weights)
     return out if last else out[0]
 
 
-def input_sums(part, order, diffs, weights, width):
+def input_sums(part, diffs, weights, width):
     blocks = LEAVING[part]
     rows, units = diffs[0].shape
 
-    def kernel(order_ref, gate_diff_ref, up_diff_ref, gate_ref, up_ref, *refs):
+    def kernel(gate_diff_ref, up_diff_ref, gate_ref, up_ref, *refs):
         outs = refs[:-3]
         gate_held, up_held, semaphores = refs[-3:]
         arriving = load_columns(
-            Copies(semaphores), order_ref, (gate_ref, up_ref), (gate_held, up_held), blocks
+            Copies(semaphores), (gate_ref, up_ref), (gate_held, up_held), blocks
         )
         for i in range(len(blocks)):
             wait(arriving[i])
@@ -399,12 +424,44 @@
 
     return pl.pallas_call(
         kernel,
-        in_specs=[SMEM, VMEM, VMEM, HBM, HBM],
+        in_specs=[VMEM, VMEM, HBM, HBM],
         out_shape=sum_shapes(part, rows, width),
         scratch_shapes=column_buffers(blocks, width, units // 2) + semaphores_for(blocks, 2),
         compiler_params=LARGE,
         name=f"input_sums_{part}",
-    )(order, *diffs, *weights)
+    )(*diffs, *weights)
+
+
+def middle_sums(diffs, hidden, weights, down_flat, width):
+    in_blocks, out_blocks = LEAVING[1:]
+    rows, units = hidden.shape
+
+    def kernel(gate_diff_ref, up_diff_ref, hidden_ref, gate_ref, up_ref, down_ref, *refs):
+        outs = refs[:-4]
+        gate_held, up_held, down_held, semaphores = refs[-4:]
+        copies = Copies(semaphores)
+        arriving = load_columns(copies, (gate_ref, up_ref), (gate_held, up_held), in_blocks)
+        down_arriving = load_rows(copies, down_ref, down_held, out_blocks)
+        for i in range(len(in_blocks)):
+            wait(arriving[i])
+            value = dot(gate_diff_ref[...], both(gate_held, i), NT)
+            value += dot(up_diff_ref[...], both(up_held, i), NT)
+            outs[i][...] = value.astype(BF)
+        for i in range(len(out_blocks)):
+            wait(down_arriving[i])
+            outs[len(in_blocks) + i][...] = dot(hidden_ref[...], down_held[i]).astype(BF)
+
+    out = pl.pallas_call(
+        kernel,
+        in_specs=[VMEM] * 3 + [HBM] * 3,
+        out_shape=sum_shapes(1, rows, width) + sum_shapes(2, rows, width),
+        scratch_shapes=column_buffers(in_blocks, width, units // 2)
+        + row_buffers(out_blocks, width, units // 2)
+        + semaphores_for(range(10), 1),
+        compiler_params=LARGE,
+        name="middle_sums",
+    )(*diffs, hidden, *weights, down_flat)
+    return out[: len(in_blocks)], out[len(in_blocks) :]
 
 
 def all_blocks(pieces):
@@ -415,7 +472,7 @@
         at += count
 
 
-def column_grads_kernel(order_ref, *refs):
+def column_grads_kernel(*refs):
     pieces = refs[:9]
     diffs, outs, held, semaphores = refs[9:11], refs[11:13], refs[13:15], refs[15]
     width, hid = held[0].shape[2:]
@@ -426,27 +483,27 @@
             grad = dot(value, diff_ref[...], TN).astype(BF)
             held_ref[block, 0] = grad[:, :hid]
             held_ref[block, 1] = grad[:, hid:]
-            target = out_ref.at[:, features_of(order_ref, block, width), :]
+            target = out_ref.at[:, features_of(block, width), :]
             leaving += copies.start([(held_ref.at[block], target)])
     wait(leaving)
 
 
-def column_grads(order, pieces, diffs):
+def column_grads(pieces, diffs):
     width = pieces[0].shape[1]
     hid = diffs[0].shape[1] // 2
     blocks = range(8)
     return pl.pallas_call(
         column_grads_kernel,
-        in_specs=[SMEM] + [VMEM] * 11,
+        in_specs=[VMEM] * 11,
         out_specs=[HBM] * 2,
         out_shape=[jax.ShapeDtypeStruct((2, 8 * width, hid), BF)] * 2,
         scratch_shapes=column_buffers(blocks, width, hid) + semaphores_for(blocks, 2),
         compiler_params=LARGE,
         name="column_grads",
-    )(order, *pieces, *diffs)
-
-
-def row_grads_kernel(order_ref, *refs):
+    )(*pieces, *diffs)
+
+
+def row_grads_kernel(*refs):
     pieces = refs[:9]
     hidden_ref, down_out, held, semaphores = refs[9:]
     width = held.shape[2]
@@ -454,66 +511,74 @@
     leaving = []
     for block, value in all_blocks(pieces):
         held[block] = dot(hidden_ref[...], value, TN).astype(BF)
-        target = down_out.at[:, features_of(order_ref, block, width)]
+        target = down_out.at[:, features_of(block, width)]
         leaving += copies.start([(held.at[block], target)])
     wait(leaving)
 
 
-def row_grads(order, pieces, hidden):
+def row_grads(pieces, hidden):
     width = pieces[0].shape[1]
     units = hidden.shape[1]
     blocks = range(8)
     return pl.pallas_call(
         row_grads_kernel,
-        in_specs=[SMEM] + [VMEM] * 10,
+        in_specs=[VMEM] * 10,
         out_specs=HBM,
         out_shape=jax.ShapeDtypeStruct((units, 8 * width), BF),
         scratch_shapes=row_buffers(blocks, width, units // 2) + semaphores_for(blocks, 1),
         compiler_params=LARGE,
         name="row_grads",
-    )(order, *pieces, hidden)
+    )(*pieces, hidden)
 
 
 def wide(value):
     return value.astype(F32)
 
 
-def second_hop_kernel(far, above1, below1, got_up, got_down, to_up, to_down, to_side):
+def second_hop(low, far, above1, below1, got_up, got_down, to_up, to_down, to_side):
+    high, cut = 2 * HALF - low, HALF - low
     to_up[:HALF] = far[:HALF]
-    to_up[HALF:] = (wide(above1[:LOW]) + wide(got_up[:LOW])).astype(BF)
+    to_up[HALF:] = (wide(above1[:low]) + wide(got_up[:low])).astype(BF)
     to_down[:HALF] = far[HALF:]
-    to_down[HALF:] = (wide(below1[HIGH:]) + wide(got_down[HIGH - HALF :])).astype(BF)
-    cut = HALF - LOW
-    to_side[:cut] = (wide(above1[LOW:HALF]) + wide(got_up[LOW:])).astype(BF)
-    to_side[cut:HIGH] = above1[HALF:]
-    to_side[HIGH : HIGH + HALF] = below1[:HALF]
-    to_side[HIGH + HALF :] = (wide(below1[HALF:HIGH]) + wide(got_down[: HIGH - HALF])).astype(BF)
-
-
-def third_hop_kernel(above, below, beside, got_up, got_down, got_side, to_up, to_down, to_side):
-    cut = HALF - LOW
-    to_up[:LOW] = (wide(above[:LOW]) + wide(got_up[:LOW])).astype(BF)
-    to_up[LOW:HALF] = (
-        wide(above[LOW:HALF]) + wide(got_up[LOW:HALF]) + wide(got_side[:cut])
+    to_down[HALF:] = (wide(below1[high:]) + wide(got_down[cut:])).astype(BF)
+    to_side[:cut] = (wide(above1[low:HALF]) + wide(got_up[low:])).astype(BF)
+    to_side[cut:high] = above1[HALF:]
+    to_side[high : high + HALF] = below1[:HALF]
+    to_side[high + HALF :] = (wide(below1[HALF:high]) + wide(got_down[:cut])).astype(BF)
+
+
+def third_hop(low, above, below, beside, got_up, got_down, got_side, to_up, to_down, to_side):
+    high, cut = 2 * HALF - low, HALF - low
+    to_up[:low] = (wide(above[:low]) + wide(got_up[:low])).astype(BF)
+    to_up[low:HALF] = (
+        wide(above[low:HALF]) + wide(got_up[low:HALF]) + wide(got_side[:cut])
     ).astype(BF)
-    to_up[HALF:] = (wide(above[HALF:]) + wide(got_side[cut:HIGH])).astype(BF)
-    to_down[:HALF] = (wide(below[:HALF]) + wide(got_side[HIGH : HIGH + HALF])).astype(BF)
-    to_down[HALF:HIGH] = (
-        wide(below[HALF:HIGH]) + wide(got_side[HIGH + HALF :]) + wide(got_down[:cut])
+    to_up[HALF:] = (wide(above[HALF:]) + wide(got_side[cut:high])).astype(BF)
+    to_down[:HALF] = (wide(below[:HALF]) + wide(got_side[high : high + HALF])).astype(BF)
+    to_down[HALF:high] = (
+        wide(below[HALF:high]) + wide(got_side[high + HALF :]) + wide(got_down[:cut])
     ).astype(BF)
-    to_down[HIGH:] = (wide(below[HIGH:]) + wide(got_down[cut:HALF])).astype(BF)
-    to_side[:LOW] = (wide(beside[:LOW]) + wide(got_up[HALF:])).astype(BF)
-    to_side[LOW:HIGH] = beside[LOW:HIGH]
-    to_side[HIGH:] = (wide(beside[HIGH:]) + wide(got_down[HALF:])).astype(BF)
+    to_down[high:] = (wide(below[high:]) + wide(got_down[cut:HALF])).astype(BF)
+    to_side[:low] = (wide(beside[:low]) + wide(got_up[HALF:])).astype(BF)
+    to_side[low:high] = beside[low:high]
+    to_side[high:] = (wide(beside[high:]) + wide(got_down[HALF:])).astype(BF)
+
+
+def out_second_kernel(*refs):
+    second_hop(OUT_LOW, *refs)
 
 
 def both_hops_kernel(*refs):
-    whole = 2 * HALF
+    size = 2 * HALF
     outs = refs[11:]
-    third_hop_kernel(*refs[:6], *[ref.at[pl.ds(0, whole)] for ref in outs])
-    second_hop_kernel(
-        *refs[6:11], *[ref.at[pl.ds(whole, ref.shape[0] - whole)] for ref in outs]
-    )
+    third_hop(OUT_LOW, *refs[:6], *[ref.at[pl.ds(0, size)] for ref in outs])
+    second_hop(IN_LOW, *refs[6:11], *[ref.at[pl.ds(size, ref.shape[0] - size)] for ref in outs])
+
+
+def in_third_kernel(above, below, beside, got_up, got_down, got_side, *outs):
+    size = 2 * HALF
+    got = [ref.at[pl.ds(size, ref.shape[0] - size)] for ref in (got_up, got_down, got_side)]
+    third_hop(IN_LOW, above, below, beside, *got, *outs)
 
 
 def last_kernel(own, from_below, from_above, from_side, total):
@@ -541,33 +606,35 @@
         return (self.links.send_up(sums[0]), self.links.send_down(sums[1]))
 
     def second(self, *args):
-        sizes = (HALF + LOW, HALF + LOW, 2 * HIGH)
-        outgoing = local_call(second_hop_kernel, "second_hop", sizes, *args)
+        outgoing = local_call(out_second_kernel, "second_hop", hop_sizes(OUT_LOW), *args)
         return outgoing, self.send(*outgoing)
 
     def both(self, *args):
-        sizes = (3 * HALF + LOW, 3 * HALF + LOW, 2 * HALF + 2 * HIGH)
+        sizes = tuple(2 * HALF + size for size in hop_sizes(IN_LOW))
         outgoing = local_call(both_hops_kernel, "both_hops", sizes, *args)
         return outgoing, self.send(*outgoing)
 
     def last(self, *args):
-        outgoing = local_call(final_hop_kernel, "third_hop", (2 * HALF,) * 3, *args)
+        outgoing = local_call(in_third_kernel, "third_hop", (2 * HALF,) * 3, *args)
         return outgoing, self.send(*outgoing)
 
     def total(self, own, got):
         return local_call(last_kernel, "last_hop", (2 * HALF,), own, *got)[0]
 
 
-def combine_kernel(pick_ref, gated_ref, out_ref, in_ref, mixed_ref, grads_ref):
-    mixed_ref[...] = dot(gated_ref[...], wide(out_ref[...]), TN, lax.Precision.HIGHEST).astype(BF)
-    grads_ref[...] = dot(pick_ref[...], in_ref[...], TN).astype(BF)
-
-
-def combine(pick, gated, out_rows, in_rows):
-    shape = jax.ShapeDtypeStruct((pick.shape[1], out_rows.shape[1]), BF)
+def combine_kernel(pick_ref, gated_ref, rows_ref, mixed_ref, grads_ref):
+    width = mixed_ref.shape[1]
+    mixed_ref[...] = dot(
+        gated_ref[...], wide(rows_ref[:, :width]), TN, lax.Precision.HIGHEST
+    ).astype(BF)
+    grads_ref[...] = dot(pick_ref[...], rows_ref[:, width:], TN).astype(BF)
+
+
+def combine(pick, gated, rows):
+    shape = jax.ShapeDtypeStruct((pick.shape[1], rows.shape[1] // 2), BF)
     return pl.pallas_call(
         combine_kernel, out_shape=[shape] * 2, compiler_params=SMALL, name="combine"
-    )(pick, gated, out_rows, in_rows)
+    )(pick, gated, rows)
 
 
 def on_device(tokens, upstream, expert_ids, gate_values, gate_weight, up_weight, down_weight):
@@ -576,7 +643,6 @@
     rows = columns * exp_dev * 8
     width = tokens.shape[1]
     links = Links(lax.axis_size("dp"))
-    order = block_order()
     columns_in = (in_hbm(gate_weight), in_hbm(up_weight))
     rows_in = in_hbm(down_weight.reshape(exp_dev * hid, features))
 
@@ -590,33 +656,35 @@
     x = Gather(links, arrived[:, :width])
     c = Gather(links, arrived[:, width:])
     x_sent = x.relay()
-    pre = gate_up(0, order, after(x.arrived[0], *x_sent), columns_in)
+    pre = gate_up(0, after(x.arrived[0], *x_sent), columns_in)
     c_sent = c.relay(pre)
-    total = cotangents(0, order, after(c.arrived[0], *c_sent), rows_in)
+    total = cotangents(0, after(c.arrived[0], *c_sent), rows_in)
     x_sent = x.ends(total)
-    pre = gate_up(1, order, after(x.arrived[1], *x_sent), columns_in, pre)
+    pre = gate_up(1, after(x.arrived[1], *x_sent), columns_in, pre)
     c_sent = c.ends(pre)
-    total = cotangents(1, order, after(c.arrived[1], *c_sent), rows_in, total)
-    pre, hidden = gate_up(2, order, after(x.arrived[2], total), columns_in, pre)
+    total = cotangents(1, after(c.arrived[1], *c_sent), rows_in, total)
+    pre, hidden, *out_cuts = gate_up(
+        2, after(x.arrived[2], total), columns_in, pre, rows_in
+    )
 
     hops = Sums(links)
-    out_cuts = output_sums(0, order, hidden, rows_in, width)
     out_got = hops.first(out_cuts)
-    out_far = output_sums(1, order, after(hidden, *out_cuts, *c.arrived[2]), rows_in, width)
-    diffs = cotangents(2, order, after(c.arrived[2], *out_far), rows_in, total, pre)
-    sent, out_got = hops.second(*out_far, *after(out_got, *diffs))
-    in_cuts = input_sums(0, order, after(diffs, *sent), columns_in, width)
-    in_got = hops.first(in_cuts)
-    in_far = input_sums(1, order, after(diffs, *in_cuts), columns_in, width)
-    out_near = output_sums(2, order, after(hidden, *in_far), rows_in, width)
+    out_far = output_sums(1, after(hidden, *out_cuts, *c.arrived[2]), rows_in, width)
+    *diffs, cut_up, cut_down = cotangents(
+        2, after(c.arrived[2], *out_far), rows_in, total, pre, columns_in
+    )
+    in_got = hops.first((cut_up, cut_down))
+    sent, out_got = hops.second(*out_far, *after(out_got, cut_up))
+    in_far, out_near = middle_sums(after(diffs, *sent), hidden, columns_in, rows_in, width)
     sent, got = hops.both(*out_near[:3], *out_got, *in_far, *in_got)
-    in_near = input_sums(2, order, after(diffs, *sent), columns_in, width)
-    down_grad = row_grads(order, after(sum(c.arrived, ()), *in_near), hidden)
-    gate_grad, up_grad = column_grads(order, after(sum(x.arrived, ()), down_grad), diffs)
+    in_near = input_sums(2, after(diffs, *sent), columns_in, width)
+    down_grad = row_grads(after(sum(c.arrived, ()), *in_near), hidden)
+    gate_grad, up_grad = column_grads(after(sum(x.arrived, ()), down_grad), diffs)
     sent, in_got = hops.last(*in_near[:3], *after(got, gate_grad))
-    out_back = exchange(hops.total(out_near[3], after(got, *sent)))
-    in_back = exchange(hops.total(in_near[3], after(in_got, out_back)))
-    mixed, token_grads = combine(pick, gated, out_back, in_back)
+    out_total = hops.total(out_near[3], after(got, *sent))
+    in_total = hops.total(in_near[3], after(in_got, out_total))
+    returned = exchange(jnp.concatenate([out_total, in_total], axis=1))
+    mixed, token_grads = combine(pick, gated, returned)
     return (mixed, token_grads, gate_grad, up_grad, down_grad.reshape(down_weight.shape))
 
 

time: 170 us -> 160 us (0.941)
  waiting for transfers between devices: 10.2 us -> 36.1 us
  blocking collectives: 67.4 us -> 52.3 us
  Pallas kernels: 48 us -> 33.9 us
  starting transfers between devices: 40 us -> 36 us
  local copies, waits for them, and re-layouts: 2.22 us -> 0.07 us
    all_to_all x3 -> x2, blocking collectives: 67.4 us -> 52.3 us  [exchange(): lax.all_to_all(value.reshape(columns, exp_dev * 8, -1), 'expert', 0, 0, t...]
    pallas_call x14 -> x11, Pallas kernels: 40.6 us -> 28.9 us  [the longest x3 7.33 us: gate_up(): pl.pallas_call(kernel, in_specs=[VMEM] * (len(pieces) + len(extra)) + [HB...]
    ppermute x7, waiting for transfers between devices: 9.23 us -> 19.7 us  [cross(): return lax.ppermute(value, 'dp', self.side)]
    ppermute x11, waiting for transfers between devices: 0.86 us -> 11.3 us  [send_up(): return lax.ppermute(value, 'dp', self.up)]
    ppermute x11, waiting for transfers between devices: 0.08 us -> 5.07 us  [send_down(): return lax.ppermute(value, 'dp', self.down)]
    ppermute x7, starting transfers between devices: 6.67 us -> 4.18 us  [cross(): return lax.ppermute(value, 'dp', self.side)]
    pallas_call x9, Pallas kernels: 4.07 us -> 1.66 us  [local_call(): pl.pallas_call(kernel, out_shape=shapes, compiler_params=SMALL, name=name)]
    unnamed x12 -> x0, local copies, waits for them, and re-layouts: 2.06 us -> none
  transfers between devices with their start and end apart: 29 -> 29, of which waited for: 5 -> 14; matrix products, arithmetic and copies ran while one was open for 0% -> 0% of each run, Pallas kernels for 26% -> 18%
where the time goes in v3:
time: 160 us; the launch traced here: 159 us
  blocking collectives  52.3 us (33%)
  waiting for transfers between devices  36.1 us (23%)
  starting transfers between devices  36 us (22%)
  Pallas kernels  33.9 us (21%)
    all_to_all x2, blocking collectives, exchange(): lax.all_to_all(value.reshape(columns, exp_dev * 8, -1), 'expert', 0, 0, t...  52.3 us
    ppermute x11, starting transfers between devices, send_down(): return lax.ppermute(value, 'dp', self.down)  25.6 us
    ppermute x7, waiting for transfers between devices, cross(): return lax.ppermute(value, 'dp', self.side)  19.7 us
    ppermute x11, waiting for transfers between devices, send_up(): return lax.ppermute(value, 'dp', self.up)  11.3 us
    pallas_call x3, Pallas kernels, gate_up(): pl.pallas_call(kernel, in_specs=[VMEM] * (len(pieces) + len(extra)) + [HB...  7.33 us
    pallas_call x3, Pallas kernels, cotangents(): pl.pallas_call(kernel, in_specs=[VMEM] * (len(pieces) + len(extra)) + [HB...  6.88 us
    ppermute x11, starting transfers between devices, send_up(): return lax.ppermute(value, 'dp', self.up)  6.18 us
    ppermute x11, waiting for transfers between devices, send_down(): return lax.ppermute(value, 'dp', self.down)  5.07 us
  transfers between devices with their start and end apart: 29, of which 14 were waited for; matrix products, arithmetic and copies ran while one was open for 0% of the time, Pallas kernels for 18%

profile of v3, /device:TPU:1, one launch (start us, length us, event | category | flops | bytes accessed | tf_op | source)
XLA Modules:
  0.0 159.4 jit_solution(14882797710727451145)
XLA Ops:
  2.7 23.8 %all_to_all.10 = bf16[16,16,1792]{2,1,0:T(8,128)(2,1)S(1)} all-to-all(bf16[16,16,1792]{2,1,0:T(8,128)(2,1)S(1)} %bitcast.17), channel_id=1, replica_groups=mesh['dp'=8,'expert'=16] {'expert'}, dimensions={0} | all-to-all | bytes 1835008 | tf_op jit(solution)/shard_map/all_to_all | solution.py:650
  31.8 5.6 %collective-permute-done.5.beside.refs_3_ = bf16[256,896]{1,0:T(8,128)(2,1)S(1)} collective-permute-done((bf16[256,896]{1,0:T(8,128)(2,1)S(1)}, bf16[256,896]{1,0:T(8,128)(2,1)S(1)}, u32[]{:S(2)}, u32[]{:S(2)}) %collective-permute-start.5) | collective-permute-done | bytes 458784 | tf_op jit(solution)/shard_map/ppermute | solution.py:116
  37.5 3.8 %collective-permute-start = (bf16[256,896]{1,0:T(8,128)(2,1)S(1)}, bf16[256,896]{1,0:T(8,128)(2,1)S(1)}, u32[]{:S(2)}, u32[]{:S(2)}) collective-permute-start(bf16[256,896]{1,0:T(8,128)(2,1)S(1)} %get-tuple-element.197.refs_0_), channel_id=1, source_target_pairs={{0,96},{16,112},{32,0},{48,16},{64,32},{80,48},{96,64},{112,80},{1... | collective-permute-start | bytes 1376264 | tf_op jit(solution)/shard_map/ppermute | solution.py:113
  43.8 3.5 %collective-permute-done.2.beside.refs_3_ = bf16[256,896]{1,0:T(8,128)(2,1)S(1)} collective-permute-done((bf16[256,896]{1,0:T(8,128)(2,1)S(1)}, bf16[256,896]{1,0:T(8,128)(2,1)S(1)}, u32[]{:S(2)}, u32[]{:S(2)}) %collective-permute-start.2) | collective-permute-done | bytes 458784 | tf_op jit(solution)/shard_map/ppermute | solution.py:116
  48.9 2.9 %gate_up_0.1.refs_3_ = f32[256,256]{1,0:T(8,128)S(1)} custom-call(bf16[256,896]{1,0:T(8,128)(2,1)S(1)} %get-tuple-element.206.refs_0_, bf16[256,896]{1,0:T(8,128)(2,1)S(1)} %collective-permute-done.3.above.refs_1_, bf16[256,896]{1,0:T(8,128)(2,1)S(1)} %collective-permute-done.4.below.refs_2_, bf16[256,896]{1,0:T(8,128)(2,1)S(1)} %collective-permute-done.5.beside.refs_3_, ...), custom_call_target="tpu_custom_call" | custom-call | tf_op jit(solution)/shard_map/gate_up_0/pallas_call | solution.py:301
  54.5 2.7 %collective-permute-done.9.above2.refs_0_.refs_4_ = bf16[240,896]{1,0:T(8,128)(2,1)S(1)} collective-permute-done((bf16[240,896]{1,0:T(8,128)(2,1)S(1)}, bf16[240,896]{1,0:T(8,128)(2,1)S(1)}, u32[]{:S(2)}, u32[]{:S(2)}) %collective-permute-start.9) | collective-permute-done | bytes 430112 | tf_op jit(solution)/shard_map/ppermute | solution.py:113
  58.4 2.7 %cotangents_0.1.refs_3_ = f32[256,128]{1,0:T(8,128)S(1)} custom-call(bf16[256,896]{1,0:T(8,128)(2,1)S(1)} %get-tuple-element.197.refs_0_, bf16[256,896]{1,0:T(8,128)(2,1)S(1)} %collective-permute-done.above.refs_1_, bf16[256,896]{1,0:T(8,128)(2,1)S(1)} %collective-permute-done.1.below.refs_2_, bf16[256,896]{1,0:T(8,128)(2,1)S(1)} %collective-permute-done.2.beside.refs_3_, ...), custom_call_target="tpu_custom_call" | custom-call | tf_op jit(solution)/shard_map/cotangents_0/pallas_call | solution.py:398
  62.8 2.5 %gate_up_1.1.refs_2_ = f32[256,256]{1,0:T(8,128)S(1)} custom-call(bf16[240,896]{1,0:T(8,128)(2,1)S(1)} %collective-permute-done.9.above2.refs_0_.refs_4_, bf16[240,896]{1,0:T(8,128)(2,1)S(1)} %collective-permute-done.10.below2.refs_1_.refs_5_, bf16[288,896]{1,0:T(8,128)(2,1)S(1)} %collective-permute-done.11.beside2.refs_2_.refs_6_, ...), custom_call_target="tpu_custom_call" | custom-call | tf_op jit(solution)/shard_map/gate_up_1/pallas_call | solution.py:301
  66.4 3.0 %collective-permute-done.8.beside2.refs_2_.refs_6_ = bf16[288,896]{1,0:T(8,128)(2,1)S(1)} collective-permute-done((bf16[288,896]{1,0:T(8,128)(2,1)S(1)}, bf16[288,896]{1,0:T(8,128)(2,1)S(1)}, u32[]{:S(2)}, u32[]{:S(2)}) %collective-permute-start.8) | collective-permute-done | bytes 516128 | tf_op jit(solution)/shard_map/ppermute | solution.py:116
  69.4 3.8 %collective-permute-start.12 = (bf16[128,896]{1,0:T(8,128)(2,1)S(1)}, bf16[128,896]{1,0:T(8,128)(2,1)S(1)}, u32[]{:S(2)}, u32[]{:S(2)}) collective-permute-start(bf16[128,896]{1,0:T(8,128)(2,1)S(1)} %get-tuple-element.153), channel_id=1, source_target_pairs={{0,96},{16,112},{32,0},{48,16},{64,32},{80,48},{96,64},{112,80},{1... | collective-permute-start | bytes 688136 | tf_op jit(solution)/shard_map/ppermute | solution.py:113
  73.3 2.2 %cotangents_1.1.refs_2_ = f32[256,128]{1,0:T(8,128)S(1)} custom-call(bf16[240,896]{1,0:T(8,128)(2,1)S(1)} %collective-permute-done.6.above2.refs_0_.refs_4_, bf16[240,896]{1,0:T(8,128)(2,1)S(1)} %collective-permute-done.7.below2.refs_1_.refs_5_, bf16[288,896]{1,0:T(8,128)(2,1)S(1)} %collective-permute-done.8.beside2.refs_2_.refs_6_, ...), custom_call_target="tpu_custom_call" | custom-call | tf_op jit(solution)/shard_map/cotangents_1/pallas_call | solution.py:398
  77.6 2.9 %collective-permute-start.17 = (bf16[128,896]{1,0:T(8,128)(2,1)S(1)}, bf16[128,896]{1,0:T(8,128)(2,1)S(1)}, u32[]{:S(2)}, u32[]{:S(2)}) collective-permute-start(bf16[128,896]{1,0:T(8,128)(2,1)S(1)} %get-tuple-element.162), channel_id=1, source_target_pairs={{0,96},{16,112},{32,0},{48,16},{64,32},{80,48},{96,64},{112,80},{1... | collective-permute-start | bytes 688136 | tf_op jit(solution)/shard_map/ppermute | solution.py:113
  86.2 2.7 %collective-permute-start.19 = (bf16[192,896]{1,0:T(8,128)(2,1)S(1)}, bf16[192,896]{1,0:T(8,128)(2,1)S(1)}, u32[]{:S(2)}, u32[]{:S(2)}) collective-permute-start(bf16[192,896]{1,0:T(8,128)(2,1)S(1)} %get-tuple-element.176), channel_id=1, source_target_pairs={{0,96},{16,112},{32,0},{48,16},{64,32},{80,48},{96,64},{112,80},{1... | collective-permute-start | bytes 1032200 | tf_op jit(solution)/shard_map/ppermute | solution.py:113
  90.4 3.9 %middle_sums.1 = (bf16[256,896]{1,0:T(8,128)(2,1)S(1)}, bf16[256,896]{1,0:T(8,128)(2,1)S(1)}, bf16[256,896]{1,0:T(8,128)(2,1)S(1)}, bf16[256,896]{1,0:T(8,128)(2...) custom-call(bf16[256,256]{1,0:T(8,128)(2,1)S(1)} %get-tuple-element.191.gate_diff_, ...), custom_call_target="tpu_custom_call" | custom-call | tf_op jit(solution)/shard_map/middle_sums/pallas_call | solution.py:454
  98.6 2.7 %collective-permute-start.24 = (bf16[496,896]{1,0:T(8,128)(2,1)S(1)}, bf16[496,896]{1,0:T(8,128)(2,1)S(1)}, u32[]{:S(2)}, u32[]{:S(2)}) collective-permute-start(bf16[496,896]{1,0:T(8,128)(2,1)S(1)} %get-tuple-element.189), channel_id=1, source_target_pairs={{0,96},{16,112},{32,0},{48,16},{64,32},{80,48},{96,64},{112,80},{1... | collective-permute-start | bytes 2666504 | tf_op jit(solution)/shard_map/ppermute | solution.py:113
  101.3 3.1 %input_sums_2.1 = (bf16[256,896]{1,0:T(8,128)(2,1)S(1)}, bf16[256,896]{1,0:T(8,128)(2,1)S(1)}, bf16[256,896]{1,0:T(8,128)(2,1)S(1)}, bf16[256,896]{1,0:T(8,128)(2,1)S(1)}) custom-call(bf16[256,256]{1,0:T(8,128)(2,1)S(1)} %get-tuple-element.191.gate_diff_ref.refs_9_, bf16[256,256]{1,0:T(8,128)(2,1)S(1)} %get-tuple-element.192.up_diff_ref.refs_10_, ...), custom_call_target="tpu_custom_call" | custom-call | tf_op jit(solution)/shard_map/input_sums_2/pallas_call | solution.py:425
  104.4 2.2 %row_grads.1 = bf16[256,7168]{1,0:T(8,128)(2,1)} custom-call(bf16[256,896]{1,0:T(8,128)(2,1)S(1)} %get-tuple-element.197.refs_0_, bf16[256,896]{1,0:T(8,128)(2,1)S(1)} %collective-permute-done.above.refs_1_, bf16[256,896]{1,0:T(8,128)(2,1)S(1)} %collective-permute-done.1.below.refs_2_, bf16[256,896]{1,0:T(8,128)(2,1)S(1)} %collective-permute-done.2.beside.refs_3_, ...), custom_call_target="tpu_custom_call" | custom-call | tf_op jit(solution)/shard_map/row_grads/pallas_call | solution.py:523
  106.7 3.5 %column_grads.1 = (bf16[2,7168,128]{2,1,0:T(8,128)(2,1)}, bf16[2,7168,128]{2,1,0:T(8,128)(2,1)}) custom-call(bf16[256,896]{1,0:T(8,128)(2,1)S(1)} %get-tuple-element.206.refs_0_, bf16[256,896]{1,0:T(8,128)(2,1)S(1)} %collective-permute-done.3.above.refs_1_, bf16[256,896]{1,0:T(8,128)(2,1)S(1)} %collective-permute-done.4.below.refs_2_, ...), custom_call_target="tpu_custom_call" | custom-call | tf_op jit(solution)/shard_map/column_grads/pallas_call | solution.py:495
  110.2 3.6 %collective-permute-done.23.got_up.from_below = bf16[496,896]{1,0:T(8,128)(2,1)S(1)} collective-permute-done((bf16[496,896]{1,0:T(8,128)(2,1)S(1)}, bf16[496,896]{1,0:T(8,128)(2,1)S(1)}, u32[]{:S(2)}, u32[]{:S(2)}) %collective-permute-start.23) | collective-permute-done | bytes 888864 | tf_op jit(solution)/shard_map/ppermute | solution.py:110
  113.8 4.0 %collective-permute-done.25.got_side.from_side = bf16[544,896]{1,0:T(8,128)(2,1)S(1)} collective-permute-done((bf16[544,896]{1,0:T(8,128)(2,1)S(1)}, bf16[544,896]{1,0:T(8,128)(2,1)S(1)}, u32[]{:S(2)}, u32[]{:S(2)}) %collective-permute-start.25) | collective-permute-done | bytes 974880 | tf_op jit(solution)/shard_map/ppermute | solution.py:116
  118.3 2.7 %collective-permute-start.27 = (bf16[256,896]{1,0:T(8,128)(2,1)S(1)}, bf16[256,896]{1,0:T(8,128)(2,1)S(1)}, u32[]{:S(2)}, u32[]{:S(2)}) collective-permute-start(bf16[256,896]{1,0:T(8,128)(2,1)S(1)} %get-tuple-element.220), channel_id=1, source_target_pairs={{0,96},{16,112},{32,0},{48,16},{64,32},{80,48},{96,64},{112,80},{1... | collective-permute-start | bytes 1376264 | tf_op jit(solution)/shard_map/ppermute | solution.py:113
  121.5 5.4 %collective-permute-done.26.from_below = bf16[256,896]{1,0:T(8,128)(2,1)S(1)} collective-permute-done((bf16[256,896]{1,0:T(8,128)(2,1)S(1)}, bf16[256,896]{1,0:T(8,128)(2,1)S(1)}, u32[]{:S(2)}, u32[]{:S(2)}) %collective-permute-start.26) | collective-permute-done | bytes 458784 | tf_op jit(solution)/shard_map/ppermute | solution.py:110
  126.9 2.3 %collective-permute-done.28.from_side = bf16[256,896]{1,0:T(8,128)(2,1)S(1)} collective-permute-done((bf16[256,896]{1,0:T(8,128)(2,1)S(1)}, bf16[256,896]{1,0:T(8,128)(2,1)S(1)}, u32[]{:S(2)}, u32[]{:S(2)}) %collective-permute-start.28) | collective-permute-done | bytes 458784 | tf_op jit(solution)/shard_map/ppermute | solution.py:116
  129.5 28.6 %all_to_all.11 = bf16[16,16,1792]{2,1,0:T(8,128)(2,1)S(1)} all-to-all(bf16[16,16,1792]{2,1,0:T(8,128)(2,1)S(1)} %bitcast.18), channel_id=1, replica_groups=mesh['dp'=8,'expert'=16] {'expert'}, dimensions={0} | all-to-all | bytes 1835008 | tf_op jit(solution)/shard_map/all_to_all | solution.py:650
  (61 shorter events, 34.4 us)
Async XLA Ops:
  26.5 10.9 %collective-permute-start.5 = (bf16[256,896]{1,0:T(8,128)(2,1)S(1)}, bf16[256,896]{1,0:T(8,128)(2,1)S(1)}, u32[]{:S(2)}, u32[]{:S(2)}) collective-permute-start(bf16[256,896]{1,0:T(8,128)(2,1)S(1)} %get-tuple-element.206.refs_0_), channel_id=1, source_target_pairs={{0,16},{16,0},{32,48},{48,32},{64,80},{80,64},{96,112},{112,96},{1... | collective-permute-start | bytes 1376264 | tf_op jit(solution)/shard_map/ppermute | solution.py:116
  26.9 14.3 %collective-permute-start.4 = (bf16[256,896]{1,0:T(8,128)(2,1)S(1)}, bf16[256,896]{1,0:T(8,128)(2,1)S(1)}, u32[]{:S(2)}, u32[]{:S(2)}) collective-permute-start(bf16[256,896]{1,0:T(8,128)(2,1)S(1)} %get-tuple-element.206.refs_0_), channel_id=1, source_target_pairs={{0,32},{16,48},{32,64},{48,80},{64,96},{80,112},{96,0},{112,16},{1... | collective-permute-start | bytes 1376264 | tf_op jit(solution)/shard_map/ppermute | solution.py:110
  28.6 12.6 %collective-permute-start.3 = (bf16[256,896]{1,0:T(8,128)(2,1)S(1)}, bf16[256,896]{1,0:T(8,128)(2,1)S(1)}, u32[]{:S(2)}, u32[]{:S(2)}) collective-permute-start(bf16[256,896]{1,0:T(8,128)(2,1)S(1)} %get-tuple-element.206.refs_0_), channel_id=1, source_target_pairs={{0,96},{16,112},{32,0},{48,16},{64,32},{80,48},{96,64},{112,80},{1... | collective-permute-start | bytes 1376264 | tf_op jit(solution)/shard_map/ppermute | solution.py:113
  30.7 16.6 %collective-permute-start.2 = (bf16[256,896]{1,0:T(8,128)(2,1)S(1)}, bf16[256,896]{1,0:T(8,128)(2,1)S(1)}, u32[]{:S(2)}, u32[]{:S(2)}) collective-permute-start(bf16[256,896]{1,0:T(8,128)(2,1)S(1)} %get-tuple-element.197.refs_0_), channel_id=1, source_target_pairs={{0,16},{16,0},{32,48},{48,32},{64,80},{80,64},{96,112},{112,96},{1... | collective-permute-start | bytes 1376264 | tf_op jit(solution)/shard_map/ppermute | solution.py:116
  31.8 20.0 %collective-permute-start.1 = (bf16[256,896]{1,0:T(8,128)(2,1)S(1)}, bf16[256,896]{1,0:T(8,128)(2,1)S(1)}, u32[]{:S(2)}, u32[]{:S(2)}) collective-permute-start(bf16[256,896]{1,0:T(8,128)(2,1)S(1)} %get-tuple-element.197.refs_0_), channel_id=1, source_target_pairs={{0,32},{16,48},{32,64},{48,80},{64,96},{80,112},{96,0},{112,16},{1... | collective-permute-start | bytes 1376264 | tf_op jit(solution)/shard_map/ppermute | solution.py:110
  37.5 14.4 %collective-permute-start = (bf16[256,896]{1,0:T(8,128)(2,1)S(1)}, bf16[256,896]{1,0:T(8,128)(2,1)S(1)}, u32[]{:S(2)}, u32[]{:S(2)}) collective-permute-start(bf16[256,896]{1,0:T(8,128)(2,1)S(1)} %get-tuple-element.197.refs_0_), channel_id=1, source_target_pairs={{0,96},{16,112},{32,0},{48,16},{64,32},{80,48},{96,64},{112,80},{1... | collective-permute-start | bytes 1376264 | tf_op jit(solution)/shard_map/ppermute | solution.py:113
  41.3 15.8 %collective-permute-start.9 = (bf16[240,896]{1,0:T(8,128)(2,1)S(1)}, bf16[240,896]{1,0:T(8,128)(2,1)S(1)}, u32[]{:S(2)}, u32[]{:S(2)}) collective-permute-start(bf16[240,896]{1,0:T(8,128)(2,1)S(1)} %get-tuple-element.125), channel_id=1, source_target_pairs={{0,96},{16,112},{32,0},{48,16},{64,32},{80,48},{96,64},{112,80},{1... | collective-permute-start | bytes 1290248 | tf_op jit(solution)/shard_map/ppermute | solution.py:113
  42.6 18.5 %collective-permute-start.11 = (bf16[288,896]{1,0:T(8,128)(2,1)S(1)}, bf16[288,896]{1,0:T(8,128)(2,1)S(1)}, u32[]{:S(2)}, u32[]{:S(2)}) collective-permute-start(bf16[288,896]{1,0:T(8,128)(2,1)S(1)} %get-tuple-element.127), channel_id=1, source_target_pairs={{0,16},{16,0},{32,48},{48,32},{64,80},{80,64},{96,112},{112,96},{1... | collective-permute-start | bytes 1548296 | tf_op jit(solution)/shard_map/ppermute | solution.py:116
  47.3 13.9 %collective-permute-start.10 = (bf16[240,896]{1,0:T(8,128)(2,1)S(1)}, bf16[240,896]{1,0:T(8,128)(2,1)S(1)}, u32[]{:S(2)}, u32[]{:S(2)}) collective-permute-start(bf16[240,896]{1,0:T(8,128)(2,1)S(1)} %get-tuple-element.126), channel_id=1, source_target_pairs={{0,32},{16,48},{32,64},{48,80},{64,96},{80,112},{96,0},{112,16},{1... | collective-permute-start | bytes 1290248 | tf_op jit(solution)/shard_map/ppermute | solution.py:110
  52.0 17.5 %collective-permute-start.8 = (bf16[288,896]{1,0:T(8,128)(2,1)S(1)}, bf16[288,896]{1,0:T(8,128)(2,1)S(1)}, u32[]{:S(2)}, u32[]{:S(2)}) collective-permute-start(bf16[288,896]{1,0:T(8,128)(2,1)S(1)} %get-tuple-element.137), channel_id=1, source_target_pairs={{0,16},{16,0},{32,48},{48,32},{64,80},{80,64},{96,112},{112,96},{1... | collective-permute-start | bytes 1548296 | tf_op jit(solution)/shard_map/ppermute | solution.py:116
  52.4 14.0 %collective-permute-start.6 = (bf16[240,896]{1,0:T(8,128)(2,1)S(1)}, bf16[240,896]{1,0:T(8,128)(2,1)S(1)}, u32[]{:S(2)}, u32[]{:S(2)}) collective-permute-start(bf16[240,896]{1,0:T(8,128)(2,1)S(1)} %get-tuple-element.135), channel_id=1, source_target_pairs={{0,96},{16,112},{32,0},{48,16},{64,32},{80,48},{96,64},{112,80},{1... | collective-permute-start | bytes 1290248 | tf_op jit(solution)/shard_map/ppermute | solution.py:113
  57.1 9.2 %collective-permute-start.7 = (bf16[240,896]{1,0:T(8,128)(2,1)S(1)}, bf16[240,896]{1,0:T(8,128)(2,1)S(1)}, u32[]{:S(2)}, u32[]{:S(2)}) collective-permute-start(bf16[240,896]{1,0:T(8,128)(2,1)S(1)} %get-tuple-element.136), channel_id=1, source_target_pairs={{0,32},{16,48},{32,64},{48,80},{64,96},{80,112},{96,0},{112,16},{1... | collective-permute-start | bytes 1290248 | tf_op jit(solution)/shard_map/ppermute | solution.py:110
  61.2 14.3 %collective-permute-start.14 = (bf16[128,896]{1,0:T(8,128)(2,1)S(1)}, bf16[128,896]{1,0:T(8,128)(2,1)S(1)}, u32[]{:S(2)}, u32[]{:S(2)}) collective-permute-start(bf16[128,896]{1,0:T(8,128)(2,1)S(1)} %get-tuple-element.145), channel_id=1, source_target_pairs={{0,96},{16,112},{32,0},{48,16},{64,32},{80,48},{96,64},{112,80},{1... | collective-permute-start | bytes 688136 | tf_op jit(solution)/shard_map/ppermute | solution.py:113
  62.8 12.8 %collective-permute-start.15 = (bf16[128,896]{1,0:T(8,128)(2,1)S(1)}, bf16[128,896]{1,0:T(8,128)(2,1)S(1)}, u32[]{:S(2)}, u32[]{:S(2)}) collective-permute-start(bf16[128,896]{1,0:T(8,128)(2,1)S(1)} %get-tuple-element.146), channel_id=1, source_target_pairs={{0,32},{16,48},{32,64},{48,80},{64,96},{80,112},{96,0},{112,16},{1... | collective-permute-start | bytes 688136 | tf_op jit(solution)/shard_map/ppermute | solution.py:110
  69.4 11.1 %collective-permute-start.12 = (bf16[128,896]{1,0:T(8,128)(2,1)S(1)}, bf16[128,896]{1,0:T(8,128)(2,1)S(1)}, u32[]{:S(2)}, u32[]{:S(2)}) collective-permute-start(bf16[128,896]{1,0:T(8,128)(2,1)S(1)} %get-tuple-element.153), channel_id=1, source_target_pairs={{0,96},{16,112},{32,0},{48,16},{64,32},{80,48},{96,64},{112,80},{1... | collective-permute-start | bytes 688136 | tf_op jit(solution)/shard_map/ppermute | solution.py:113
  85.8 12.0 %collective-permute-start.20 = (bf16[384,896]{1,0:T(8,128)(2,1)S(1)}, bf16[384,896]{1,0:T(8,128)(2,1)S(1)}, u32[]{:S(2)}, u32[]{:S(2)}) collective-permute-start(bf16[384,896]{1,0:T(8,128)(2,1)S(1)} %get-tuple-element.177), channel_id=1, source_target_pairs={{0,16},{16,0},{32,48},{48,32},{64,80},{80,64},{96,112},{112,96},{1... | collective-permute-start | bytes 2064392 | tf_op jit(solution)/shard_map/ppermute | solution.py:116
  86.2 10.4 %collective-permute-start.18 = (bf16[192,896]{1,0:T(8,128)(2,1)S(1)}, bf16[192,896]{1,0:T(8,128)(2,1)S(1)}, u32[]{:S(2)}, u32[]{:S(2)}) collective-permute-start(bf16[192,896]{1,0:T(8,128)(2,1)S(1)} %get-tuple-element.175), channel_id=1, source_target_pairs={{0,32},{16,48},{32,64},{48,80},{64,96},{80,112},{96,0},{112,16},{1... | collective-permute-start | bytes 1032200 | tf_op jit(solution)/shard_map/ppermute | solution.py:110
  86.2 10.4 %collective-permute-start.19 = (bf16[192,896]{1,0:T(8,128)(2,1)S(1)}, bf16[192,896]{1,0:T(8,128)(2,1)S(1)}, u32[]{:S(2)}, u32[]{:S(2)}) collective-permute-start(bf16[192,896]{1,0:T(8,128)(2,1)S(1)} %get-tuple-element.176), channel_id=1, source_target_pairs={{0,96},{16,112},{32,0},{48,16},{64,32},{80,48},{96,64},{112,80},{1... | collective-permute-start | bytes 1032200 | tf_op jit(solution)/shard_map/ppermute | solution.py:113
  98.3 19.6 %collective-permute-start.25 = (bf16[544,896]{1,0:T(8,128)(2,1)S(1)}, bf16[544,896]{1,0:T(8,128)(2,1)S(1)}, u32[]{:S(2)}, u32[]{:S(2)}) collective-permute-start(bf16[544,896]{1,0:T(8,128)(2,1)S(1)} %get-tuple-element.190), channel_id=1, source_target_pairs={{0,16},{16,0},{32,48},{48,32},{64,80},{80,64},{96,112},{112,96},{1... | collective-permute-start | bytes 2924552 | tf_op jit(solution)/shard_map/ppermute | solution.py:116
  98.6 15.2 %collective-permute-start.23 = (bf16[496,896]{1,0:T(8,128)(2,1)S(1)}, bf16[496,896]{1,0:T(8,128)(2,1)S(1)}, u32[]{:S(2)}, u32[]{:S(2)}) collective-permute-start(bf16[496,896]{1,0:T(8,128)(2,1)S(1)} %get-tuple-element.188), channel_id=1, source_target_pairs={{0,32},{16,48},{32,64},{48,80},{64,96},{80,112},{96,0},{112,16},{1... | collective-permute-start | bytes 2666504 | tf_op jit(solution)/shard_map/ppermute | solution.py:110
  98.6 15.2 %collective-permute-start.24 = (bf16[496,896]{1,0:T(8,128)(2,1)S(1)}, bf16[496,896]{1,0:T(8,128)(2,1)S(1)}, u32[]{:S(2)}, u32[]{:S(2)}) collective-permute-start(bf16[496,896]{1,0:T(8,128)(2,1)S(1)} %get-tuple-element.189), channel_id=1, source_target_pairs={{0,96},{16,112},{32,0},{48,16},{64,32},{80,48},{96,64},{112,80},{1... | collective-permute-start | bytes 2666504 | tf_op jit(solution)/shard_map/ppermute | solution.py:113
  118.2 8.7 %collective-permute-start.26 = (bf16[256,896]{1,0:T(8,128)(2,1)S(1)}, bf16[256,896]{1,0:T(8,128)(2,1)S(1)}, u32[]{:S(2)}, u32[]{:S(2)}) collective-permute-start(bf16[256,896]{1,0:T(8,128)(2,1)S(1)} %get-tuple-element.219), channel_id=1, source_target_pairs={{0,32},{16,48},{32,64},{48,80},{64,96},{80,112},{96,0},{112,16},{1... | collective-permute-start | bytes 1376264 | tf_op jit(solution)/shard_map/ppermute | solution.py:110
  118.3 8.6 %collective-permute-start.27 = (bf16[256,896]{1,0:T(8,128)(2,1)S(1)}, bf16[256,896]{1,0:T(8,128)(2,1)S(1)}, u32[]{:S(2)}, u32[]{:S(2)}) collective-permute-start(bf16[256,896]{1,0:T(8,128)(2,1)S(1)} %get-tuple-element.220), channel_id=1, source_target_pairs={{0,96},{16,112},{32,0},{48,16},{64,32},{80,48},{96,64},{112,80},{1... | collective-permute-start | bytes 1376264 | tf_op jit(solution)/shard_map/ppermute | solution.py:113
  121.0 8.2 %collective-permute-start.28 = (bf16[256,896]{1,0:T(8,128)(2,1)S(1)}, bf16[256,896]{1,0:T(8,128)(2,1)S(1)}, u32[]{:S(2)}, u32[]{:S(2)}) collective-permute-start(bf16[256,896]{1,0:T(8,128)(2,1)S(1)} %get-tuple-element.221), channel_id=1, source_target_pairs={{0,16},{16,0},{32,48},{48,32},{64,80},{80,64},{96,112},{112,96},{1... | collective-permute-start | bytes 1376264 | tf_op jit(solution)/shard_map/ppermute | solution.py:116
  (5 other events, 38.3 us)

commit v4 on v3

--- a/solution.py
+++ b/solution.py
@@ -8,7 +8,7 @@
 BF = jnp.bfloat16
 F32 = jnp.float32
 HALF = 128
-GATHER_LOW, OUT_LOW, IN_LOW = 112, 64, 112
+GATHER_LOW, OUT_LOW, IN_LOW = 112, 80, 112
 ARRIVING = ((0, 1, 2, 3), (4, 5, 6), (7,))
 LEAVING = ((7,), (4, 5, 6), (1, 2, 3, 0))
 MIB = 1024 * 1024
@@ -43,6 +43,14 @@
 def wait(copies):
     for copy in copies:
         copy.wait()
+
+
+def exact_dot(weights, values, dims):
+    high = weights.astype(BF)
+    rest = weights - high.astype(F32)
+    middle = rest.astype(BF)
+    low = (rest - middle.astype(F32)).astype(BF)
+    return (dot(low, values, dims) + dot(middle, values, dims)) + dot(high, values, dims)
 
 
 def dispatch_kernel(
@@ -74,7 +82,7 @@
     gated_ref[...] = gated
     wait(arriving)
     x_ref[...] = dot(pick, held[0]).astype(BF)
-    c_ref[...] = dot(gated, held[1].astype(F32), precision=lax.Precision.HIGHEST).astype(BF)
+    c_ref[...] = exact_dot(gated, held[1], ((1,), (0,))).astype(BF)
 
 
 def dispatch(ids, gates, tokens, upstream, total):
@@ -247,14 +255,35 @@
     return [pltpu.SemaphoreType.DMA((each * len(blocks),))]
 
 
+def fetch_kernel(gate_ref, up_ref, down_ref, gate_held, up_held, down_held, semaphores):
+    copies = Copies(semaphores)
+    arriving = load_columns(copies, (gate_ref, up_ref), (gate_held, up_held), ARRIVING[2])
+    arriving += load_rows(copies, down_ref, down_held, ARRIVING[2])
+    for started in arriving:
+        wait(started)
+
+
+def fetch_last(weights, down_flat, width):
+    hid = weights[0].shape[2]
+    columns = jax.ShapeDtypeStruct((1, 2, width, hid), BF)
+    return pl.pallas_call(
+        fetch_kernel,
+        in_specs=[HBM] * 3,
+        out_shape=(columns, columns, jax.ShapeDtypeStruct((1, 2 * hid, width), BF)),
+        scratch_shapes=semaphores_for(range(3), 1),
+        compiler_params=SMALL,
+        name="fetch_last",
+    )(*weights, down_flat)
+
+
 NT = ((1,), (1,))
 TN = ((0,), (0,))
 
 
-def gate_up(part, pieces, weights, before=None, down_flat=None):
+def gate_up(part, pieces, weights, before=None, down_held=None):
     blocks = ARRIVING[part]
     rows, width = 2 * HALF, pieces[0].shape[1]
-    hid = weights[0].shape[2]
+    hid = weights[0].shape[-1]
     last = part == len(ARRIVING) - 1
 
     def kernel(*refs):
@@ -262,15 +291,14 @@
         held_pieces, refs = refs[:count], refs[count:]
         if before is not None:
             before_ref, refs = refs[0], refs[1:]
-        columns, refs = refs[:2], refs[2:]
         if last:
-            down_ref, pre_ref, hidden_ref, *cuts, gate_held, up_held, down_held, semaphores = refs
+            gate_held, up_held, down_ref, pre_ref, hidden_ref, *cuts = refs
+            arriving = [()]
         else:
-            pre_ref, gate_held, up_held, semaphores = refs
-        copies = Copies(semaphores)
-        arriving = load_columns(copies, columns, (gate_held, up_held), blocks)
-        if last:
-            down_arriving = load_rows(copies, down_ref, down_held, blocks)
+            gate_ref, up_ref, pre_ref, gate_held, up_held, semaphores = refs
+            arriving = load_columns(
+                Copies(semaphores), (gate_ref, up_ref), (gate_held, up_held), blocks
+            )
         first = row_slot((rows, hid))
         for i, value in enumerate(arrived_blocks(part, held_pieces)):
             wait(arriving[i])
@@ -288,21 +316,20 @@
             gate = pre_ref[:, :hid]
             hidden = pair(first, (gate * jax.nn.sigmoid(gate) * pre_ref[:, hid:]).astype(BF))
             hidden_ref[...] = hidden
-            wait(down_arriving[0])
-            store_sum(0, 0, dot(hidden, down_held[0]).astype(BF), cuts)
+            store_sum(0, 0, dot(hidden, down_ref[0]).astype(BF), cuts)
 
     shapes = [jax.ShapeDtypeStruct((rows, 2 * hid), F32)]
-    scratch = column_buffers(blocks, width, hid)
+    scratch = column_buffers(blocks, width, hid) + semaphores_for(blocks, 2)
+    extra = [] if before is None else [before]
     if last:
         shapes += [jax.ShapeDtypeStruct((rows, 2 * hid), BF)] + sum_shapes(0, rows, width)
-        scratch += row_buffers(blocks, width, hid)
-        weights = (*weights, down_flat)
-    extra = [] if before is None else [before]
+        scratch = []
+        weights = (*weights, down_held)
     out = pl.pallas_call(
         kernel,
-        in_specs=[VMEM] * (len(pieces) + len(extra)) + [HBM] * len(weights),
+        in_specs=[VMEM] * (len(pieces) + len(extra)) + [VMEM if last else HBM] * len(weights),
         out_shape=shapes,
-        scratch_shapes=scratch + semaphores_for(blocks, 3),
+        scratch_shapes=scratch,
         compiler_params=LARGE,
         name=f"gate_up_{part}",
     )(*pieces, *extra, *weights)
@@ -347,7 +374,7 @@
 def cotangents(part, pieces, down_flat, before=None, pre=None, weights=()):
     blocks = ARRIVING[part]
     rows, width = 2 * HALF, pieces[0].shape[1]
-    hid = down_flat.shape[0] // 2
+    hid = down_flat.shape[-2] // 2
     last = part == len(ARRIVING) - 1
 
     def kernel(*refs):
@@ -356,17 +383,11 @@
         if before is not None:
             before_ref, refs = refs[0], refs[1:]
         if last:
-            pre_ref, refs = refs[0], refs[1:]
-        down_ref, refs = refs[0], refs[1:]
-        if last:
-            columns, refs = refs[:2], refs[2:]
-            *outs, down_held, gate_held, up_held, semaphores = refs
+            pre_ref, down_held, gate_held, up_held, *outs = refs
+            arriving = [()]
         else:
-            *outs, down_held, semaphores = refs
-        copies = Copies(semaphores)
-        arriving = load_rows(copies, down_ref, down_held, blocks)
-        if last:
-            columns_arriving = load_columns(copies, columns, (gate_held, up_held), blocks)
+            down_ref, *outs, down_held, semaphores = refs
+            arriving = load_rows(Copies(semaphores), down_ref, down_held, blocks)
         first = row_slot((rows, hid))
         total = before_ref[...] if before is not None else None
         for i, value in enumerate(arrived_blocks(part, held_pieces)):
@@ -384,22 +405,22 @@
         gate_diff, up_diff = pair(first, gate_diff), pair(first, up_diff)
         outs[0][...] = gate_diff
         outs[1][...] = up_diff
-        wait(columns_arriving[0])
         value = dot(gate_diff, both(gate_held, 0), NT) + dot(up_diff, both(up_held, 0), NT)
         store_sum(0, 0, value.astype(BF), outs[2:])
 
-    scratch = row_buffers(blocks, width, hid)
     if last:
         shapes = [jax.ShapeDtypeStruct((rows, 2 * hid), BF)] * 2 + sum_shapes(0, rows, width)
-        scratch += column_buffers(blocks, width, hid)
+        scratch = []
     else:
         shapes = [jax.ShapeDtypeStruct((rows, hid), F32)]
+        scratch = row_buffers(blocks, width, hid) + semaphores_for(blocks, 1)
     extra = [value for value in (before, pre) if value is not None]
+    held = [VMEM if last else HBM] * (1 + len(weights))
     out = pl.pallas_call(
         kernel,
-        in_specs=[VMEM] * (len(pieces) + len(extra)) + [HBM] * (1 + len(weights)),
+        in_specs=[VMEM] * (len(pieces) + len(extra)) + held,
         out_shape=shapes,
-        scratch_shapes=scratch + semaphores_for(blocks, 3),
+        scratch_shapes=scratch,
         compiler_params=LARGE,
         name=f"cotangents_{part}",
     )(*pieces, *extra, down_flat, *weights)
@@ -624,9 +645,7 @@
 
 def combine_kernel(pick_ref, gated_ref, rows_ref, mixed_ref, grads_ref):
     width = mixed_ref.shape[1]
-    mixed_ref[...] = dot(
-        gated_ref[...], wide(rows_ref[:, :width]), TN, lax.Precision.HIGHEST
-    ).astype(BF)
+    mixed_ref[...] = exact_dot(gated_ref[...], rows_ref[:, :width], TN).astype(BF)
     grads_ref[...] = dot(pick_ref[...], rows_ref[:, width:], TN).astype(BF)
 
 
@@ -657,21 +676,22 @@
     c = Gather(links, arrived[:, width:])
     x_sent = x.relay()
     pre = gate_up(0, after(x.arrived[0], *x_sent), columns_in)
-    c_sent = c.relay(pre)
+    *last_columns, last_rows = fetch_last(after(columns_in, pre), rows_in, width)
+    c_sent = c.relay(pre, last_rows)
     total = cotangents(0, after(c.arrived[0], *c_sent), rows_in)
     x_sent = x.ends(total)
     pre = gate_up(1, after(x.arrived[1], *x_sent), columns_in, pre)
     c_sent = c.ends(pre)
     total = cotangents(1, after(c.arrived[1], *c_sent), rows_in, total)
     pre, hidden, *out_cuts = gate_up(
-        2, after(x.arrived[2], total), columns_in, pre, rows_in
+        2, after(x.arrived[2], total), last_columns, pre, last_rows
     )
 
     hops = Sums(links)
     out_got = hops.first(out_cuts)
-    out_far = output_sums(1, after(hidden, *out_cuts, *c.arrived[2]), rows_in, width)
+    out_far = output_sums(1, after(hidden, *out_cuts), rows_in, width)
     *diffs, cut_up, cut_down = cotangents(
-        2, after(c.arrived[2], *out_far), rows_in, total, pre, columns_in
+        2, after(c.arrived[2], *out_far), last_rows, total, pre, last_columns
     )
     in_got = hops.first((cut_up, cut_down))
     sent, out_got = hops.second(*out_far, *after(out_got, cut_up))

time: 160 us -> 156 us (0.975)
  Pallas kernels: 33.9 us -> 32 us
  blocking collectives: 52.3 us -> 50.5 us
    ppermute x7, waiting for transfers between devices: 19.7 us -> 14.6 us  [cross(): return lax.ppermute(value, 'dp', self.side)]
    ppermute x11, waiting for transfers between devices: 11.3 us -> 15.7 us  [send_up(): return lax.ppermute(value, 'dp', self.up)]
    all_to_all x2, blocking collectives: 52.3 us -> 50.5 us  [exchange(): lax.all_to_all(value.reshape(columns, exp_dev * 8, -1), 'expert', 0, 0, t...]
    pallas_call x6 -> x7, Pallas kernels: 14.2 us -> 12.9 us  [the longest x3 5.98 us: gate_up(): pl.pallas_call(kernel, in_specs=[VMEM] * (len(pieces) + len(extra)) + [VM...]
  transfers between devices with their start and end apart: 29 -> 29, of which waited for: 14 -> 12; matrix products, arithmetic and copies ran while one was open for 0% -> 0% of each run, Pallas kernels for 18% -> 18%
where the time goes in v4:
time: 156 us
  blocking collectives  50.5 us (32%)
  starting transfers between devices  36.3 us (23%)
  waiting for transfers between devices  36.1 us (23%)
  Pallas kernels  32 us (21%)
    all_to_all x2, blocking collectives, exchange(): lax.all_to_all(value.reshape(columns, exp_dev * 8, -1), 'expert', 0, 0, t...  50.5 us
    ppermute x11, starting transfers between devices, send_down(): return lax.ppermute(value, 'dp', self.down)  26 us
    ppermute x11, waiting for transfers between devices, send_up(): return lax.ppermute(value, 'dp', self.up)  15.7 us
    ppermute x7, waiting for transfers between devices, cross(): return lax.ppermute(value, 'dp', self.side)  14.6 us
    pallas_call x3, Pallas kernels, gate_up(): pl.pallas_call(kernel, in_specs=[VMEM] * (len(pieces) + len(extra)) + [VM...  5.98 us
    ppermute x11, starting transfers between devices, send_up(): return lax.ppermute(value, 'dp', self.up)  5.89 us
    ppermute x11, waiting for transfers between devices, send_down(): return lax.ppermute(value, 'dp', self.down)  5.8 us
    pallas_call x3, Pallas kernels, cotangents(): pl.pallas_call(kernel, in_specs=[VMEM] * (len(pieces) + len(extra)) + hel...  5.56 us
  transfers between devices with their start and end apart: 29, of which 12 were waited for; matrix products, arithmetic and copies ran while one was open for 0% of the time, Pallas kernels for 18%

profile of v4, /device:TPU:1, one launch (start us, length us, event | category | flops | bytes accessed | tf_op | source)
XLA Modules:
  0.0 156.0 jit_solution(17730969716293735234)
XLA Ops:
  2.3 23.7 %all_to_all.10 = bf16[16,16,1792]{2,1,0:T(8,128)(2,1)S(1)} all-to-all(bf16[16,16,1792]{2,1,0:T(8,128)(2,1)S(1)} %bitcast.16), channel_id=1, replica_groups=mesh['dp'=8,'expert'=16] {'expert'}, dimensions={0} | all-to-all | bytes 1835008 | tf_op jit(solution)/shard_map/all_to_all | solution.py:669
  28.2 2.1 %collective-permute-start.3 = (bf16[256,896]{1,0:T(8,128)(2,1)S(1)}, bf16[256,896]{1,0:T(8,128)(2,1)S(1)}, u32[]{:S(2)}, u32[]{:S(2)}) collective-permute-start(bf16[256,896]{1,0:T(8,128)(2,1)S(1)} %get-tuple-element.216.refs_0_), channel_id=1, source_target_pairs={{0,96},{16,112},{32,0},{48,16},{64,32},{80,48},{96,64},{112,80},{1... | collective-permute-start | bytes 1376264 | tf_op jit(solution)/shard_map/ppermute | solution.py:121
  31.5 5.6 %collective-permute-done.5.beside.refs_3_ = bf16[256,896]{1,0:T(8,128)(2,1)S(1)} collective-permute-done((bf16[256,896]{1,0:T(8,128)(2,1)S(1)}, bf16[256,896]{1,0:T(8,128)(2,1)S(1)}, u32[]{:S(2)}, u32[]{:S(2)}) %collective-permute-start.5) | collective-permute-done | bytes 458784 | tf_op jit(solution)/shard_map/ppermute | solution.py:124
  37.1 3.8 %collective-permute-start = (bf16[256,896]{1,0:T(8,128)(2,1)S(1)}, bf16[256,896]{1,0:T(8,128)(2,1)S(1)}, u32[]{:S(2)}, u32[]{:S(2)}) collective-permute-start(bf16[256,896]{1,0:T(8,128)(2,1)S(1)} %get-tuple-element.207.refs_0_), channel_id=1, source_target_pairs={{0,96},{16,112},{32,0},{48,16},{64,32},{80,48},{96,64},{112,80},{1... | collective-permute-start | bytes 1376264 | tf_op jit(solution)/shard_map/ppermute | solution.py:121
  43.4 3.5 %collective-permute-done.2.beside.refs_3_ = bf16[256,896]{1,0:T(8,128)(2,1)S(1)} collective-permute-done((bf16[256,896]{1,0:T(8,128)(2,1)S(1)}, bf16[256,896]{1,0:T(8,128)(2,1)S(1)}, u32[]{:S(2)}, u32[]{:S(2)}) %collective-permute-start.2) | collective-permute-done | bytes 458784 | tf_op jit(solution)/shard_map/ppermute | solution.py:124
  48.6 2.9 %gate_up_0.1.refs_3_ = f32[256,256]{1,0:T(8,128)S(1)} custom-call(bf16[256,896]{1,0:T(8,128)(2,1)S(1)} %get-tuple-element.216.refs_0_, bf16[256,896]{1,0:T(8,128)(2,1)S(1)} %collective-permute-done.3.above.refs_1_, bf16[256,896]{1,0:T(8,128)(2,1)S(1)} %collective-permute-done.4.below.refs_2_, bf16[256,896]{1,0:T(8,128)(2,1)S(1)} %collective-permute-done.5.beside.refs_3_, ...), custom_call_target="tpu_custom_call" | custom-call | tf_op jit(solution)/shard_map/gate_up_0/pallas_call | solution.py:328
  58.1 2.7 %cotangents_0.1.refs_3_ = f32[256,128]{1,0:T(8,128)S(1)} custom-call(bf16[256,896]{1,0:T(8,128)(2,1)S(1)} %get-tuple-element.207.refs_0_, bf16[256,896]{1,0:T(8,128)(2,1)S(1)} %collective-permute-done.above.refs_1_, bf16[256,896]{1,0:T(8,128)(2,1)S(1)} %collective-permute-done.1.below.refs_2_, bf16[256,896]{1,0:T(8,128)(2,1)S(1)} %collective-permute-done.2.beside.refs_3_, ...), custom_call_target="tpu_custom_call" | custom-call | tf_op jit(solution)/shard_map/cotangents_0/pallas_call | solution.py:419
  62.4 2.5 %gate_up_1.1.refs_2_ = f32[256,256]{1,0:T(8,128)S(1)} custom-call(bf16[240,896]{1,0:T(8,128)(2,1)S(1)} %collective-permute-done.9.above2.refs_0_.refs_4_, bf16[240,896]{1,0:T(8,128)(2,1)S(1)} %collective-permute-done.10.below2.refs_1_.refs_5_, bf16[288,896]{1,0:T(8,128)(2,1)S(1)} %collective-permute-done.11.beside2.refs_2_.refs_6_, ...), custom_call_target="tpu_custom_call" | custom-call | tf_op jit(solution)/shard_map/gate_up_1/pallas_call | solution.py:328
  66.0 3.0 %collective-permute-done.8.beside2.refs_2_.refs_6_ = bf16[288,896]{1,0:T(8,128)(2,1)S(1)} collective-permute-done((bf16[288,896]{1,0:T(8,128)(2,1)S(1)}, bf16[288,896]{1,0:T(8,128)(2,1)S(1)}, u32[]{:S(2)}, u32[]{:S(2)}) %collective-permute-start.8) | collective-permute-done | bytes 516128 | tf_op jit(solution)/shard_map/ppermute | solution.py:124
  69.1 3.8 %collective-permute-start.12 = (bf16[128,896]{1,0:T(8,128)(2,1)S(1)}, bf16[128,896]{1,0:T(8,128)(2,1)S(1)}, u32[]{:S(2)}, u32[]{:S(2)}) collective-permute-start(bf16[128,896]{1,0:T(8,128)(2,1)S(1)} %get-tuple-element.161), channel_id=1, source_target_pairs={{0,96},{16,112},{32,0},{48,16},{64,32},{80,48},{96,64},{112,80},{1... | collective-permute-start | bytes 688136 | tf_op jit(solution)/shard_map/ppermute | solution.py:121
  72.9 2.2 %cotangents_1.1.refs_2_ = f32[256,128]{1,0:T(8,128)S(1)} custom-call(bf16[240,896]{1,0:T(8,128)(2,1)S(1)} %collective-permute-done.6.above2.refs_0_.refs_4_, bf16[240,896]{1,0:T(8,128)(2,1)S(1)} %collective-permute-done.7.below2.refs_1_.refs_5_, bf16[288,896]{1,0:T(8,128)(2,1)S(1)} %collective-permute-done.8.beside2.refs_2_.refs_6_, ...), custom_call_target="tpu_custom_call" | custom-call | tf_op jit(solution)/shard_map/cotangents_1/pallas_call | solution.py:419
  75.9 2.9 %collective-permute-start.17 = (bf16[128,896]{1,0:T(8,128)(2,1)S(1)}, bf16[128,896]{1,0:T(8,128)(2,1)S(1)}, u32[]{:S(2)}, u32[]{:S(2)}) collective-permute-start(bf16[128,896]{1,0:T(8,128)(2,1)S(1)} %get-tuple-element.172), channel_id=1, source_target_pairs={{0,96},{16,112},{32,0},{48,16},{64,32},{80,48},{96,64},{112,80},{1... | collective-permute-start | bytes 688136 | tf_op jit(solution)/shard_map/ppermute | solution.py:121
  81.5 3.2 %collective-permute-done.16.refs_3_ = bf16[128,896]{1,0:T(8,128)(2,1)S(1)} collective-permute-done((bf16[128,896]{1,0:T(8,128)(2,1)S(1)}, bf16[128,896]{1,0:T(8,128)(2,1)S(1)}, u32[]{:S(2)}, u32[]{:S(2)}) %collective-permute-start.16) | collective-permute-done | bytes 229408 | tf_op jit(solution)/shard_map/ppermute | solution.py:118
  85.0 2.7 %collective-permute-start.19 = (bf16[208,896]{1,0:T(8,128)(2,1)S(1)}, bf16[208,896]{1,0:T(8,128)(2,1)S(1)}, u32[]{:S(2)}, u32[]{:S(2)}) collective-permute-start(bf16[208,896]{1,0:T(8,128)(2,1)S(1)} %get-tuple-element.186), channel_id=1, source_target_pairs={{0,96},{16,112},{32,0},{48,16},{64,32},{80,48},{96,64},{112,80},{1... | collective-permute-start | bytes 1118216 | tf_op jit(solution)/shard_map/ppermute | solution.py:121
  89.2 3.9 %middle_sums.1 = (bf16[256,896]{1,0:T(8,128)(2,1)S(1)}, bf16[256,896]{1,0:T(8,128)(2,1)S(1)}, bf16[256,896]{1,0:T(8,128)(2,1)S(1)}, bf16[256,896]{1,0:T(8,128)(2...) custom-call(bf16[256,256]{1,0:T(8,128)(2,1)S(1)} %get-tuple-element.201.gate_diff_, ...), custom_call_target="tpu_custom_call" | custom-call | tf_op jit(solution)/shard_map/middle_sums/pallas_call | solution.py:475
  93.1 3.2 %collective-permute-done.22.refs_10_ = bf16[128,896]{1,0:T(8,128)(2,1)S(1)} collective-permute-done((bf16[128,896]{1,0:T(8,128)(2,1)S(1)}, bf16[128,896]{1,0:T(8,128)(2,1)S(1)}, u32[]{:S(2)}, u32[]{:S(2)}) %collective-permute-start.22) | collective-permute-done | bytes 229408 | tf_op jit(solution)/shard_map/ppermute | solution.py:121
  99.0 2.7 %collective-permute-start.24 = (bf16[496,896]{1,0:T(8,128)(2,1)S(1)}, bf16[496,896]{1,0:T(8,128)(2,1)S(1)}, u32[]{:S(2)}, u32[]{:S(2)}) collective-permute-start(bf16[496,896]{1,0:T(8,128)(2,1)S(1)} %get-tuple-element.199), channel_id=1, source_target_pairs={{0,96},{16,112},{32,0},{48,16},{64,32},{80,48},{96,64},{112,80},{1... | collective-permute-start | bytes 2666504 | tf_op jit(solution)/shard_map/ppermute | solution.py:121
  101.7 3.1 %input_sums_2.1 = (bf16[256,896]{1,0:T(8,128)(2,1)S(1)}, bf16[256,896]{1,0:T(8,128)(2,1)S(1)}, bf16[256,896]{1,0:T(8,128)(2,1)S(1)}, bf16[256,896]{1,0:T(8,128)(2,1)S(1)}) custom-call(bf16[256,256]{1,0:T(8,128)(2,1)S(1)} %get-tuple-element.201.gate_diff_ref.refs_9_, bf16[256,256]{1,0:T(8,128)(2,1)S(1)} %get-tuple-element.202.up_diff_ref.refs_10_, ...), custom_call_target="tpu_custom_call" | custom-call | tf_op jit(solution)/shard_map/input_sums_2/pallas_call | solution.py:446
  104.8 2.2 %row_grads.1 = bf16[256,7168]{1,0:T(8,128)(2,1)} custom-call(bf16[256,896]{1,0:T(8,128)(2,1)S(1)} %get-tuple-element.207.refs_0_, bf16[256,896]{1,0:T(8,128)(2,1)S(1)} %collective-permute-done.above.refs_1_, bf16[256,896]{1,0:T(8,128)(2,1)S(1)} %collective-permute-done.1.below.refs_2_, bf16[256,896]{1,0:T(8,128)(2,1)S(1)} %collective-permute-done.2.beside.refs_3_, ...), custom_call_target="tpu_custom_call" | custom-call | tf_op jit(solution)/shard_map/row_grads/pallas_call | solution.py:544
  107.0 3.5 %column_grads.1 = (bf16[2,7168,128]{2,1,0:T(8,128)(2,1)}, bf16[2,7168,128]{2,1,0:T(8,128)(2,1)}) custom-call(bf16[256,896]{1,0:T(8,128)(2,1)S(1)} %get-tuple-element.216.refs_0_, bf16[256,896]{1,0:T(8,128)(2,1)S(1)} %collective-permute-done.3.above.refs_1_, bf16[256,896]{1,0:T(8,128)(2,1)S(1)} %collective-permute-done.4.below.refs_2_, ...), custom_call_target="tpu_custom_call" | custom-call | tf_op jit(solution)/shard_map/column_grads/pallas_call | solution.py:516
  110.6 5.4 %collective-permute-done.23.got_up.from_below = bf16[496,896]{1,0:T(8,128)(2,1)S(1)} collective-permute-done((bf16[496,896]{1,0:T(8,128)(2,1)S(1)}, bf16[496,896]{1,0:T(8,128)(2,1)S(1)}, u32[]{:S(2)}, u32[]{:S(2)}) %collective-permute-start.23) | collective-permute-done | bytes 888864 | tf_op jit(solution)/shard_map/ppermute | solution.py:118
  117.6 2.7 %collective-permute-start.27 = (bf16[256,896]{1,0:T(8,128)(2,1)S(1)}, bf16[256,896]{1,0:T(8,128)(2,1)S(1)}, u32[]{:S(2)}, u32[]{:S(2)}) collective-permute-start(bf16[256,896]{1,0:T(8,128)(2,1)S(1)} %get-tuple-element.230), channel_id=1, source_target_pairs={{0,96},{16,112},{32,0},{48,16},{64,32},{80,48},{96,64},{112,80},{1... | collective-permute-start | bytes 1376264 | tf_op jit(solution)/shard_map/ppermute | solution.py:121
  120.5 6.1 %collective-permute-done.26.from_below = bf16[256,896]{1,0:T(8,128)(2,1)S(1)} collective-permute-done((bf16[256,896]{1,0:T(8,128)(2,1)S(1)}, bf16[256,896]{1,0:T(8,128)(2,1)S(1)}, u32[]{:S(2)}, u32[]{:S(2)}) %collective-permute-start.26) | collective-permute-done | bytes 458784 | tf_op jit(solution)/shard_map/ppermute | solution.py:118
  128.2 26.7 %all_to_all.11 = bf16[16,16,1792]{2,1,0:T(8,128)(2,1)S(1)} all-to-all(bf16[16,16,1792]{2,1,0:T(8,128)(2,1)S(1)} %bitcast.17), channel_id=1, replica_groups=mesh['dp'=8,'expert'=16] {'expert'}, dimensions={0} | all-to-all | bytes 1835008 | tf_op jit(solution)/shard_map/all_to_all | solution.py:669
  (62 shorter events, 31.0 us)
Async XLA Ops:
  26.2 10.9 %collective-permute-start.5 = (bf16[256,896]{1,0:T(8,128)(2,1)S(1)}, bf16[256,896]{1,0:T(8,128)(2,1)S(1)}, u32[]{:S(2)}, u32[]{:S(2)}) collective-permute-start(bf16[256,896]{1,0:T(8,128)(2,1)S(1)} %get-tuple-element.216.refs_0_), channel_id=1, source_target_pairs={{0,16},{16,0},{32,48},{48,32},{64,80},{80,64},{96,112},{112,96},{1... | collective-permute-start | bytes 1376264 | tf_op jit(solution)/shard_map/ppermute | solution.py:124
  26.6 14.3 %collective-permute-start.4 = (bf16[256,896]{1,0:T(8,128)(2,1)S(1)}, bf16[256,896]{1,0:T(8,128)(2,1)S(1)}, u32[]{:S(2)}, u32[]{:S(2)}) collective-permute-start(bf16[256,896]{1,0:T(8,128)(2,1)S(1)} %get-tuple-element.216.refs_0_), channel_id=1, source_target_pairs={{0,32},{16,48},{32,64},{48,80},{64,96},{80,112},{96,0},{112,16},{1... | collective-permute-start | bytes 1376264 | tf_op jit(solution)/shard_map/ppermute | solution.py:118
  28.2 12.7 %collective-permute-start.3 = (bf16[256,896]{1,0:T(8,128)(2,1)S(1)}, bf16[256,896]{1,0:T(8,128)(2,1)S(1)}, u32[]{:S(2)}, u32[]{:S(2)}) collective-permute-start(bf16[256,896]{1,0:T(8,128)(2,1)S(1)} %get-tuple-element.216.refs_0_), channel_id=1, source_target_pairs={{0,96},{16,112},{32,0},{48,16},{64,32},{80,48},{96,64},{112,80},{1... | collective-permute-start | bytes 1376264 | tf_op jit(solution)/shard_map/ppermute | solution.py:121
  30.3 16.6 %collective-permute-start.2 = (bf16[256,896]{1,0:T(8,128)(2,1)S(1)}, bf16[256,896]{1,0:T(8,128)(2,1)S(1)}, u32[]{:S(2)}, u32[]{:S(2)}) collective-permute-start(bf16[256,896]{1,0:T(8,128)(2,1)S(1)} %get-tuple-element.207.refs_0_), channel_id=1, source_target_pairs={{0,16},{16,0},{32,48},{48,32},{64,80},{80,64},{96,112},{112,96},{1... | collective-permute-start | bytes 1376264 | tf_op jit(solution)/shard_map/ppermute | solution.py:124
  31.5 21.3 %collective-permute-start.1 = (bf16[256,896]{1,0:T(8,128)(2,1)S(1)}, bf16[256,896]{1,0:T(8,128)(2,1)S(1)}, u32[]{:S(2)}, u32[]{:S(2)}) collective-permute-start(bf16[256,896]{1,0:T(8,128)(2,1)S(1)} %get-tuple-element.207.refs_0_), channel_id=1, source_target_pairs={{0,32},{16,48},{32,64},{48,80},{64,96},{80,112},{96,0},{112,16},{1... | collective-permute-start | bytes 1376264 | tf_op jit(solution)/shard_map/ppermute | solution.py:118
  37.1 15.7 %collective-permute-start = (bf16[256,896]{1,0:T(8,128)(2,1)S(1)}, bf16[256,896]{1,0:T(8,128)(2,1)S(1)}, u32[]{:S(2)}, u32[]{:S(2)}) collective-permute-start(bf16[256,896]{1,0:T(8,128)(2,1)S(1)} %get-tuple-element.207.refs_0_), channel_id=1, source_target_pairs={{0,96},{16,112},{32,0},{48,16},{64,32},{80,48},{96,64},{112,80},{1... | collective-permute-start | bytes 1376264 | tf_op jit(solution)/shard_map/ppermute | solution.py:121
  41.0 15.8 %collective-permute-start.9 = (bf16[240,896]{1,0:T(8,128)(2,1)S(1)}, bf16[240,896]{1,0:T(8,128)(2,1)S(1)}, u32[]{:S(2)}, u32[]{:S(2)}) collective-permute-start(bf16[240,896]{1,0:T(8,128)(2,1)S(1)} %get-tuple-element.130), channel_id=1, source_target_pairs={{0,96},{16,112},{32,0},{48,16},{64,32},{80,48},{96,64},{112,80},{1... | collective-permute-start | bytes 1290248 | tf_op jit(solution)/shard_map/ppermute | solution.py:121
  42.3 18.5 %collective-permute-start.11 = (bf16[288,896]{1,0:T(8,128)(2,1)S(1)}, bf16[288,896]{1,0:T(8,128)(2,1)S(1)}, u32[]{:S(2)}, u32[]{:S(2)}) collective-permute-start(bf16[288,896]{1,0:T(8,128)(2,1)S(1)} %get-tuple-element.132), channel_id=1, source_target_pairs={{0,16},{16,0},{32,48},{48,32},{64,80},{80,64},{96,112},{112,96},{1... | collective-permute-start | bytes 1548296 | tf_op jit(solution)/shard_map/ppermute | solution.py:124
  46.9 13.8 %collective-permute-start.10 = (bf16[240,896]{1,0:T(8,128)(2,1)S(1)}, bf16[240,896]{1,0:T(8,128)(2,1)S(1)}, u32[]{:S(2)}, u32[]{:S(2)}) collective-permute-start(bf16[240,896]{1,0:T(8,128)(2,1)S(1)} %get-tuple-element.131), channel_id=1, source_target_pairs={{0,32},{16,48},{32,64},{48,80},{64,96},{80,112},{96,0},{112,16},{1... | collective-permute-start | bytes 1290248 | tf_op jit(solution)/shard_map/ppermute | solution.py:118
  52.9 16.1 %collective-permute-start.8 = (bf16[288,896]{1,0:T(8,128)(2,1)S(1)}, bf16[288,896]{1,0:T(8,128)(2,1)S(1)}, u32[]{:S(2)}, u32[]{:S(2)}) collective-permute-start(bf16[288,896]{1,0:T(8,128)(2,1)S(1)} %get-tuple-element.145), channel_id=1, source_target_pairs={{0,16},{16,0},{32,48},{48,32},{64,80},{80,64},{96,112},{112,96},{1... | collective-permute-start | bytes 1548296 | tf_op jit(solution)/shard_map/ppermute | solution.py:124
  53.3 12.7 %collective-permute-start.6 = (bf16[240,896]{1,0:T(8,128)(2,1)S(1)}, bf16[240,896]{1,0:T(8,128)(2,1)S(1)}, u32[]{:S(2)}, u32[]{:S(2)}) collective-permute-start(bf16[240,896]{1,0:T(8,128)(2,1)S(1)} %get-tuple-element.143), channel_id=1, source_target_pairs={{0,96},{16,112},{32,0},{48,16},{64,32},{80,48},{96,64},{112,80},{1... | collective-permute-start | bytes 1290248 | tf_op jit(solution)/shard_map/ppermute | solution.py:121
  56.8 9.2 %collective-permute-start.7 = (bf16[240,896]{1,0:T(8,128)(2,1)S(1)}, bf16[240,896]{1,0:T(8,128)(2,1)S(1)}, u32[]{:S(2)}, u32[]{:S(2)}) collective-permute-start(bf16[240,896]{1,0:T(8,128)(2,1)S(1)} %get-tuple-element.144), channel_id=1, source_target_pairs={{0,32},{16,48},{32,64},{48,80},{64,96},{80,112},{96,0},{112,16},{1... | collective-permute-start | bytes 1290248 | tf_op jit(solution)/shard_map/ppermute | solution.py:118
  60.8 14.3 %collective-permute-start.14 = (bf16[128,896]{1,0:T(8,128)(2,1)S(1)}, bf16[128,896]{1,0:T(8,128)(2,1)S(1)}, u32[]{:S(2)}, u32[]{:S(2)}) collective-permute-start(bf16[128,896]{1,0:T(8,128)(2,1)S(1)} %get-tuple-element.153), channel_id=1, source_target_pairs={{0,96},{16,112},{32,0},{48,16},{64,32},{80,48},{96,64},{112,80},{1... | collective-permute-start | bytes 688136 | tf_op jit(solution)/shard_map/ppermute | solution.py:121
  62.3 12.8 %collective-permute-start.15 = (bf16[128,896]{1,0:T(8,128)(2,1)S(1)}, bf16[128,896]{1,0:T(8,128)(2,1)S(1)}, u32[]{:S(2)}, u32[]{:S(2)}) collective-permute-start(bf16[128,896]{1,0:T(8,128)(2,1)S(1)} %get-tuple-element.154), channel_id=1, source_target_pairs={{0,32},{16,48},{32,64},{48,80},{64,96},{80,112},{96,0},{112,16},{1... | collective-permute-start | bytes 688136 | tf_op jit(solution)/shard_map/ppermute | solution.py:118
  69.1 11.7 %collective-permute-start.12 = (bf16[128,896]{1,0:T(8,128)(2,1)S(1)}, bf16[128,896]{1,0:T(8,128)(2,1)S(1)}, u32[]{:S(2)}, u32[]{:S(2)}) collective-permute-start(bf16[128,896]{1,0:T(8,128)(2,1)S(1)} %get-tuple-element.161), channel_id=1, source_target_pairs={{0,96},{16,112},{32,0},{48,16},{64,32},{80,48},{96,64},{112,80},{1... | collective-permute-start | bytes 688136 | tf_op jit(solution)/shard_map/ppermute | solution.py:121
  84.9 12.4 %collective-permute-start.20 = (bf16[352,896]{1,0:T(8,128)(2,1)S(1)}, bf16[352,896]{1,0:T(8,128)(2,1)S(1)}, u32[]{:S(2)}, u32[]{:S(2)}) collective-permute-start(bf16[352,896]{1,0:T(8,128)(2,1)S(1)} %get-tuple-element.187), channel_id=1, source_target_pairs={{0,16},{16,0},{32,48},{48,32},{64,80},{80,64},{96,112},{112,96},{1... | collective-permute-start | bytes 1892360 | tf_op jit(solution)/shard_map/ppermute | solution.py:124
  84.9 12.3 %collective-permute-start.18 = (bf16[208,896]{1,0:T(8,128)(2,1)S(1)}, bf16[208,896]{1,0:T(8,128)(2,1)S(1)}, u32[]{:S(2)}, u32[]{:S(2)}) collective-permute-start(bf16[208,896]{1,0:T(8,128)(2,1)S(1)} %get-tuple-element.185), channel_id=1, source_target_pairs={{0,32},{16,48},{32,64},{48,80},{64,96},{80,112},{96,0},{112,16},{1... | collective-permute-start | bytes 1118216 | tf_op jit(solution)/shard_map/ppermute | solution.py:118
  85.0 12.3 %collective-permute-start.19 = (bf16[208,896]{1,0:T(8,128)(2,1)S(1)}, bf16[208,896]{1,0:T(8,128)(2,1)S(1)}, u32[]{:S(2)}, u32[]{:S(2)}) collective-permute-start(bf16[208,896]{1,0:T(8,128)(2,1)S(1)} %get-tuple-element.186), channel_id=1, source_target_pairs={{0,96},{16,112},{32,0},{48,16},{64,32},{80,48},{96,64},{112,80},{1... | collective-permute-start | bytes 1118216 | tf_op jit(solution)/shard_map/ppermute | solution.py:121
  88.1 9.2 %collective-permute-start.21 = (bf16[128,896]{1,0:T(8,128)(2,1)S(1)}, bf16[128,896]{1,0:T(8,128)(2,1)S(1)}, u32[]{:S(2)}, u32[]{:S(2)}) collective-permute-start(bf16[128,896]{1,0:T(8,128)(2,1)S(1)} %get-tuple-element.182), channel_id=1, source_target_pairs={{0,32},{16,48},{32,64},{48,80},{64,96},{80,112},{96,0},{112,16},{1... | collective-permute-start | bytes 688136 | tf_op jit(solution)/shard_map/ppermute | solution.py:118
  97.8 19.4 %collective-permute-start.25 = (bf16[544,896]{1,0:T(8,128)(2,1)S(1)}, bf16[544,896]{1,0:T(8,128)(2,1)S(1)}, u32[]{:S(2)}, u32[]{:S(2)}) collective-permute-start(bf16[544,896]{1,0:T(8,128)(2,1)S(1)} %get-tuple-element.200), channel_id=1, source_target_pairs={{0,16},{16,0},{32,48},{48,32},{64,80},{80,64},{96,112},{112,96},{1... | collective-permute-start | bytes 2924552 | tf_op jit(solution)/shard_map/ppermute | solution.py:124
  99.0 17.0 %collective-permute-start.23 = (bf16[496,896]{1,0:T(8,128)(2,1)S(1)}, bf16[496,896]{1,0:T(8,128)(2,1)S(1)}, u32[]{:S(2)}, u32[]{:S(2)}) collective-permute-start(bf16[496,896]{1,0:T(8,128)(2,1)S(1)} %get-tuple-element.198), channel_id=1, source_target_pairs={{0,32},{16,48},{32,64},{48,80},{64,96},{80,112},{96,0},{112,16},{1... | collective-permute-start | bytes 2666504 | tf_op jit(solution)/shard_map/ppermute | solution.py:118
  99.0 17.0 %collective-permute-start.24 = (bf16[496,896]{1,0:T(8,128)(2,1)S(1)}, bf16[496,896]{1,0:T(8,128)(2,1)S(1)}, u32[]{:S(2)}, u32[]{:S(2)}) collective-permute-start(bf16[496,896]{1,0:T(8,128)(2,1)S(1)} %get-tuple-element.199), channel_id=1, source_target_pairs={{0,96},{16,112},{32,0},{48,16},{64,32},{80,48},{96,64},{112,80},{1... | collective-permute-start | bytes 2666504 | tf_op jit(solution)/shard_map/ppermute | solution.py:121
  117.5 9.1 %collective-permute-start.26 = (bf16[256,896]{1,0:T(8,128)(2,1)S(1)}, bf16[256,896]{1,0:T(8,128)(2,1)S(1)}, u32[]{:S(2)}, u32[]{:S(2)}) collective-permute-start(bf16[256,896]{1,0:T(8,128)(2,1)S(1)} %get-tuple-element.229), channel_id=1, source_target_pairs={{0,32},{16,48},{32,64},{48,80},{64,96},{80,112},{96,0},{112,16},{1... | collective-permute-start | bytes 1376264 | tf_op jit(solution)/shard_map/ppermute | solution.py:118
  117.6 9.0 %collective-permute-start.27 = (bf16[256,896]{1,0:T(8,128)(2,1)S(1)}, bf16[256,896]{1,0:T(8,128)(2,1)S(1)}, u32[]{:S(2)}, u32[]{:S(2)}) collective-permute-start(bf16[256,896]{1,0:T(8,128)(2,1)S(1)} %get-tuple-element.230), channel_id=1, source_target_pairs={{0,96},{16,112},{32,0},{48,16},{64,32},{80,48},{96,64},{112,80},{1... | collective-permute-start | bytes 1376264 | tf_op jit(solution)/shard_map/ppermute | solution.py:121
  (5 other events, 41.8 us)

commit v5 on v4

--- a/solution.py
+++ b/solution.py
@@ -678,9 +678,9 @@
     pre = gate_up(0, after(x.arrived[0], *x_sent), columns_in)
     *last_columns, last_rows = fetch_last(after(columns_in, pre), rows_in, width)
     c_sent = c.relay(pre, last_rows)
-    total = cotangents(0, after(c.arrived[0], *c_sent), rows_in)
-    x_sent = x.ends(total)
-    pre = gate_up(1, after(x.arrived[1], *x_sent), columns_in, pre)
+    x_sent = x.ends(*c_sent)
+    total = cotangents(0, after(c.arrived[0], *x_sent), rows_in)
+    pre = gate_up(1, after(x.arrived[1], total), columns_in, pre)
     c_sent = c.ends(pre)
     total = cotangents(1, after(c.arrived[1], *c_sent), rows_in, total)
     pre, hidden, *out_cuts = gate_up(

time: 156 us -> 156 us (level)
  waiting for transfers between devices: 36.1 us -> 31.3 us
  starting transfers between devices: 36.3 us -> 39.7 us
    ppermute x11, starting transfers between devices: 26 us -> 29.6 us  [send_down(): return lax.ppermute(value, 'dp', self.down)]
    ppermute x11, waiting for transfers between devices: 15.7 us -> 13.7 us  [send_up(): return lax.ppermute(value, 'dp', self.up)]
    ppermute x7, waiting for transfers between devices: 14.6 us -> 12.7 us  [cross(): return lax.ppermute(value, 'dp', self.side)]
where the time goes in v5:
time: 156 us
  blocking collectives  51.9 us (33%)
  starting transfers between devices  39.7 us (25%)
  Pallas kernels  32 us (21%)
  waiting for transfers between devices  31.3 us (20%)
    all_to_all x2, blocking collectives, exchange(): lax.all_to_all(value.reshape(columns, exp_dev * 8, -1), 'expert', 0, 0, t...  51.9 us
    ppermute x11, starting transfers between devices, send_down(): return lax.ppermute(value, 'dp', self.down)  29.6 us
    ppermute x11, waiting for transfers between devices, send_up(): return lax.ppermute(value, 'dp', self.up)  13.7 us
    ppermute x7, waiting for transfers between devices, cross(): return lax.ppermute(value, 'dp', self.side)  12.7 us
    pallas_call x3, Pallas kernels, gate_up(): pl.pallas_call(kernel, in_specs=[VMEM] * (len(pieces) + len(extra)) + [VM...  5.99 us
    pallas_call x3, Pallas kernels, cotangents(): pl.pallas_call(kernel, in_specs=[VMEM] * (len(pieces) + len(extra)) + hel...  5.56 us
    ppermute x11, starting transfers between devices, send_up(): return lax.ppermute(value, 'dp', self.up)  5.45 us
    ppermute x11, waiting for transfers between devices, send_down(): return lax.ppermute(value, 'dp', self.down)  4.88 us
  transfers between devices with their start and end apart: 29, of which 12 were waited for; matrix products, arithmetic and copies ran while one was open for 0% of the time, Pallas kernels for 18%

profile of v5, /device:TPU:1, one launch (start us, length us, event | category | flops | bytes accessed | tf_op | source)
XLA Modules:
  0.0 156.0 jit_solution(4419182081071165036)
XLA Ops:
  2.3 23.7 %all_to_all.10 = bf16[16,16,1792]{2,1,0:T(8,128)(2,1)S(1)} all-to-all(bf16[16,16,1792]{2,1,0:T(8,128)(2,1)S(1)} %bitcast.16), channel_id=1, replica_groups=mesh['dp'=8,'expert'=16] {'expert'}, dimensions={0} | all-to-all | bytes 1835008 | tf_op jit(solution)/shard_map/all_to_all | solution.py:669
  28.2 2.1 %collective-permute-start.3 = (bf16[256,896]{1,0:T(8,128)(2,1)S(1)}, bf16[256,896]{1,0:T(8,128)(2,1)S(1)}, u32[]{:S(2)}, u32[]{:S(2)}) collective-permute-start(bf16[256,896]{1,0:T(8,128)(2,1)S(1)} %get-tuple-element.216.refs_0_), channel_id=1, source_target_pairs={{0,96},{16,112},{32,0},{48,16},{64,32},{80,48},{96,64},{112,80},{1... | collective-permute-start | bytes 1376264 | tf_op jit(solution)/shard_map/ppermute | solution.py:121
  31.5 5.6 %collective-permute-done.5.beside.refs_3_ = bf16[256,896]{1,0:T(8,128)(2,1)S(1)} collective-permute-done((bf16[256,896]{1,0:T(8,128)(2,1)S(1)}, bf16[256,896]{1,0:T(8,128)(2,1)S(1)}, u32[]{:S(2)}, u32[]{:S(2)}) %collective-permute-start.5) | collective-permute-done | bytes 458784 | tf_op jit(solution)/shard_map/ppermute | solution.py:124
  37.1 3.8 %collective-permute-start = (bf16[256,896]{1,0:T(8,128)(2,1)S(1)}, bf16[256,896]{1,0:T(8,128)(2,1)S(1)}, u32[]{:S(2)}, u32[]{:S(2)}) collective-permute-start(bf16[256,896]{1,0:T(8,128)(2,1)S(1)} %get-tuple-element.207.refs_0_), channel_id=1, source_target_pairs={{0,96},{16,112},{32,0},{48,16},{64,32},{80,48},{96,64},{112,80},{1... | collective-permute-start | bytes 1376264 | tf_op jit(solution)/shard_map/ppermute | solution.py:121
  43.4 3.5 %collective-permute-done.2.beside.refs_3_ = bf16[256,896]{1,0:T(8,128)(2,1)S(1)} collective-permute-done((bf16[256,896]{1,0:T(8,128)(2,1)S(1)}, bf16[256,896]{1,0:T(8,128)(2,1)S(1)}, u32[]{:S(2)}, u32[]{:S(2)}) %collective-permute-start.2) | collective-permute-done | bytes 458784 | tf_op jit(solution)/shard_map/ppermute | solution.py:124
  48.6 2.9 %gate_up_0.1.refs_3_ = f32[256,256]{1,0:T(8,128)S(1)} custom-call(bf16[256,896]{1,0:T(8,128)(2,1)S(1)} %get-tuple-element.216.refs_0_, bf16[256,896]{1,0:T(8,128)(2,1)S(1)} %collective-permute-done.3.above.refs_1_, bf16[256,896]{1,0:T(8,128)(2,1)S(1)} %collective-permute-done.4.below.refs_2_, bf16[256,896]{1,0:T(8,128)(2,1)S(1)} %collective-permute-done.5.beside.refs_3_, ...), custom_call_target="tpu_custom_call" | custom-call | tf_op jit(solution)/shard_map/gate_up_0/pallas_call | solution.py:328
  53.3 2.1 %collective-permute-start.6 = (bf16[240,896]{1,0:T(8,128)(2,1)S(1)}, bf16[240,896]{1,0:T(8,128)(2,1)S(1)}, u32[]{:S(2)}, u32[]{:S(2)}) collective-permute-start(bf16[240,896]{1,0:T(8,128)(2,1)S(1)} %get-tuple-element.143), channel_id=1, source_target_pairs={{0,96},{16,112},{32,0},{48,16},{64,32},{80,48},{96,64},{112,80},{1... | collective-permute-start | bytes 1290248 | tf_op jit(solution)/shard_map/ppermute | solution.py:121
  58.1 3.7 %collective-permute-start.14 = (bf16[128,896]{1,0:T(8,128)(2,1)S(1)}, bf16[128,896]{1,0:T(8,128)(2,1)S(1)}, u32[]{:S(2)}, u32[]{:S(2)}) collective-permute-start(bf16[128,896]{1,0:T(8,128)(2,1)S(1)} %get-tuple-element.149), channel_id=1, source_target_pairs={{0,96},{16,112},{32,0},{48,16},{64,32},{80,48},{96,64},{112,80},{1... | collective-permute-start | bytes 688136 | tf_op jit(solution)/shard_map/ppermute | solution.py:121
  61.9 2.7 %cotangents_0.1.refs_3_ = f32[256,128]{1,0:T(8,128)S(1)} custom-call(bf16[256,896]{1,0:T(8,128)(2,1)S(1)} %get-tuple-element.207.refs_0_, bf16[256,896]{1,0:T(8,128)(2,1)S(1)} %collective-permute-done.above.refs_1_, bf16[256,896]{1,0:T(8,128)(2,1)S(1)} %collective-permute-done.1.below.refs_2_, bf16[256,896]{1,0:T(8,128)(2,1)S(1)} %collective-permute-done.2.beside.refs_3_, ...), custom_call_target="tpu_custom_call" | custom-call | tf_op jit(solution)/shard_map/cotangents_0/pallas_call | solution.py:419
  64.5 2.5 %gate_up_1.1.refs_2_ = f32[256,256]{1,0:T(8,128)S(1)} custom-call(bf16[240,896]{1,0:T(8,128)(2,1)S(1)} %collective-permute-done.9.above2.refs_0_.refs_4_, bf16[240,896]{1,0:T(8,128)(2,1)S(1)} %collective-permute-done.10.below2.refs_1_.refs_5_, bf16[288,896]{1,0:T(8,128)(2,1)S(1)} %collective-permute-done.11.beside2.refs_2_.refs_6_, ...), custom_call_target="tpu_custom_call" | custom-call | tf_op jit(solution)/shard_map/gate_up_1/pallas_call | solution.py:328
  69.1 3.8 %collective-permute-start.12 = (bf16[128,896]{1,0:T(8,128)(2,1)S(1)}, bf16[128,896]{1,0:T(8,128)(2,1)S(1)}, u32[]{:S(2)}, u32[]{:S(2)}) collective-permute-start(bf16[128,896]{1,0:T(8,128)(2,1)S(1)} %get-tuple-element.161), channel_id=1, source_target_pairs={{0,96},{16,112},{32,0},{48,16},{64,32},{80,48},{96,64},{112,80},{1... | collective-permute-start | bytes 688136 | tf_op jit(solution)/shard_map/ppermute | solution.py:121
  72.9 2.2 %cotangents_1.1.refs_2_ = f32[256,128]{1,0:T(8,128)S(1)} custom-call(bf16[240,896]{1,0:T(8,128)(2,1)S(1)} %collective-permute-done.6.above2.refs_0_.refs_4_, bf16[240,896]{1,0:T(8,128)(2,1)S(1)} %collective-permute-done.7.below2.refs_1_.refs_5_, bf16[288,896]{1,0:T(8,128)(2,1)S(1)} %collective-permute-done.8.beside2.refs_2_.refs_6_, ...), custom_call_target="tpu_custom_call" | custom-call | tf_op jit(solution)/shard_map/cotangents_1/pallas_call | solution.py:419
  75.9 2.9 %collective-permute-start.17 = (bf16[128,896]{1,0:T(8,128)(2,1)S(1)}, bf16[128,896]{1,0:T(8,128)(2,1)S(1)}, u32[]{:S(2)}, u32[]{:S(2)}) collective-permute-start(bf16[128,896]{1,0:T(8,128)(2,1)S(1)} %get-tuple-element.172), channel_id=1, source_target_pairs={{0,96},{16,112},{32,0},{48,16},{64,32},{80,48},{96,64},{112,80},{1... | collective-permute-start | bytes 688136 | tf_op jit(solution)/shard_map/ppermute | solution.py:121
  84.3 2.4 %collective-permute-start.19 = (bf16[208,896]{1,0:T(8,128)(2,1)S(1)}, bf16[208,896]{1,0:T(8,128)(2,1)S(1)}, u32[]{:S(2)}, u32[]{:S(2)}) collective-permute-start(bf16[208,896]{1,0:T(8,128)(2,1)S(1)} %get-tuple-element.186), channel_id=1, source_target_pairs={{0,96},{16,112},{32,0},{48,16},{64,32},{80,48},{96,64},{112,80},{1... | collective-permute-start | bytes 1118216 | tf_op jit(solution)/shard_map/ppermute | solution.py:121
  88.2 3.9 %middle_sums.1 = (bf16[256,896]{1,0:T(8,128)(2,1)S(1)}, bf16[256,896]{1,0:T(8,128)(2,1)S(1)}, bf16[256,896]{1,0:T(8,128)(2,1)S(1)}, bf16[256,896]{1,0:T(8,128)(2...) custom-call(bf16[256,256]{1,0:T(8,128)(2,1)S(1)} %get-tuple-element.201.gate_diff_, ...), custom_call_target="tpu_custom_call" | custom-call | tf_op jit(solution)/shard_map/middle_sums/pallas_call | solution.py:475
  92.1 2.8 %collective-permute-done.22.refs_10_ = bf16[128,896]{1,0:T(8,128)(2,1)S(1)} collective-permute-done((bf16[128,896]{1,0:T(8,128)(2,1)S(1)}, bf16[128,896]{1,0:T(8,128)(2,1)S(1)}, u32[]{:S(2)}, u32[]{:S(2)}) %collective-permute-start.22) | collective-permute-done | bytes 229408 | tf_op jit(solution)/shard_map/ppermute | solution.py:121
  97.9 2.7 %collective-permute-start.24 = (bf16[496,896]{1,0:T(8,128)(2,1)S(1)}, bf16[496,896]{1,0:T(8,128)(2,1)S(1)}, u32[]{:S(2)}, u32[]{:S(2)}) collective-permute-start(bf16[496,896]{1,0:T(8,128)(2,1)S(1)} %get-tuple-element.199), channel_id=1, source_target_pairs={{0,96},{16,112},{32,0},{48,16},{64,32},{80,48},{96,64},{112,80},{1... | collective-permute-start | bytes 2666504 | tf_op jit(solution)/shard_map/ppermute | solution.py:121
  100.5 3.1 %input_sums_2.1 = (bf16[256,896]{1,0:T(8,128)(2,1)S(1)}, bf16[256,896]{1,0:T(8,128)(2,1)S(1)}, bf16[256,896]{1,0:T(8,128)(2,1)S(1)}, bf16[256,896]{1,0:T(8,128)(2,1)S(1)}) custom-call(bf16[256,256]{1,0:T(8,128)(2,1)S(1)} %get-tuple-element.201.gate_diff_ref.refs_9_, bf16[256,256]{1,0:T(8,128)(2,1)S(1)} %get-tuple-element.202.up_diff_ref.refs_10_, ...), custom_call_target="tpu_custom_call" | custom-call | tf_op jit(solution)/shard_map/input_sums_2/pallas_call | solution.py:446
  103.6 2.2 %row_grads.1 = bf16[256,7168]{1,0:T(8,128)(2,1)} custom-call(bf16[256,896]{1,0:T(8,128)(2,1)S(1)} %get-tuple-element.207.refs_0_, bf16[256,896]{1,0:T(8,128)(2,1)S(1)} %collective-permute-done.above.refs_1_, bf16[256,896]{1,0:T(8,128)(2,1)S(1)} %collective-permute-done.1.below.refs_2_, bf16[256,896]{1,0:T(8,128)(2,1)S(1)} %collective-permute-done.2.beside.refs_3_, ...), custom_call_target="tpu_custom_call" | custom-call | tf_op jit(solution)/shard_map/row_grads/pallas_call | solution.py:544
  105.9 3.5 %column_grads.1 = (bf16[2,7168,128]{2,1,0:T(8,128)(2,1)}, bf16[2,7168,128]{2,1,0:T(8,128)(2,1)}) custom-call(bf16[256,896]{1,0:T(8,128)(2,1)S(1)} %get-tuple-element.216.refs_0_, bf16[256,896]{1,0:T(8,128)(2,1)S(1)} %collective-permute-done.3.above.refs_1_, bf16[256,896]{1,0:T(8,128)(2,1)S(1)} %collective-permute-done.4.below.refs_2_, ...), custom_call_target="tpu_custom_call" | custom-call | tf_op jit(solution)/shard_map/column_grads/pallas_call | solution.py:516
  109.4 5.1 %collective-permute-done.23.got_up.from_below = bf16[496,896]{1,0:T(8,128)(2,1)S(1)} collective-permute-done((bf16[496,896]{1,0:T(8,128)(2,1)S(1)}, bf16[496,896]{1,0:T(8,128)(2,1)S(1)}, u32[]{:S(2)}, u32[]{:S(2)}) %collective-permute-start.23) | collective-permute-done | bytes 888864 | tf_op jit(solution)/shard_map/ppermute | solution.py:118
  115.5 3.4 %collective-permute-start.27 = (bf16[256,896]{1,0:T(8,128)(2,1)S(1)}, bf16[256,896]{1,0:T(8,128)(2,1)S(1)}, u32[]{:S(2)}, u32[]{:S(2)}) collective-permute-start(bf16[256,896]{1,0:T(8,128)(2,1)S(1)} %get-tuple-element.230), channel_id=1, source_target_pairs={{0,96},{16,112},{32,0},{48,16},{64,32},{80,48},{96,64},{112,80},{1... | collective-permute-start | bytes 1376264 | tf_op jit(solution)/shard_map/ppermute | solution.py:121
  119.1 6.3 %collective-permute-done.26.from_below = bf16[256,896]{1,0:T(8,128)(2,1)S(1)} collective-permute-done((bf16[256,896]{1,0:T(8,128)(2,1)S(1)}, bf16[256,896]{1,0:T(8,128)(2,1)S(1)}, u32[]{:S(2)}, u32[]{:S(2)}) %collective-permute-start.26) | collective-permute-done | bytes 458784 | tf_op jit(solution)/shard_map/ppermute | solution.py:118
  126.8 28.2 %all_to_all.11 = bf16[16,16,1792]{2,1,0:T(8,128)(2,1)S(1)} all-to-all(bf16[16,16,1792]{2,1,0:T(8,128)(2,1)S(1)} %bitcast.17), channel_id=1, replica_groups=mesh['dp'=8,'expert'=16] {'expert'}, dimensions={0} | all-to-all | bytes 1835008 | tf_op jit(solution)/shard_map/all_to_all | solution.py:669
  (62 shorter events, 30.0 us)
Async XLA Ops:
  26.2 10.9 %collective-permute-start.5 = (bf16[256,896]{1,0:T(8,128)(2,1)S(1)}, bf16[256,896]{1,0:T(8,128)(2,1)S(1)}, u32[]{:S(2)}, u32[]{:S(2)}) collective-permute-start(bf16[256,896]{1,0:T(8,128)(2,1)S(1)} %get-tuple-element.216.refs_0_), channel_id=1, source_target_pairs={{0,16},{16,0},{32,48},{48,32},{64,80},{80,64},{96,112},{112,96},{1... | collective-permute-start | bytes 1376264 | tf_op jit(solution)/shard_map/ppermute | solution.py:124
  26.6 14.3 %collective-permute-start.4 = (bf16[256,896]{1,0:T(8,128)(2,1)S(1)}, bf16[256,896]{1,0:T(8,128)(2,1)S(1)}, u32[]{:S(2)}, u32[]{:S(2)}) collective-permute-start(bf16[256,896]{1,0:T(8,128)(2,1)S(1)} %get-tuple-element.216.refs_0_), channel_id=1, source_target_pairs={{0,32},{16,48},{32,64},{48,80},{64,96},{80,112},{96,0},{112,16},{1... | collective-permute-start | bytes 1376264 | tf_op jit(solution)/shard_map/ppermute | solution.py:118
  28.2 12.7 %collective-permute-start.3 = (bf16[256,896]{1,0:T(8,128)(2,1)S(1)}, bf16[256,896]{1,0:T(8,128)(2,1)S(1)}, u32[]{:S(2)}, u32[]{:S(2)}) collective-permute-start(bf16[256,896]{1,0:T(8,128)(2,1)S(1)} %get-tuple-element.216.refs_0_), channel_id=1, source_target_pairs={{0,96},{16,112},{32,0},{48,16},{64,32},{80,48},{96,64},{112,80},{1... | collective-permute-start | bytes 1376264 | tf_op jit(solution)/shard_map/ppermute | solution.py:121
  30.3 16.6 %collective-permute-start.2 = (bf16[256,896]{1,0:T(8,128)(2,1)S(1)}, bf16[256,896]{1,0:T(8,128)(2,1)S(1)}, u32[]{:S(2)}, u32[]{:S(2)}) collective-permute-start(bf16[256,896]{1,0:T(8,128)(2,1)S(1)} %get-tuple-element.207.refs_0_), channel_id=1, source_target_pairs={{0,16},{16,0},{32,48},{48,32},{64,80},{80,64},{96,112},{112,96},{1... | collective-permute-start | bytes 1376264 | tf_op jit(solution)/shard_map/ppermute | solution.py:124
  31.5 21.3 %collective-permute-start.1 = (bf16[256,896]{1,0:T(8,128)(2,1)S(1)}, bf16[256,896]{1,0:T(8,128)(2,1)S(1)}, u32[]{:S(2)}, u32[]{:S(2)}) collective-permute-start(bf16[256,896]{1,0:T(8,128)(2,1)S(1)} %get-tuple-element.207.refs_0_), channel_id=1, source_target_pairs={{0,32},{16,48},{32,64},{48,80},{64,96},{80,112},{96,0},{112,16},{1... | collective-permute-start | bytes 1376264 | tf_op jit(solution)/shard_map/ppermute | solution.py:118
  37.1 15.7 %collective-permute-start = (bf16[256,896]{1,0:T(8,128)(2,1)S(1)}, bf16[256,896]{1,0:T(8,128)(2,1)S(1)}, u32[]{:S(2)}, u32[]{:S(2)}) collective-permute-start(bf16[256,896]{1,0:T(8,128)(2,1)S(1)} %get-tuple-element.207.refs_0_), channel_id=1, source_target_pairs={{0,96},{16,112},{32,0},{48,16},{64,32},{80,48},{96,64},{112,80},{1... | collective-permute-start | bytes 1376264 | tf_op jit(solution)/shard_map/ppermute | solution.py:121
  41.0 15.8 %collective-permute-start.9 = (bf16[240,896]{1,0:T(8,128)(2,1)S(1)}, bf16[240,896]{1,0:T(8,128)(2,1)S(1)}, u32[]{:S(2)}, u32[]{:S(2)}) collective-permute-start(bf16[240,896]{1,0:T(8,128)(2,1)S(1)} %get-tuple-element.130), channel_id=1, source_target_pairs={{0,96},{16,112},{32,0},{48,16},{64,32},{80,48},{96,64},{112,80},{1... | collective-permute-start | bytes 1290248 | tf_op jit(solution)/shard_map/ppermute | solution.py:121
  42.3 15.8 %collective-permute-start.11 = (bf16[288,896]{1,0:T(8,128)(2,1)S(1)}, bf16[288,896]{1,0:T(8,128)(2,1)S(1)}, u32[]{:S(2)}, u32[]{:S(2)}) collective-permute-start(bf16[288,896]{1,0:T(8,128)(2,1)S(1)} %get-tuple-element.132), channel_id=1, source_target_pairs={{0,16},{16,0},{32,48},{48,32},{64,80},{80,64},{96,112},{112,96},{1... | collective-permute-start | bytes 1548296 | tf_op jit(solution)/shard_map/ppermute | solution.py:124
  46.9 11.2 %collective-permute-start.10 = (bf16[240,896]{1,0:T(8,128)(2,1)S(1)}, bf16[240,896]{1,0:T(8,128)(2,1)S(1)}, u32[]{:S(2)}, u32[]{:S(2)}) collective-permute-start(bf16[240,896]{1,0:T(8,128)(2,1)S(1)} %get-tuple-element.131), channel_id=1, source_target_pairs={{0,32},{16,48},{32,64},{48,80},{64,96},{80,112},{96,0},{112,16},{1... | collective-permute-start | bytes 1290248 | tf_op jit(solution)/shard_map/ppermute | solution.py:118
  52.9 16.1 %collective-permute-start.8 = (bf16[288,896]{1,0:T(8,128)(2,1)S(1)}, bf16[288,896]{1,0:T(8,128)(2,1)S(1)}, u32[]{:S(2)}, u32[]{:S(2)}) collective-permute-start(bf16[288,896]{1,0:T(8,128)(2,1)S(1)} %get-tuple-element.145), channel_id=1, source_target_pairs={{0,16},{16,0},{32,48},{48,32},{64,80},{80,64},{96,112},{112,96},{1... | collective-permute-start | bytes 1548296 | tf_op jit(solution)/shard_map/ppermute | solution.py:124
  53.3 13.7 %collective-permute-start.6 = (bf16[240,896]{1,0:T(8,128)(2,1)S(1)}, bf16[240,896]{1,0:T(8,128)(2,1)S(1)}, u32[]{:S(2)}, u32[]{:S(2)}) collective-permute-start(bf16[240,896]{1,0:T(8,128)(2,1)S(1)} %get-tuple-element.143), channel_id=1, source_target_pairs={{0,96},{16,112},{32,0},{48,16},{64,32},{80,48},{96,64},{112,80},{1... | collective-permute-start | bytes 1290248 | tf_op jit(solution)/shard_map/ppermute | solution.py:121
  56.8 10.2 %collective-permute-start.7 = (bf16[240,896]{1,0:T(8,128)(2,1)S(1)}, bf16[240,896]{1,0:T(8,128)(2,1)S(1)}, u32[]{:S(2)}, u32[]{:S(2)}) collective-permute-start(bf16[240,896]{1,0:T(8,128)(2,1)S(1)} %get-tuple-element.144), channel_id=1, source_target_pairs={{0,32},{16,48},{32,64},{48,80},{64,96},{80,112},{96,0},{112,16},{1... | collective-permute-start | bytes 1290248 | tf_op jit(solution)/shard_map/ppermute | solution.py:118
  58.1 17.0 %collective-permute-start.14 = (bf16[128,896]{1,0:T(8,128)(2,1)S(1)}, bf16[128,896]{1,0:T(8,128)(2,1)S(1)}, u32[]{:S(2)}, u32[]{:S(2)}) collective-permute-start(bf16[128,896]{1,0:T(8,128)(2,1)S(1)} %get-tuple-element.149), channel_id=1, source_target_pairs={{0,96},{16,112},{32,0},{48,16},{64,32},{80,48},{96,64},{112,80},{1... | collective-permute-start | bytes 688136 | tf_op jit(solution)/shard_map/ppermute | solution.py:121
  61.9 13.3 %collective-permute-start.15 = (bf16[128,896]{1,0:T(8,128)(2,1)S(1)}, bf16[128,896]{1,0:T(8,128)(2,1)S(1)}, u32[]{:S(2)}, u32[]{:S(2)}) collective-permute-start(bf16[128,896]{1,0:T(8,128)(2,1)S(1)} %get-tuple-element.150), channel_id=1, source_target_pairs={{0,32},{16,48},{32,64},{48,80},{64,96},{80,112},{96,0},{112,16},{1... | collective-permute-start | bytes 688136 | tf_op jit(solution)/shard_map/ppermute | solution.py:118
  69.1 11.7 %collective-permute-start.12 = (bf16[128,896]{1,0:T(8,128)(2,1)S(1)}, bf16[128,896]{1,0:T(8,128)(2,1)S(1)}, u32[]{:S(2)}, u32[]{:S(2)}) collective-permute-start(bf16[128,896]{1,0:T(8,128)(2,1)S(1)} %get-tuple-element.161), channel_id=1, source_target_pairs={{0,96},{16,112},{32,0},{48,16},{64,32},{80,48},{96,64},{112,80},{1... | collective-permute-start | bytes 688136 | tf_op jit(solution)/shard_map/ppermute | solution.py:121
  83.3 12.8 %collective-permute-start.20 = (bf16[352,896]{1,0:T(8,128)(2,1)S(1)}, bf16[352,896]{1,0:T(8,128)(2,1)S(1)}, u32[]{:S(2)}, u32[]{:S(2)}) collective-permute-start(bf16[352,896]{1,0:T(8,128)(2,1)S(1)} %get-tuple-element.187), channel_id=1, source_target_pairs={{0,16},{16,0},{32,48},{48,32},{64,80},{80,64},{96,112},{112,96},{1... | collective-permute-start | bytes 1892360 | tf_op jit(solution)/shard_map/ppermute | solution.py:124
  83.6 12.5 %collective-permute-start.18 = (bf16[208,896]{1,0:T(8,128)(2,1)S(1)}, bf16[208,896]{1,0:T(8,128)(2,1)S(1)}, u32[]{:S(2)}, u32[]{:S(2)}) collective-permute-start(bf16[208,896]{1,0:T(8,128)(2,1)S(1)} %get-tuple-element.185), channel_id=1, source_target_pairs={{0,32},{16,48},{32,64},{48,80},{64,96},{80,112},{96,0},{112,16},{1... | collective-permute-start | bytes 1118216 | tf_op jit(solution)/shard_map/ppermute | solution.py:118
  84.3 11.9 %collective-permute-start.19 = (bf16[208,896]{1,0:T(8,128)(2,1)S(1)}, bf16[208,896]{1,0:T(8,128)(2,1)S(1)}, u32[]{:S(2)}, u32[]{:S(2)}) collective-permute-start(bf16[208,896]{1,0:T(8,128)(2,1)S(1)} %get-tuple-element.186), channel_id=1, source_target_pairs={{0,96},{16,112},{32,0},{48,16},{64,32},{80,48},{96,64},{112,80},{1... | collective-permute-start | bytes 1118216 | tf_op jit(solution)/shard_map/ppermute | solution.py:121
  86.7 8.2 %collective-permute-start.22 = (bf16[128,896]{1,0:T(8,128)(2,1)S(1)}, bf16[128,896]{1,0:T(8,128)(2,1)S(1)}, u32[]{:S(2)}, u32[]{:S(2)}) collective-permute-start(bf16[128,896]{1,0:T(8,128)(2,1)S(1)} %get-tuple-element.197), channel_id=1, source_target_pairs={{0,96},{16,112},{32,0},{48,16},{64,32},{80,48},{96,64},{112,80},{1... | collective-permute-start | bytes 688136 | tf_op jit(solution)/shard_map/ppermute | solution.py:121
  96.6 18.4 %collective-permute-start.25 = (bf16[544,896]{1,0:T(8,128)(2,1)S(1)}, bf16[544,896]{1,0:T(8,128)(2,1)S(1)}, u32[]{:S(2)}, u32[]{:S(2)}) collective-permute-start(bf16[544,896]{1,0:T(8,128)(2,1)S(1)} %get-tuple-element.200), channel_id=1, source_target_pairs={{0,16},{16,0},{32,48},{48,32},{64,80},{80,64},{96,112},{112,96},{1... | collective-permute-start | bytes 2924552 | tf_op jit(solution)/shard_map/ppermute | solution.py:124
  97.8 16.6 %collective-permute-start.23 = (bf16[496,896]{1,0:T(8,128)(2,1)S(1)}, bf16[496,896]{1,0:T(8,128)(2,1)S(1)}, u32[]{:S(2)}, u32[]{:S(2)}) collective-permute-start(bf16[496,896]{1,0:T(8,128)(2,1)S(1)} %get-tuple-element.198), channel_id=1, source_target_pairs={{0,32},{16,48},{32,64},{48,80},{64,96},{80,112},{96,0},{112,16},{1... | collective-permute-start | bytes 2666504 | tf_op jit(solution)/shard_map/ppermute | solution.py:118
  97.9 16.6 %collective-permute-start.24 = (bf16[496,896]{1,0:T(8,128)(2,1)S(1)}, bf16[496,896]{1,0:T(8,128)(2,1)S(1)}, u32[]{:S(2)}, u32[]{:S(2)}) collective-permute-start(bf16[496,896]{1,0:T(8,128)(2,1)S(1)} %get-tuple-element.199), channel_id=1, source_target_pairs={{0,96},{16,112},{32,0},{48,16},{64,32},{80,48},{96,64},{112,80},{1... | collective-permute-start | bytes 2666504 | tf_op jit(solution)/shard_map/ppermute | solution.py:121
  115.4 10.0 %collective-permute-start.26 = (bf16[256,896]{1,0:T(8,128)(2,1)S(1)}, bf16[256,896]{1,0:T(8,128)(2,1)S(1)}, u32[]{:S(2)}, u32[]{:S(2)}) collective-permute-start(bf16[256,896]{1,0:T(8,128)(2,1)S(1)} %get-tuple-element.229), channel_id=1, source_target_pairs={{0,32},{16,48},{32,64},{48,80},{64,96},{80,112},{96,0},{112,16},{1... | collective-permute-start | bytes 1376264 | tf_op jit(solution)/shard_map/ppermute | solution.py:118
  115.5 10.0 %collective-permute-start.27 = (bf16[256,896]{1,0:T(8,128)(2,1)S(1)}, bf16[256,896]{1,0:T(8,128)(2,1)S(1)}, u32[]{:S(2)}, u32[]{:S(2)}) collective-permute-start(bf16[256,896]{1,0:T(8,128)(2,1)S(1)} %get-tuple-element.230), channel_id=1, source_target_pairs={{0,96},{16,112},{32,0},{48,16},{64,32},{80,48},{96,64},{112,80},{1... | collective-permute-start | bytes 1376264 | tf_op jit(solution)/shard_map/ppermute | solution.py:121
  (5 other events, 37.6 us)
